TPU v7x, 32 devices: a whole 2x2x4 slice. The times are simulated.
32 devices in a mesh: pair: 4 (over y, x), tensor: 8 (over z, core).
Axes of the slice: x: 2, y: 2, z: 4, core: 2. Of those that a mesh axis runs over, the one named last changes fastest.
Arguments:
- queries: bfloat16 [8, 64, 1024], P('pair', 'tensor'), may hold values from -6 to 6
- documents: bfloat16 [16, 128, 1024], P('pair', 'tensor'), may hold values from -6 to 6
- doc_len: int32 [16], replicated, may hold values from 32 to 128
- route: int32 [4, 4], replicated, may hold values from -1 to 3, as said below
- pair_list: int32 [12, 3], P('pair'), may hold values from 0 to 3, as said below
- attn_gain: float32 [1024], replicated
- w_query: bfloat16 [1024, 8192], P(None, 'tensor')
- w_key: bfloat16 [1024, 8192], P(None, 'tensor')
- w_value: bfloat16 [1024, 8192], P(None, 'tensor'), may hold values from -0.1875 to 0.1875
- w_output: bfloat16 [8192, 1024], P('tensor'), may hold values from -0.5 to 0.5
- ffn_gain: float32 [1024], replicated, may hold values from 0.1 to 1.9
- w_in: bfloat16 [1024, 32768], P(None, 'tensor'), may hold values from -0.1875 to 0.1875
- w_down: bfloat16 [32768, 1024], P('tensor'), may hold values from -0.25 to 0.25
Outputs:
- doc_states: bfloat16 [16, 128, 1024], P('pair', 'tensor')
Inputs may be any that keep to these rules, and one draw needn't show every extreme that they name: route[s, g] is the local index, among the 4 documents of pair index s, of the one document s sends to owner g, or -1 where it sends none; each owner receives exactly min(6, number of pair indices) documents. `pair_list`: rows p * 3 to p * 3 + 2 belong to owner p; column 0 is below 2; columns 1 and 2 differ and name pair indices that send a document to that owner; each document an owner receives fills one or more roles of its pairs.
All inputs are finite; a program needn't handle non-finite values.
Results may differ from a plain program's by a relative error of at most 0.018.
Values may be sent and summed in bfloat16 or wider, within the bound.
No kernel may reach another device: no remote copies, remote signals or barrier semaphores. Data moves between devices by JAX's collectives and lax.ppermute only.
A program may use at most 128 MiB of HBM per device.

v0:
```python
import math

import jax
import jax.numpy as jnp
from jax import lax
from jax.sharding import PartitionSpec as P

HEAD = 128


def rms_norm(values, gain):
    spread = jnp.mean(values * values, -1, keepdims=True)
    return values * lax.rsqrt(spread + 1e-06) * gain


def select_rows(picker, source):
    return jnp.einsum(
        "pn,nld->pld", picker.astype(jnp.bfloat16), source, preferred_element_type=jnp.float32
    ).astype(jnp.bfloat16)


def local(
    queries,
    documents,
    doc_len,
    route,
    pair_list,
    attn_gain,
    w_query,
    w_key,
    w_value,
    w_output,
    ffn_gain,
    w_in,
    w_down,
):
    owners_count = lax.axis_size("pair")
    my_owner = lax.axis_index("pair")
    my_slice = lax.axis_index("tensor")
    doc_count, doc_rows, width = documents.shape
    query_rows = queries.shape[1]
    pairs = pair_list.shape[0]
    total_docs = doc_len.shape[0]
    seg_rows = query_rows + 2 * doc_rows
    local_heads = w_query.shape[1] // HEAD
    owner_range = jnp.arange(owners_count, dtype=jnp.int32)
    incoming_route = lax.dynamic_slice_in_dim(route, my_owner, 1, 1)[:, 0]
    outgoing_route = lax.dynamic_slice_in_dim(route, my_owner, 1, 0)[0]
    source_ids = owner_range * doc_count + jnp.maximum(incoming_route, 0)
    first_pick = pair_list[:, 1][:, None] == owner_range[None, :]
    second_pick = pair_list[:, 2][:, None] == owner_range[None, :]
    first_ids = jnp.sum(jnp.where(first_pick, source_ids[None, :], 0), 1)
    second_ids = jnp.sum(jnp.where(second_pick, source_ids[None, :], 0), 1)
    doc_range = jnp.arange(total_docs, dtype=jnp.int32)
    first_global = first_ids[:, None] == doc_range[None, :]
    second_global = second_ids[:, None] == doc_range[None, :]
    first_len = jnp.sum(jnp.where(first_global, doc_len[None, :], 0), 1)
    second_len = jnp.sum(jnp.where(second_global, doc_len[None, :], 0), 1)
    send_pick = outgoing_route[:, None] == jnp.arange(doc_count, dtype=jnp.int32)[None, :]
    outgoing = select_rows(send_pick, documents)
    arrived = lax.all_to_all(outgoing, "pair", split_axis=0, concat_axis=0, tiled=True)
    first_rows = select_rows(first_pick, arrived)
    second_rows = select_rows(second_pick, arrived)
    query_pick = pair_list[:, 0][:, None] == jnp.arange(queries.shape[0], dtype=jnp.int32)[None, :]
    query_rows_sel = select_rows(query_pick, queries)
    own_tokens = jnp.concatenate([query_rows_sel, first_rows, second_rows], 1)
    local_pos = my_slice * doc_rows + jnp.arange(doc_rows, dtype=jnp.int32)
    first_valid = (local_pos[None, :] < first_len[:, None]).astype(jnp.float32)
    second_valid = (local_pos[None, :] < second_len[:, None]).astype(jnp.float32)
    key_index = jnp.arange(lax.axis_size("tensor") * seg_rows, dtype=jnp.int32)
    slice_of = key_index // seg_rows
    within = key_index % seg_rows
    first_part = (within >= query_rows) & (within < query_rows + doc_rows)
    second_part = within >= query_rows + doc_rows
    first_doc_pos = slice_of * doc_rows + within - query_rows
    second_doc_pos = slice_of * doc_rows + within - query_rows - doc_rows
    key_ok = (
        (within < query_rows)[None, :]
        | first_part[None, :] & (first_doc_pos[None, :] < first_len[:, None])
        | second_part[None, :] & (second_doc_pos[None, :] < second_len[:, None])
    )
    tokens_all = lax.all_gather(own_tokens, "tensor", axis=1, tiled=True)
    values_all = tokens_all.astype(jnp.float32)
    normed_all = rms_norm(values_all, attn_gain).astype(jnp.bfloat16)
    rows_all = normed_all.shape[1]
    query_heads = (
        jnp.einsum("prd,de->pre", normed_all, w_query, preferred_element_type=jnp.float32)
        .astype(jnp.bfloat16)
        .reshape(pairs, rows_all, local_heads, HEAD)
    )
    key_heads = (
        jnp.einsum("prd,de->pre", normed_all, w_key, preferred_element_type=jnp.float32)
        .astype(jnp.bfloat16)
        .reshape(pairs, rows_all, local_heads, HEAD)
    )
    value_heads = (
        jnp.einsum("prd,de->pre", normed_all, w_value, preferred_element_type=jnp.float32)
        .astype(jnp.bfloat16)
        .reshape(pairs, rows_all, local_heads, HEAD)
    )
    scores = jnp.einsum(
        "prhd,pshd->phrs", query_heads, key_heads, preferred_element_type=jnp.float32
    ) / math.sqrt(HEAD)
    scores = jnp.where(key_ok[:, None, None, :], scores, jnp.float32(-1e30))
    top = jnp.max(scores, -1, keepdims=True)
    expo = jnp.exp(scores - top)
    probs = (expo / jnp.sum(expo, -1, keepdims=True)).astype(jnp.bfloat16)
    context = jnp.einsum("phrs,pshd->prhd", probs, value_heads, preferred_element_type=jnp.float32)
    context = context.astype(jnp.bfloat16).reshape(pairs, rows_all, local_heads * HEAD)
    hidden_all = values_all + lax.psum(
        jnp.einsum("pre,ed->prd", context, w_output, preferred_element_type=jnp.float32).astype(
            jnp.bfloat16
        ),
        "tensor",
    ).astype(jnp.float32)
    ffn_all = rms_norm(hidden_all, ffn_gain).astype(jnp.bfloat16)
    units = jax.nn.relu(
        jnp.einsum("prd,df->prf", ffn_all, w_in, preferred_element_type=jnp.float32)
    ).astype(jnp.bfloat16)
    layer_all = hidden_all + lax.psum(
        jnp.einsum("prf,fd->prd", units, w_down, preferred_element_type=jnp.float32).astype(
            jnp.bfloat16
        ),
        "tensor",
    ).astype(jnp.float32)
    layer_own = lax.dynamic_slice_in_dim(layer_all, my_slice * seg_rows, seg_rows, 1)
    first_seg = layer_own[:, query_rows : query_rows + doc_rows] * first_valid[:, :, None]
    second_seg = layer_own[:, query_rows + doc_rows :] * second_valid[:, :, None]
    back = jnp.einsum(
        "pn,pld->nld", first_pick.astype(jnp.float32), first_seg, precision=lax.Precision.HIGHEST
    )
    back = back + jnp.einsum(
        "pn,pld->nld", second_pick.astype(jnp.float32), second_seg, precision=lax.Precision.HIGHEST
    )
    returned = lax.all_to_all(
        back.astype(jnp.bfloat16), "pair", split_axis=0, concat_axis=0, tiled=True
    ).astype(back.dtype)
    home_pick = (outgoing_route[None, :] == jnp.arange(doc_count, dtype=jnp.int32)[:, None]).astype(
        jnp.float32
    )
    totals = jnp.einsum("kn,nld->kld", home_pick, returned, precision=lax.Precision.HIGHEST)
    return totals.astype(jnp.bfloat16)


def solution(mesh):
    placed = (
        P("pair", "tensor", None),
        P("pair", "tensor", None),
        P(),
        P(),
        P("pair", None),
        P(),
        P(None, "tensor"),
        P(None, "tensor"),
        P(None, "tensor"),
        P("tensor", None),
        P(),
        P(None, "tensor"),
        P("tensor", None),
    )
    return jax.shard_map(
        local, mesh=mesh, in_specs=placed, out_specs=P("pair", "tensor", None), check_vma=False
    )
```

profile of v0, /device:TPU:0, one launch (start us, length us, event | category | flops | bytes accessed | tf_op | source)
XLA Modules:
  0.0 267.1 jit_solution(9283545649258657422)
XLA Ops:
  6.5 0.8 fusion.95
  7.4 1.2 convolution_convert_fusion.3
  9.3 5.2 %all-to-all-start = ((bf16[4,16,1024]{2,1,0:T(8,128)(2,1)}), bf16[4,16,1024]{2,1,0:T(8,128)(2,1)S(1)}, u32[]{:S(2)}, u32[]{:S(2)}) async-start(bf16[4,16,1024]{2,1,0:T(8,128)(2,1)} %copy.59), calls=%async_computation | async-start | bytes 262144 | tf_op jit(solution)/shard_map/all_to_all | solution.py:61
  14.4 1.0 slice_reduce_fusion.1
  15.4 1.0 convolution_convert_fusion.4
  16.4 3.0 %all-to-all-done = bf16[4,16,1024]{2,1,0:T(8,128)(2,1)S(1)} async-done(((bf16[4,16,1024]{2,1,0:T(8,128)(2,1)}), bf16[4,16,1024]{2,1,0:T(8,128)(2,1)S(1)}, u32[]{:S(2)}, u32[]{:S(2)}) %all-to-all-start) | async-done | bytes 131104 | tf_op jit(solution)/shard_map/all_to_all | solution.py:61
  20.2 0.8 copy.64
  21.1 0.9 maximum_reduce_fusion
  22.1 0.9 select_reduce_fusion.2
  23.1 25.9 %all-gather.2.cloned.1.call-done = bf16[3,320,1024]{2,1,0:T(8,128)(2,1)} async-done(((bf16[3,40,1024]{2,1,0:T(8,128)(2,1)}), bf16[3,320,1024]{2,1,0:T(8,128)(2,1)}) %all-gather.2.cloned.1.call-update) | async-done | bytes 1966096 | tf_op jit(solution)/shard_map/all_gather | solution.py:82
  48.9 2.0 fusion.12
  51.0 3.9 %convert_bitcast_fusion.2 = bf16[3,40,8,8,128]{4,3,2,1,0:T(8,128)(2,1)S(1)} fusion(bf16[1024,1024]{1,0:T(8,128)(2,1)S(1)} %copy-done, bf16[3,320,1024]{2,1,0:T(8,128)(2,1)} %all-gather.2.cloned.1.call-done, f32[1024]{0:T(1024)S(1)} %copy-done.7, f32[3,320]{1,0:T(4,128)S(1)} %add_rsqrt_fusion.1), kind=kOutput, calls=%fused_computation.43 | convolution fusion | flops 2018181120 | bytes 6037248 | tf_op jit(solution)/shard_map/prd,de->pre/dot_general | solution.py:87
  55.0 2.3 convert_bitcast_fusion.1
  57.2 6.1 %fusion.25 = f32[3,8,320,320]{2,3,1,0:T(8,128)} fusion(bf16[3,40,8,8,128]{4,3,2,1,0:T(8,128)(2,1)S(1)} %convert_bitcast_fusion.1, bf16[3,40,8,8,128]{4,3,2,1,0:T(8,128)(2,1)S(1)} %convert_bitcast_fusion.2), kind=kOutput, calls=%fused_computation.32 | convolution fusion | flops 629145600 | bytes 13762560 | tf_op jit(solution)/shard_map/prhd,pshd->phrs/dot_general | solution.py:101
  63.3 17.0 %fusion.100 = (f32[3,8,320]{2,1,0:T(8,128)S(1)}, f32[3,8,320,320]{2,3,1,0:T(8,128)}) fusion(f32[3,8,320,320]{2,3,1,0:T(8,128)} %fusion.25, pred[3,320]{1,0:T(4,128)(4,1)S(1)} %and_or_fusion), kind=kOutput, calls=%fused_computation.125 | output fusion | flops 14745919 | bytes 19692480 | tf_op jit(solution)/shard_map/sub | solution.py:106
  80.3 2.4 convert_bitcast_fusion.3
  82.8 6.5 %convert_bitcast_fusion = bf16[3,8,40,8,128]{4,3,2,1,0:T(8,128)(2,1)S(1)} fusion(f32[3,8,320,320]{2,3,1,0:T(8,128)} %get-tuple-element.19, f32[3,8,320]{2,1,0:T(8,128)S(1)} %get-tuple-element.18, bf16[3,40,8,8,128]{4,3,2,1,0:T(8,128)(2,1)S(1)} %convert_bitcast_fusion.3), kind=kOutput, calls=%fused_computation.41 | convolution fusion | flops 635043840 | bytes 13793280 | tf_op jit(solution)/shard_map/phrs,pshd->prhd/dot_general | solution.py:108
  89.3 3.5 %fusion.40 = bf16[3,320,1024]{2,1,0:T(8,128)(2,1)} fusion(bf16[1024,1024]{1,0:T(8,128)(2,1)S(1)} %copy-done.6, bf16[3,8,40,8,128]{4,3,2,1,0:T(8,128)(2,1)S(1)} %convert_bitcast_fusion), kind=kOutput, calls=%fused_computation.45 | convolution fusion | flops 2014248960 | bytes 6029312 | tf_op jit(solution)/shard_map/pre,ed->prd/dot_general | solution.py:111
  92.8 63.6 %all-reduce.3.cloned.1.call-done = bf16[3,320,1024]{2,1,0:T(8,128)(2,1)} async-done(((bf16[3,320,1024]{2,1,0:T(8,128)(2,1)}), bf16[3,320,1024]{2,1,0:T(8,128)(2,1)}) %all-reduce.3.cloned.1.call-update) | async-done | bytes 1966096 | tf_op jit(solution)/shard_map/psum | solution.py:110
  156.5 4.1 %multiply_reduce_fusion = (f32[3,320]{1,0:T(4,128)S(1)}, f32[3,320,1024]{2,1,0:T(8,128)}) fusion(bf16[3,320,1024]{2,1,0:T(8,128)(2,1)} %all-reduce.3.cloned.1.call-done, bf16[3,320,1024]{2,1,0:T(8,128)(2,1)S(1)} %copy-done.3), kind=kLoop, calls=%fused_computation.21 | loop fusion | flops 4914240 | bytes 7868160 | tf_op jit(solution)/shard_map/reduce_sum | solution.py:12
  160.6 24.9 %fusion.47 = bf16[3,320,1024]{2,1,0:T(8,128)(2,1)} fusion(bf16[4096,1024]{1,0:T(8,128)(2,1)} %param.25, bf16[1024,4096]{1,0:T(8,128)(2,1)} %param.24, f32[1024]{0:T(1024)S(1)} %copy-done.8, f32[3,320]{1,0:T(4,128)S(1)} %add_rsqrt_fusion, bf16[3,320,1024]{2,1,0:T(8,128)(2,1)} %all-gather.2.cloned.1.call-done, ...), kind=kOutput, calls=%fused_computation.46 | convolution fusion | flops 16120872960 | bytes 22683392 | tf_op jit(solution)/shard_map/prf,fd->prd/dot_general | solution.py:121
  185.5 63.5 %all-reduce.5.cloned.1.call-done = bf16[3,320,1024]{2,1,0:T(8,128)(2,1)} async-done(((bf16[3,320,1024]{2,1,0:T(8,128)(2,1)}), bf16[3,320,1024]{2,1,0:T(8,128)(2,1)}) %all-reduce.5.cloned.1.call-update) | async-done | bytes 1966096 | tf_op jit(solution)/shard_map/psum | solution.py:120
  249.1 1.1 dynamic-slice_add_fusion
  251.3 8.4 %all_to_all.10 = bf16[4,16,1024]{2,1,0:T(8,128)(2,1)S(1)} all-to-all(bf16[4,16,1024]{2,1,0:T(8,128)(2,1)S(1)} %copy.72), channel_id=1, replica_groups=mesh['pair'=4,'tensor'=8] {'pair'}, dimensions={0} | all-to-all | bytes 262144 | tf_op jit(solution)/shard_map/all_to_all | solution.py:135
  (44 shorter events, 3.9 us)
Async XLA Ops:
  6.5 44.4 %copy-start = (bf16[1024,1024]{1,0:T(8,128)(2,1)S(1)}, bf16[1024,1024]{1,0:T(8,128)(2,1)}, u32[]{:S(2)}) copy-start(bf16[1024,1024]{1,0:T(8,128)(2,1)} %param.19) | copy-start | bytes 6291460
  6.5 44.4 %copy-start.7 = (f32[1024]{0:T(1024)S(1)}, f32[1024]{0:T(1024)}, u32[]{:S(2)}) copy-start(f32[1024]{0:T(1024)} %param.18) | copy-start | bytes 12292
  9.3 10.2 %all-to-all-start = ((bf16[4,16,1024]{2,1,0:T(8,128)(2,1)}), bf16[4,16,1024]{2,1,0:T(8,128)(2,1)S(1)}, u32[]{:S(2)}, u32[]{:S(2)}) async-start(bf16[4,16,1024]{2,1,0:T(8,128)(2,1)} %copy.59), calls=%async_computation | async-start | bytes 262144 | tf_op jit(solution)/shard_map/all_to_all | solution.py:61
  14.4 34.5 %all-gather.2.cloned.1.call-start = ((), (), s32[]{:S(2)}) async-start(), calls=%async_computation.2 | async-start | bytes 2211840 | tf_op jit(solution)/shard_map/all_gather | solution.py:82
  21.1 135.4 %all-reduce.3.cloned.1.call-start = ((), (), s32[]{:S(2)}) async-start(), calls=%async_computation.3 | async-start | bytes 3932160 | tf_op jit(solution)/shard_map/psum | solution.py:110
  51.0 4.0 %copy-start.2 = (bf16[3,320,1024]{2,1,0:T(8,128)(2,1)S(1)}, bf16[3,320,1024]{2,1,0:T(8,128)(2,1)}, u32[]{:S(2)}) copy-start(bf16[3,320,1024]{2,1,0:T(8,128)(2,1)} %all-gather.2.cloned.1.call-done) | copy-start | bytes 5898244
  51.0 4.0 %copy-start.4 = (bf16[1024,1024]{1,0:T(8,128)(2,1)S(1)}, bf16[1024,1024]{1,0:T(8,128)(2,1)}, u32[]{:S(2)}) copy-start(bf16[1024,1024]{1,0:T(8,128)(2,1)} %param.20) | copy-start | bytes 6291460
  63.3 17.0 %copy-start.5 = (bf16[1024,1024]{1,0:T(8,128)(2,1)S(1)}, bf16[1024,1024]{1,0:T(8,128)(2,1)}, u32[]{:S(2)}) copy-start(bf16[1024,1024]{1,0:T(8,128)(2,1)} %param.21) | copy-start | bytes 6291460
  82.8 6.5 %copy-start.6 = (bf16[1024,1024]{1,0:T(8,128)(2,1)S(1)}, bf16[1024,1024]{1,0:T(8,128)(2,1)}, u32[]{:S(2)}) copy-start(bf16[1024,1024]{1,0:T(8,128)(2,1)} %param.22) | copy-start | bytes 6291460
  89.3 67.2 %copy-start.3 = (bf16[3,320,1024]{2,1,0:T(8,128)(2,1)S(1)}, bf16[3,320,1024]{2,1,0:T(8,128)(2,1)}, u32[]{:S(2)}) copy-start(bf16[3,320,1024]{2,1,0:T(8,128)(2,1)} %all-gather.2.cloned.1.call-done) | copy-start | bytes 5898244
  92.8 67.8 %copy-start.8 = (f32[1024]{0:T(1024)S(1)}, f32[1024]{0:T(1024)}, u32[]{:S(2)}) copy-start(f32[1024]{0:T(1024)} %param.23) | copy-start | bytes 12292
  92.8 156.3 %all-reduce.5.cloned.1.call-start = ((), (), s32[]{:S(2)}) async-start(), calls=%async_computation.4 | async-start | bytes 3932160 | tf_op jit(solution)/shard_map/psum | solution.py:120
  160.5 100.1 %copy-start.1 = (bf16[1024,1024]{1,0:T(8,128)(2,1)S(1)}, bf16[1024,1024]{1,0:T(8,128)(2,1)}, u32[]{:S(2)}) copy-start(bf16[1024,1024]{1,0:T(8,128)(2,1)} %param.19) | copy-start | bytes 6291460
Sparse Core Ops, SparseCore 0:
  21.2 27.7 all-gather.1
  92.9 63.5 all-reduce.2
  185.6 63.4 all-reduce.4
where the time goes:
time: 268 us; the launch traced here: 267 us
  waiting for transfers between devices  156 us (58%)
  matrix products  53.4 us (20%)
  other arithmetic  26.5 us (10%)
  between operations  13.3 us (5%)
  blocking collectives  8.42 us (3%)
  starting transfers between devices  5.25 us (2%)
  local copies, waits for them, and re-layouts  4.11 us (2%)
    psum x1, waiting for transfers between devices, local(): lax.psum(jnp.einsum('pre,ed->prd', context, w_output, preferred_element_t...  63.6 us
    psum x1, waiting for transfers between devices, local(): lax.psum(jnp.einsum('prf,fd->prd', units, w_down, preferred_element_type=...  63.5 us
    all_gather x1, waiting for transfers between devices, local(): tokens_all = lax.all_gather(own_tokens, 'tensor', axis=1, tiled=True)  25.9 us
    dot_general x1, matrix products, local(): jnp.einsum('prf,fd->prd', units, w_down, preferred_element_type=jnp.float32)  24.9 us
    sub x1, other arithmetic, local(): expo = jnp.exp(scores - top)  17 us
    all_to_all x1, blocking collectives, local(): lax.all_to_all(back.astype(jnp.bfloat16), 'pair', split_axis=0, concat_ax...  8.42 us
    dot_general x1, matrix products, local(): jnp.einsum('phrs,pshd->prhd', probs, value_heads, preferred_element_type=...  6.48 us
    dot_general x1, matrix products, local(): jnp.einsum('prhd,pshd->phrs', query_heads, key_heads, preferred_element_t...  6.1 us
  transfers between devices with their start and end apart: 4, of which 4 were waited for; matrix products, arithmetic and copies ran while one was open for 2% of the time, Pallas kernels for 0%

commit v1 on v0

v1 whole, which is shorter than its diff:
```python
import functools
import math

import jax
import jax.numpy as jnp
from jax import lax
from jax.experimental import pallas as pl
from jax.experimental.pallas import tpu as pltpu
from jax.sharding import PartitionSpec as P

HEAD = 128
LIMIT = 32 * 1024 * 1024


def rms_norm(values, gain):
    spread = jnp.mean(values * values, -1, keepdims=True)
    return values * lax.rsqrt(spread + 1e-06) * gain


def swap(values, bit, axis):
    count = lax.axis_size(axis)
    return lax.ppermute(values, axis, [(i, i ^ bit) for i in range(count)])


def gather_blocks(values, bits):
    for bit in bits:
        values = jnp.concatenate([values, swap(values, bit, "tensor")], 1)
    return values


def halve(values, bit):
    half = values.shape[1] // 2
    return values[:, :half], swap(values[:, half:], bit, "tensor")


def attend_kernel(pair, bits, meta, q_ref, kd_ref, vd_ref, kq_ref, vq_ref, wo_ref, out_ref, ctx_ref):
    slots, blocks, rows, width = q_ref.shape
    keys = blocks * rows
    my_slice = meta[0, 5]
    query, first, second = meta[pair, 0], meta[pair, 1], meta[pair, 2]
    lane = lax.broadcasted_iota(jnp.int32, (1, keys), 1)
    block, row = lane // rows, lane % rows
    origin = jnp.zeros_like(lane)
    for place, bit in enumerate(bits):
        origin = origin + ((block >> place) & 1) * bit
    position = (origin ^ my_slice) * rows + row
    low = jnp.float32(-1e30)
    bias_first = jnp.where(position < meta[pair, 3], 0.0, low)
    bias_second = jnp.where(position < meta[pair, 4], 0.0, low)
    query_keys = kq_ref.shape[1] * kq_ref.shape[2]
    bias = jnp.concatenate([bias_first, bias_second, jnp.zeros((1, query_keys), jnp.float32)], 1)
    scale = math.log2(math.e) / math.sqrt(HEAD)

    def both(ref, at):
        return [ref[first, :, :, at].reshape(keys, HEAD), ref[second, :, :, at].reshape(keys, HEAD)]

    for head in range(width // HEAD):
        at = slice(head * HEAD, (head + 1) * HEAD)
        qs = jnp.concatenate(both(q_ref, at), 0)
        ks = jnp.concatenate(both(kd_ref, at) + [kq_ref[query, :, :, at].reshape(query_keys, HEAD)], 0)
        vs = jnp.concatenate(both(vd_ref, at) + [vq_ref[query, :, :, at].reshape(query_keys, HEAD)], 0)
        scores = lax.dot_general(qs, ks, (((1,), (1,)), ((), ())), preferred_element_type=jnp.float32)
        scores = scores * scale + bias
        top = jnp.max(scores, -1, keepdims=True)
        expo = jnp.exp2(scores - top)
        total = jnp.sum(expo, -1, keepdims=True)
        mixed = jnp.dot(expo.astype(jnp.bfloat16), vs, preferred_element_type=jnp.float32)
        ctx_ref[:, at] = (mixed / total).astype(jnp.bfloat16)
    product = jnp.dot(ctx_ref[...], wo_ref[...], preferred_element_type=jnp.float32)
    out_ref[...] = product.astype(jnp.bfloat16).reshape(out_ref.shape)


def attend(pair, bits, meta, q, kd, vd, kq, vq, w_output):
    slots, blocks, rows, width = q.shape
    model = w_output.shape[1]
    full = lambda a: pl.BlockSpec(a.shape, lambda i, m, n=a.ndim: (0,) * n)
    ops = (q, kd, vd, kq, vq, w_output)
    return pl.pallas_call(
        functools.partial(attend_kernel, pair, bits),
        out_shape=jax.ShapeDtypeStruct((2, blocks, rows, model), jnp.bfloat16),
        grid_spec=pltpu.PrefetchScalarGridSpec(
            num_scalar_prefetch=1,
            grid=(1,),
            in_specs=[full(a) for a in ops],
            out_specs=pl.BlockSpec((2, blocks, rows, model), lambda i, m: (0, 0, 0, 0)),
            scratch_shapes=[pltpu.VMEM((2 * blocks * rows, width), jnp.bfloat16)],
        ),
        compiler_params=pltpu.CompilerParams(vmem_limit_bytes=LIMIT),
        cost_estimate=pl.CostEstimate(
            flops=2 * 2 * blocks * rows * width * (model + 6 * blocks * rows),
            bytes_accessed=2 * model * width,
            transcendentals=width // HEAD * 6 * (blocks * rows) ** 2,
        ),
        name="attend",
    )(meta, *ops)


def settle_kernel(pair, meta, kept_ref, came_ref, rows_ref, gain_ref, hidden_ref, ffn_ref):
    for role in range(2):
        slot = meta[pair, 1 + role]
        summed = kept_ref[role, 0].astype(jnp.float32) + came_ref[role, 0].astype(jnp.float32)
        summed = summed.astype(jnp.bfloat16).astype(jnp.float32)
        hidden = rows_ref[slot].astype(jnp.float32) + summed
        hidden_ref[role] = hidden
        ffn_ref[role, 0] = rms_norm(hidden, gain_ref[...]).astype(jnp.bfloat16)


def settle(pair, meta, kept, came, rows, gain):
    _, _, count, width = kept.shape
    full = lambda a: pl.BlockSpec(a.shape, lambda i, m, n=a.ndim: (0,) * n)
    ops = (kept, came, rows, gain.reshape(1, width))
    return pl.pallas_call(
        functools.partial(settle_kernel, pair),
        out_shape=[
            jax.ShapeDtypeStruct((2, count, width), jnp.float32),
            jax.ShapeDtypeStruct((2, 1, count, width), jnp.bfloat16),
        ],
        grid_spec=pltpu.PrefetchScalarGridSpec(
            num_scalar_prefetch=1,
            grid=(1,),
            in_specs=[full(a) for a in ops],
            out_specs=[
                pl.BlockSpec((2, count, width), lambda i, m: (0, 0, 0)),
                pl.BlockSpec((2, 1, count, width), lambda i, m: (0, 0, 0, 0)),
            ],
        ),
        compiler_params=pltpu.CompilerParams(vmem_limit_bytes=LIMIT),
        name="settle",
    )(meta, *ops)


def expand_kernel(pair, first_call, meta, kept_ref, came_ref, w_ref, *rest):
    old_ref, out_ref = (None, rest[0]) if first_call else rest
    _, half, rows, width = kept_ref.shape
    tall = 2 * half * rows
    tile = w_ref.shape[1]
    tokens = jnp.concatenate(
        [kept_ref[...].reshape(tall, width), came_ref[...].reshape(tall, width)], 0
    )
    units = jnp.maximum(jnp.dot(tokens, w_ref[...], preferred_element_type=jnp.float32), 0.0)
    out_ref[...] = jnp.zeros_like(out_ref) if first_call else old_ref[...]
    for role in range(2):
        slot = meta[pair, 1 + role]
        for part in range(2):
            begin = part * tall + role * half * rows
            new = units[begin : begin + half * rows].reshape(half, rows, tile)
            here = pl.ds(part * half, half)
            held = out_ref[slot, here].astype(jnp.float32)
            out_ref[slot, here] = (held + new.astype(jnp.bfloat16).astype(jnp.float32)).astype(jnp.bfloat16)


def expand(pair, meta, kept, came, w_in, slots, old):
    _, half, rows, width = kept.shape
    units = w_in.shape[1]
    tile = min(1024, units)
    full = lambda a: pl.BlockSpec(a.shape, lambda i, m, n=a.ndim: (0,) * n)
    held = pl.BlockSpec((slots, 2 * half, rows, tile), lambda i, m: (0, 0, 0, i))
    ops = (kept, came, w_in) + (() if old is None else (old,))
    specs = [full(kept), full(came), pl.BlockSpec((width, tile), lambda i, m: (0, i))]
    return pl.pallas_call(
        functools.partial(expand_kernel, pair, old is None),
        out_shape=jax.ShapeDtypeStruct((slots, 2 * half, rows, units), jnp.bfloat16),
        grid_spec=pltpu.PrefetchScalarGridSpec(
            num_scalar_prefetch=1,
            grid=(units // tile,),
            in_specs=specs + ([] if old is None else [held]),
            out_specs=held,
        ),
        input_output_aliases={} if old is None else {4: 0},
        compiler_params=pltpu.CompilerParams(vmem_limit_bytes=LIMIT),
        cost_estimate=pl.CostEstimate(
            flops=2 * 4 * half * rows * width * units,
            bytes_accessed=2 * width * units,
            transcendentals=0,
        ),
        name="expand",
    )(meta, *ops)


def local(
    queries,
    documents,
    doc_len,
    route,
    pair_list,
    attn_gain,
    w_query,
    w_key,
    w_value,
    w_output,
    ffn_gain,
    w_in,
    w_down,
):
    owners = lax.axis_size("pair")
    slices = lax.axis_size("tensor")
    me = lax.axis_index("pair")
    my_slice = lax.axis_index("tensor")
    doc_count, doc_rows, width = documents.shape
    query_count, query_rows, _ = queries.shape
    pairs = pair_list.shape[0]
    slots = min(2 * pairs, owners)
    heads_width = w_query.shape[1]
    down_bits = [1 << i for i in range(slices.bit_length() - 1)]
    up_bits = down_bits[::-1]

    partner = me ^ jnp.arange(owners, dtype=jnp.int32)
    sent = jnp.maximum(lax.dynamic_slice_in_dim(route, me, 1, 0)[0], 0)
    incoming = lax.dynamic_slice_in_dim(route, me, 1, 1)[:, 0]
    source_len = jnp.sum(
        jnp.where(
            (jnp.arange(owners, dtype=jnp.int32) * doc_count + incoming)[:, None]
            == jnp.arange(doc_len.shape[0], dtype=jnp.int32)[None, :],
            doc_len[None, :],
            0,
        ),
        1,
    )
    taken = (incoming >= 0).astype(jnp.int32)
    if slots == owners:
        slot_of_source = partner
    else:
        earlier = jnp.arange(owners)[:, None] > jnp.arange(owners)[None, :]
        slot_of_source = jnp.sum(jnp.where(earlier, taken[None, :], 0), 1)

    def pick(table, index):
        return jnp.sum(jnp.where(jnp.arange(owners, dtype=jnp.int32) == index, table, 0))

    def by_source(table, index):
        return jnp.sum(
            jnp.where(index[:, None] == jnp.arange(owners, dtype=jnp.int32)[None, :], table[None, :], 0), 1
        )

    first, second = pair_list[:, 1], pair_list[:, 2]
    meta = jnp.stack(
        [
            pair_list[:, 0],
            by_source(slot_of_source, first),
            by_source(slot_of_source, second),
            by_source(source_len, first),
            by_source(source_len, second),
            jnp.full((pairs,), my_slice, jnp.int32),
        ],
        1,
    )

    arrived = []
    for k in range(owners):
        block = lax.dynamic_index_in_dim(documents, pick(sent, partner[k]), 0, False)
        arrived.append(block if k == 0 else swap(block, k, "pair"))
    norm = lambda a: rms_norm(a.astype(jnp.float32), attn_gain).astype(jnp.bfloat16)
    own_queries = norm(queries).reshape(1, 1, query_count * query_rows, width)
    if slots == owners:
        rows_own = jnp.stack(arrived)
        early = jnp.concatenate([norm(arrived[0])[None, None], own_queries], 2)
        late = norm(jnp.stack(arrived[1:]))[:, None]
    else:
        place = jnp.stack([jnp.where(pick(taken, partner[k]) > 0, pick(slot_of_source, partner[k]), -1) for k in range(owners)])
        rows_own = jnp.einsum(
            "sk,krd->srd",
            (jnp.arange(slots, dtype=jnp.int32)[:, None] == place[None, :]).astype(jnp.bfloat16),
            jnp.stack(arrived),
            preferred_element_type=jnp.float32,
        ).astype(jnp.bfloat16)
        early = own_queries
        late = norm(rows_own)[:, None]

    early = gather_blocks(early, up_bits)
    late = gather_blocks(late, up_bits)

    def project(rows, w):
        return jnp.einsum("sbrd,de->sbre", rows, w, preferred_element_type=jnp.float32).astype(jnp.bfloat16)

    early_docs = early.shape[2] - query_count * query_rows
    split_queries = lambda a: a[0, :, early_docs:].reshape(slices, query_count, query_rows, heads_width).swapaxes(0, 1)
    early_k, early_v = project(early, w_key), project(early, w_value)
    kq, vq = split_queries(early_k), split_queries(early_v)
    q, kd, vd = project(late, w_query), project(late, w_key), project(late, w_value)
    if early_docs:
        q = jnp.concatenate([project(early[:, :, :early_docs], w_query), q], 0)
        kd = jnp.concatenate([early_k[:, :, :early_docs], kd], 0)
        vd = jnp.concatenate([early_v[:, :, :early_docs], vd], 0)

    hidden, units = [], None
    for pair in range(pairs):
        part = attend(pair, up_bits, meta, q, kd, vd, kq, vq, w_output)
        for bit in down_bits:
            kept, came = halve(part, bit)
            if bit != down_bits[-1]:
                part = kept + came
        own, ffn = settle(pair, meta, kept, came, rows_own, ffn_gain)
        hidden.append(own)
        ffn = gather_blocks(ffn, up_bits[:-1])
        other = swap(ffn, up_bits[-1], "tensor")
        units = expand(pair, meta, ffn, other, w_in, slots, units)

    parts = []
    columns = 2
    step = width // columns
    for c in range(columns):
        part = jnp.einsum(
            "sbrf,fd->sbrd", units, w_down[:, c * step : (c + 1) * step], preferred_element_type=jnp.float32
        ).astype(jnp.bfloat16)
        for bit in down_bits:
            kept, came = halve(part, bit)
            part = kept + came
        parts.append(part[:, 0])
    total = jnp.concatenate(parts, 2).astype(jnp.float32)
    hidden = jnp.stack(hidden)
    picks = meta[:, 1:3, None] == jnp.arange(slots, dtype=jnp.int32)[None, None, :]
    slot_len = jnp.max(jnp.where(picks, meta[:, 3:5, None], 0), (0, 1))
    for p in range(pairs):
        for role in range(2):
            total = total + jnp.where(picks[p, role][:, None, None], hidden[p, role][None], 0.0)
    position = my_slice * doc_rows + jnp.arange(doc_rows, dtype=jnp.int32)
    total = jnp.where((position[None, :] < slot_len[:, None])[:, :, None], total, 0.0).astype(jnp.bfloat16)

    result = jnp.zeros((doc_count, doc_rows, width), jnp.float32)
    outgoing = lax.dynamic_slice_in_dim(route, me, 1, 0)[0]
    for k in range(owners):
        if slots == owners:
            block = total[k]
        else:
            here = (jnp.arange(slots, dtype=jnp.int32) == place[k])[:, None, None]
            block = jnp.sum(jnp.where(here, total.astype(jnp.float32), 0.0), 0).astype(jnp.bfloat16)
        if k:
            block = swap(block, k, "pair")
        target = pick(outgoing, partner[k])
        here = (target == jnp.arange(doc_count, dtype=jnp.int32))[:, None, None]
        result = result + jnp.where(here, block.astype(jnp.float32)[None], 0.0)
    return result.astype(jnp.bfloat16)


def solution(mesh):
    placed = (
        P("pair", "tensor", None),
        P("pair", "tensor", None),
        P(),
        P(),
        P("pair", None),
        P(),
        P(None, "tensor"),
        P(None, "tensor"),
        P(None, "tensor"),
        P("tensor", None),
        P(),
        P(None, "tensor"),
        P("tensor", None),
    )
    return jax.shard_map(
        local, mesh=mesh, in_specs=placed, out_specs=P("pair", "tensor", None), check_vma=False
    )
```

time: 268 us -> 145 us (0.54)
  waiting for transfers between devices: 156 us -> 31 us
  matrix products: 53.4 us -> 14.1 us
  starting transfers between devices: 5.25 us -> 41.5 us
  Pallas kernels: 0 us -> 27.9 us
  other arithmetic: 26.5 us -> 15.7 us
  blocking collectives: 8.42 us -> 0 us
  between operations: 13.3 us -> 8.19 us
    psum x2 -> x0, waiting for transfers between devices: 127 us -> none  [the longest x1 63.6 us: local(): lax.psum(jnp.einsum('pre,ed->prd', context, w_output, preferred_element_t...]
    ppermute x0 -> x36, starting transfers between devices: none -> 41.5 us  [swap(): return lax.ppermute(values, axis, [(i, i ^ bit) for i in range(count)])]
    dot_general x14 -> x8, matrix products: 53.4 us -> 14.1 us  [the longest x6 9.43 us: project(): jnp.einsum('sbrd,de->sbre', rows, w, preferred_element_type=jnp.float32)]
    ppermute x0 -> x36, waiting for transfers between devices: none -> 31 us  [swap(): return lax.ppermute(values, axis, [(i, i ^ bit) for i in range(count)])]
    pallas_call x0 -> x9, Pallas kernels: none -> 27.9 us  [the longest x3 14.5 us: expand(): pl.pallas_call(functools.partial(expand_kernel, pair, old is None), out_s...]
    all_gather x1 -> x0, waiting for transfers between devices: 25.9 us -> none  [local(): tokens_all = lax.all_gather(own_tokens, 'tensor', axis=1, tiled=True)]
    sub x2 -> x0, other arithmetic: 17 us -> none  [the longest x1 17 us: local(): expo = jnp.exp(scores - top)]
    all_to_all x1 -> x0, blocking collectives: 8.42 us -> none  [local(): lax.all_to_all(back.astype(jnp.bfloat16), 'pair', split_axis=0, concat_ax...]
  transfers between devices with their start and end apart: 4 -> 36, of which waited for: 4 -> 17; matrix products, arithmetic and copies ran while one was open for 2% -> 13% of each run, Pallas kernels for 0% -> 13%
where the time goes in v1:
time: 145 us; the launch traced here: 144 us
  starting transfers between devices  41.5 us (29%)
  waiting for transfers between devices  31 us (21%)
  Pallas kernels  27.9 us (19%)
  other arithmetic  15.7 us (11%)
  matrix products  14.1 us (10%)
  between operations  8.19 us (6%)
  local copies, waits for them, and re-layouts  5.72 us (4%)
    ppermute x36, starting transfers between devices, swap(): return lax.ppermute(values, axis, [(i, i ^ bit) for i in range(count)])  41.5 us
    ppermute x36, waiting for transfers between devices, swap(): return lax.ppermute(values, axis, [(i, i ^ bit) for i in range(count)])  31 us
    pallas_call x3, Pallas kernels, expand(): pl.pallas_call(functools.partial(expand_kernel, pair, old is None), out_s...  14.5 us
    pallas_call x3, Pallas kernels, attend(): pl.pallas_call(functools.partial(attend_kernel, pair, bits), out_shape=ja...  11.3 us
    dot_general x6, matrix products, project(): jnp.einsum('sbrd,de->sbre', rows, w, preferred_element_type=jnp.float32)  9.43 us
    dot_general x2, matrix products, local(): jnp.einsum('sbrf,fd->sbrd', units, w_down[:, c * step:(c + 1) * step], pr...  4.65 us
    reduce_sum x1, other arithmetic, pick(): jnp.sum(jnp.where(jnp.arange(owners, dtype=jnp.int32) == index, table, 0))  4.02 us
  transfers between devices with their start and end apart: 36, of which 17 were waited for; matrix products, arithmetic and copies ran while one was open for 13% of the time, Pallas kernels for 13%

profile of v1, /device:TPU:0, one launch (start us, length us, event | category | flops | bytes accessed | tf_op | source)
XLA Modules:
  0.0 144.0 jit_solution(5116147825874656167)
XLA Ops:
  0.7 4.0 %fusion.67 = (s32[]{:T(128)}, s32[]{:T(128)}, s32[]{:T(128)}, s32[]{:T(128)}, s32[]{:T(128)}, /*index=5*/s32[]{:T(128)}, s32[]{:T(128)}, s32[]{:T(128)}) fusion(s32[]{:T(128)} %bitcast, s32[]{:T(128)} %bitcast.11, s32[]{:T(128)} %bitcast.14, s32[]{:T(128)} %bitcast.17, s32[4,4]{1,0:T(4,128)} %param.16, s32[]{:T(128)S(6)} %select_n.99), kind=kLoop, calls=%fused_computation.138 | loop fusion | flops 76 | bytes 68 | tf_op jit(solution)/shard_map/reduce_sum | solution.py:227
  11.3 3.9 %collective-permute-start.5 = (bf16[16,1024]{1,0:T(8,128)(2,1)S(1)}, bf16[16,1024]{1,0:T(8,128)(2,1)S(1)}, u32[]{:S(2)}, u32[]{:S(2)}) collective-permute-start(bf16[16,1024]{1,0:T(8,128)(2,1)S(1)} %get-tuple-element.56), channel_id=1, source_target_pairs={{0,24},{8,16},{16,8},{24,0},{1,25},{9,17},{17,9},{25,1},{2,26},{10... | collective-permute-start | bytes 98312 | tf_op jit(solution)/shard_map/ppermute | solution.py:22
  20.9 3.1 %collective-permute-start = (bf16[1,1,32,1024]{3,2,1,0:T(8,128)(2,1)S(1)}, bf16[1,1,32,1024]{3,2,1,0:T(8,128)(2,1)S(1)}, u32[]{:S(2)}, u32[]{:S(2)}) collective-permute-start(bf16[1,1,32,1024]{3,2,1,0:T(8,128)(2,1)S(1)} %pad_maximum_fusion.13), channel_id=1, source_target_pairs={{0,4},{1,5},{2,6},{3,7},{4,0},{5,1},{6,2},{7,3},{8,12},{9,13},{10,... | collective-permute-start | bytes 196616 | tf_op jit(solution)/shard_map/ppermute | solution.py:22
  30.2 3.6 %collective-permute-done.6 = bf16[3,1,16,1024]{3,2,1,0:T(8,128)(2,1)S(1)} collective-permute-done((bf16[3,1,16,1024]{3,2,1,0:T(8,128)(2,1)S(1)}, bf16[3,1,16,1024]{3,2,1,0:T(8,128)(2,1)S(1)}, u32[]{:S(2)}, u32[]{:S(2)}) %collective-permute-start.6) | collective-permute-done | bytes 98336 | tf_op jit(solution)/shard_map/ppermute | solution.py:22
  40.8 2.3 %fusion.45 = bf16[1,8,32,1024]{3,2,1,0:T(8,128)(2,1)S(1)} fusion(bf16[1024,1024]{1,0:T(8,128)(2,1)} %param.20, bf16[1,4,32,1024]{3,2,1,0:T(8,128)(2,1)S(1)} %collective-permute-done.2, bf16[1,2,32,1024]{3,2,1,0:T(8,128)(2,1)S(1)} %collective-permute-done.1, bf16[1,1,32,1024]{3,2,1,0:T(8,128)(2,1)S(1)} %collective-permute-done, ...), kind=kOutput, calls=%fused_computation.27 | convolution fusion | flops 539754496 | bytes 3145728 | tf_op jit(solution)/shard_map/sbrd,de->sbre/dot_general | solution.py:272
  47.3 2.1 %fusion.19 = bf16[3,8,16,1024]{3,2,1,0:T(8,128)(2,1)S(1)} fusion(bf16[1024,1024]{1,0:T(8,128)(2,1)S(1)} %copy-done.3, bf16[3,4,16,1024]{3,2,1,0:T(8,128)(2,1)S(1)} %collective-permute-done.8, bf16[3,2,16,1024]{3,2,1,0:T(8,128)(2,1)} %collective-permute-done.7, bf16[3,1,16,1024]{3,2,1,0:T(8,128)(2,1)S(1)} %collective-permute-done.6, ...), kind=kOutput, calls=%fused_computation.19 | convolution fusion | flops 806879232 | bytes 3670016 | tf_op jit(solution)/shard_map/sbrd,de->sbre/dot_general | solution.py:272
  52.9 3.7 %attend.3 = bf16[2,8,16,1024]{3,2,1,0:T(8,128)(2,1)S(1)} custom-call(s32[3,6]{1,0:T(4,128)S(1)} %stack.61.meta, bf16[4,8,16,1024]{3,2,1,0:T(8,128)(2,1)S(1)} %get-tuple-element.75.q_ref, bf16[4,8,16,1024]{3,2,1,0:T(8,128)(2,1)S(1)} %get-tuple-element.76.kd_ref, bf16[4,8,16,1024]{3,2,1,0:T(8,128)(2,1)S(1)} %pad_maximum_fusion.2.vd_ref, ...), custom_call_target="tpu_custom_call" | custom-call | flops 939524096 | bytes 2097152 | tf_op jit(solution)/shard_map/attend/pallas_call | solution.py:78
  57.2 3.7 %attend.4 = bf16[2,8,16,1024]{3,2,1,0:T(8,128)(2,1)S(1)} custom-call(s32[3,6]{1,0:T(4,128)S(1)} %stack.61.meta, bf16[4,8,16,1024]{3,2,1,0:T(8,128)(2,1)S(1)} %get-tuple-element.75.q_ref, bf16[4,8,16,1024]{3,2,1,0:T(8,128)(2,1)S(1)} %get-tuple-element.76.kd_ref, bf16[4,8,16,1024]{3,2,1,0:T(8,128)(2,1)S(1)} %pad_maximum_fusion.2.vd_ref, ...), custom_call_target="tpu_custom_call" | custom-call | flops 939524096 | bytes 2097152 | tf_op jit(solution)/shard_map/attend/pallas_call | solution.py:78
  61.1 3.9 %attend.5 = bf16[2,8,16,1024]{3,2,1,0:T(8,128)(2,1)S(1)} custom-call(s32[3,6]{1,0:T(4,128)S(1)} %stack.61.meta, bf16[4,8,16,1024]{3,2,1,0:T(8,128)(2,1)S(1)} %get-tuple-element.75.q_ref, bf16[4,8,16,1024]{3,2,1,0:T(8,128)(2,1)S(1)} %get-tuple-element.76.kd_ref, bf16[4,8,16,1024]{3,2,1,0:T(8,128)(2,1)S(1)} %pad_maximum_fusion.2.vd_ref, ...), custom_call_target="tpu_custom_call" | custom-call | flops 939524096 | bytes 2097152 | tf_op jit(solution)/shard_map/attend/pallas_call | solution.py:78
  76.5 2.4 %collective-permute-done.22 = bf16[2,2,16,1024]{3,2,1,0:T(8,128)(2,1)S(1)} collective-permute-done((bf16[2,2,16,1024]{3,2,1,0:T(8,128)(2,1)S(1)}, bf16[2,2,16,1024]{3,2,1,0:T(8,128)(2,1)S(1)}, u32[]{:S(2)}, u32[]{:S(2)}) %collective-permute-start.22) | collective-permute-done | bytes 131104 | tf_op jit(solution)/shard_map/ppermute | solution.py:22
  80.0 2.7 %collective-permute-start.12 = (bf16[2,1,16,1024]{3,2,1,0:T(8,128)(2,1)S(1)}, bf16[2,1,16,1024]{3,2,1,0:T(8,128)(2,1)S(1)}, u32[]{:S(2)}, u32[]{:S(2)}) collective-permute-start(bf16[2,1,16,1024]{3,2,1,0:T(8,128)(2,1)S(1)} %get-tuple-element.11), channel_id=1, source_target_pairs={{0,4},{1,5},{2,6},{3,7},{4,0},{5,1},{6,2},{7,3},{8,12},{9,13},{10,... | collective-permute-start | bytes 196616 | tf_op jit(solution)/shard_map/ppermute | solution.py:22
  83.9 3.4 %collective-permute-done.23.came_ref = bf16[2,1,16,1024]{3,2,1,0:T(8,128)(2,1)S(1)} collective-permute-done((bf16[2,1,16,1024]{3,2,1,0:T(8,128)(2,1)S(1)}, bf16[2,1,16,1024]{3,2,1,0:T(8,128)(2,1)S(1)}, u32[]{:S(2)}, u32[]{:S(2)}) %collective-permute-start.23) | collective-permute-done | bytes 65568 | tf_op jit(solution)/shard_map/ppermute | solution.py:22
  88.7 3.8 %collective-permute-start.13 = (bf16[2,2,16,1024]{3,2,1,0:T(8,128)(2,1)S(1)}, bf16[2,2,16,1024]{3,2,1,0:T(8,128)(2,1)S(1)}, u32[]{:S(2)}, u32[]{:S(2)}) collective-permute-start(bf16[2,2,16,1024]{3,2,1,0:T(8,128)(2,1)S(1)} %pad_maximum_fusion.10), channel_id=1, source_target_pairs={{0,2},{1,3},{2,0},{3,1},{4,6},{5,7},{6,4},{7,5},{8,10},{9,11},{10,... | collective-permute-start | bytes 393224 | tf_op jit(solution)/shard_map/ppermute | solution.py:22
  93.3 2.2 %collective-permute-start.25 = (bf16[2,2,16,1024]{3,2,1,0:T(8,128)(2,1)S(1)}, bf16[2,2,16,1024]{3,2,1,0:T(8,128)(2,1)S(1)}, u32[]{:S(2)}, u32[]{:S(2)}) collective-permute-start(bf16[2,2,16,1024]{3,2,1,0:T(8,128)(2,1)S(1)} %pad_maximum_fusion.12), channel_id=1, source_target_pairs={{0,2},{1,3},{2,0},{3,1},{4,6},{5,7},{6,4},{7,5},{8,10},{9,11},{10,... | collective-permute-start | bytes 393224 | tf_op jit(solution)/shard_map/ppermute | solution.py:22
  95.5 4.2 %collective-permute-done.25 = bf16[2,2,16,1024]{3,2,1,0:T(8,128)(2,1)S(1)} collective-permute-done((bf16[2,2,16,1024]{3,2,1,0:T(8,128)(2,1)S(1)}, bf16[2,2,16,1024]{3,2,1,0:T(8,128)(2,1)S(1)}, u32[]{:S(2)}, u32[]{:S(2)}) %collective-permute-start.25) | collective-permute-done | bytes 131104 | tf_op jit(solution)/shard_map/ppermute | solution.py:22
  101.3 4.8 %expand.3.rest_0_ = bf16[4,8,16,4096]{3,2,1,0:T(8,128)(2,1)S(1)} custom-call(s32[3,6]{1,0:T(4,128)S(1)} %stack.61.meta, bf16[2,4,16,1024]{3,2,1,0:T(8,128)(2,1)S(1)} %constant_dynamic-update-slice_fusion.6.kept_ref, bf16[2,4,16,1024]{3,2,1,0:T(8,128)(2,1)S(1)} %collective-permute-done.26.came_ref, bf16[1024,4096]{1,0:T(8,128)(2,1)S(1)} %bitcast.153), custom_call_target="tpu_custom_call" | custom-call | flops 2147483648 | bytes 8388608 | tf_op jit(solution)/shard_map/expand/pallas_call | solution.py:160
  106.1 4.9 %expand.4.rest_0_ = bf16[4,8,16,4096]{3,2,1,0:T(8,128)(2,1)S(1)} custom-call(s32[3,6]{1,0:T(4,128)S(1)} %stack.61.meta, bf16[2,4,16,1024]{3,2,1,0:T(8,128)(2,1)S(1)} %constant_dynamic-update-slice_fusion.3.kept_ref, bf16[2,4,16,1024]{3,2,1,0:T(8,128)(2,1)S(1)} %collective-permute-done.20.came_ref, ...), custom_call_target="tpu_custom_call", output_to_operand_aliasing={{}: (4, {})} | custom-call | flops 2147483648 | bytes 8388608 | tf_op jit(solution)/shard_map/expand/pallas_call | solution.py:160
  111.0 4.9 %expand.5 = bf16[4,8,16,4096]{3,2,1,0:T(8,128)(2,1)S(1)} custom-call(s32[3,6]{1,0:T(4,128)S(1)} %stack.61.meta, bf16[2,4,16,1024]{3,2,1,0:T(8,128)(2,1)S(1)} %constant_dynamic-update-slice_fusion.kept_ref, bf16[2,4,16,1024]{3,2,1,0:T(8,128)(2,1)S(1)} %collective-permute-done.14.came_ref, ...), custom_call_target="tpu_custom_call", output_to_operand_aliasing={{}: (4, {})} | custom-call | flops 2147483648 | bytes 8388608 | tf_op jit(solution)/shard_map/expand/pallas_call | solution.py:160
  115.9 2.3 %fusion.28 = bf16[4,8,16,512]{3,2,0,1:T(8,128)(2,1)S(1)} fusion(bf16[4096,1024]{1,0:T(8,128)(2,1)S(1)} %bitcast.178, bf16[4,8,16,4096]{3,2,1,0:T(8,128)(2,1)S(1)} %expand.5), kind=kOutput, calls=%fused_computation.22 | convolution fusion | flops 2147745792 | bytes 8912896 | tf_op jit(solution)/shard_map/sbrf,fd->sbrd/dot_general | solution.py:301
  118.5 2.3 %fusion.33 = bf16[4,8,16,512]{3,2,1,0:T(8,128)(2,1)S(1)} fusion(bf16[4,8,16,4096]{3,2,1,0:T(8,128)(2,1)S(1)} %expand.5, bf16[4096,1024]{1,0:T(8,128)(2,1)S(1)} %bitcast.178), kind=kOutput, calls=%fused_computation.23 | convolution fusion | flops 2147745792 | bytes 8912896 | tf_op jit(solution)/shard_map/sbrf,fd->sbrd/dot_general | solution.py:301
  123.6 4.2 %collective-permute-done.31 = bf16[4,2,16,512]{3,2,0,1:T(8,128)(2,1)S(1)} collective-permute-done((bf16[4,2,16,512]{3,2,0,1:T(8,128)(2,1)S(1)}, bf16[4,2,16,512]{3,2,0,1:T(8,128)(2,1)S(1)}, u32[]{:S(2)}, u32[]{:S(2)}) %collective-permute-start.31) | collective-permute-done | bytes 131104 | tf_op jit(solution)/shard_map/ppermute | solution.py:22
  127.8 2.2 %collective-permute-start.32 = (bf16[4,1,16,512]{3,2,0,1:T(8,128)(2,1)S(1)}, bf16[4,1,16,512]{3,2,0,1:T(8,128)(2,1)S(1)}, u32[]{:S(2)}, u32[]{:S(2)}) collective-permute-start(bf16[4,1,16,512]{3,2,0,1:T(8,128)(2,1)S(1)} %slice.282), channel_id=1, source_target_pairs={{0,4},{1,5},{2,6},{3,7},{4,0},{5,1},{6,2},{7,3},{8,12},{9,13},{10,... | collective-permute-start | bytes 196616 | tf_op jit(solution)/shard_map/ppermute | solution.py:22
  130.0 2.8 %collective-permute-start.29 = (bf16[4,1,16,512]{3,2,1,0:T(8,128)(2,1)S(1)}, bf16[4,1,16,512]{3,2,1,0:T(8,128)(2,1)S(1)}, u32[]{:S(2)}, u32[]{:S(2)}) collective-permute-start(bf16[4,1,16,512]{3,2,1,0:T(8,128)(2,1)S(1)} %slice.276), channel_id=1, source_target_pairs={{0,4},{1,5},{2,6},{3,7},{4,0},{5,1},{6,2},{7,3},{8,12},{9,13},{10,... | collective-permute-start | bytes 196616 | tf_op jit(solution)/shard_map/ppermute | solution.py:22
  136.1 2.6 %collective-permute-start.35 = (bf16[16,1024]{1,0:T(8,128)(2,1)S(1)}, bf16[16,1024]{1,0:T(8,128)(2,1)S(1)}, u32[]{:S(2)}, u32[]{:S(2)}) collective-permute-start(bf16[16,1024]{1,0:T(8,128)(2,1)S(1)} %get-tuple-element.40), channel_id=1, source_target_pairs={{0,24},{8,16},{16,8},{24,0},{1,25},{9,17},{17,9},{25,1},{2,26},{10... | collective-permute-start | bytes 98312 | tf_op jit(solution)/shard_map/ppermute | solution.py:22
  (177 shorter events, 55.9 us)
Async XLA Ops:
  11.3 16.0 %collective-permute-start.5 = (bf16[16,1024]{1,0:T(8,128)(2,1)S(1)}, bf16[16,1024]{1,0:T(8,128)(2,1)S(1)}, u32[]{:S(2)}, u32[]{:S(2)}) collective-permute-start(bf16[16,1024]{1,0:T(8,128)(2,1)S(1)} %get-tuple-element.56), channel_id=1, source_target_pairs={{0,24},{8,16},{16,8},{24,0},{1,25},{9,17},{17,9},{25,1},{2,26},{10... | collective-permute-start | bytes 98312 | tf_op jit(solution)/shard_map/ppermute | solution.py:22
  15.2 12.0 %collective-permute-start.4 = (bf16[16,1024]{1,0:T(8,128)(2,1)S(1)}, bf16[16,1024]{1,0:T(8,128)(2,1)S(1)}, u32[]{:S(2)}, u32[]{:S(2)}) collective-permute-start(bf16[16,1024]{1,0:T(8,128)(2,1)S(1)} %get-tuple-element.57), channel_id=1, source_target_pairs={{0,16},{8,24},{16,0},{24,8},{1,17},{9,25},{17,1},{25,9},{2,18},{10... | collective-permute-start | bytes 98312 | tf_op jit(solution)/shard_map/ppermute | solution.py:22
  15.8 11.5 %collective-permute-start.3 = (bf16[16,1024]{1,0:T(8,128)(2,1)S(1)}, bf16[16,1024]{1,0:T(8,128)(2,1)S(1)}, u32[]{:S(2)}, u32[]{:S(2)}) collective-permute-start(bf16[16,1024]{1,0:T(8,128)(2,1)S(1)} %get-tuple-element.55), channel_id=1, source_target_pairs={{0,8},{8,0},{16,24},{24,16},{1,9},{9,1},{17,25},{25,17},{2,10},{10... | collective-permute-start | bytes 98312 | tf_op jit(solution)/shard_map/ppermute | solution.py:22
  20.9 7.3 %collective-permute-start = (bf16[1,1,32,1024]{3,2,1,0:T(8,128)(2,1)S(1)}, bf16[1,1,32,1024]{3,2,1,0:T(8,128)(2,1)S(1)}, u32[]{:S(2)}, u32[]{:S(2)}) collective-permute-start(bf16[1,1,32,1024]{3,2,1,0:T(8,128)(2,1)S(1)} %pad_maximum_fusion.13), channel_id=1, source_target_pairs={{0,4},{1,5},{2,6},{3,7},{4,0},{5,1},{6,2},{7,3},{8,12},{9,13},{10,... | collective-permute-start | bytes 196616 | tf_op jit(solution)/shard_map/ppermute | solution.py:22
  28.3 7.7 %collective-permute-start.1 = (bf16[1,2,32,1024]{3,2,1,0:T(8,128)(2,1)S(1)}, bf16[1,2,32,1024]{3,2,1,0:T(8,128)(2,1)S(1)}, u32[]{:S(2)}, u32[]{:S(2)}) collective-permute-start(bf16[1,2,32,1024]{3,2,1,0:T(8,128)(2,1)S(1)} %pad_maximum_fusion.8), channel_id=1, source_target_pairs={{0,2},{1,3},{2,0},{3,1},{4,6},{5,7},{6,4},{7,5},{8,10},{9,11},{10,... | collective-permute-start | bytes 393224 | tf_op jit(solution)/shard_map/ppermute | solution.py:22
  33.9 5.8 %collective-permute-start.7 = (bf16[3,2,16,1024]{3,2,1,0:T(8,128)(2,1)S(1)}, bf16[3,2,16,1024]{3,2,1,0:T(8,128)(2,1)}, u32[]{:S(2)}, u32[]{:S(2)}) collective-permute-start(bf16[3,2,16,1024]{3,2,1,0:T(8,128)(2,1)S(1)} %pad_maximum_fusion.7), channel_id=1, source_target_pairs={{0,2},{1,3},{2,0},{3,1},{4,6},{5,7},{6,4},{7,5},{8,10},{9,11},{10,... | collective-permute-start | bytes 589832 | tf_op jit(solution)/shard_map/ppermute | solution.py:22
  56.7 8.9 %collective-permute-start.9 = (bf16[2,4,16,1024]{3,2,1,0:T(8,128)(2,1)S(1)}, bf16[2,4,16,1024]{3,2,1,0:T(8,128)(2,1)S(1)}, u32[]{:S(2)}, u32[]{:S(2)}) collective-permute-start(bf16[2,4,16,1024]{3,2,1,0:T(8,128)(2,1)S(1)} %slice.254), channel_id=1, source_target_pairs={{0,1},{1,0},{2,3},{3,2},{4,5},{5,4},{6,7},{7,6},{8,9},{9,8},{10,11... | collective-permute-start | bytes 786440 | tf_op jit(solution)/shard_map/ppermute | solution.py:22
  61.0 6.7 %collective-permute-start.15 = (bf16[2,4,16,1024]{3,2,1,0:T(8,128)(2,1)S(1)}, bf16[2,4,16,1024]{3,2,1,0:T(8,128)(2,1)S(1)}, u32[]{:S(2)}, u32[]{:S(2)}) collective-permute-start(bf16[2,4,16,1024]{3,2,1,0:T(8,128)(2,1)S(1)} %slice.260), channel_id=1, source_target_pairs={{0,1},{1,0},{2,3},{3,2},{4,5},{5,4},{6,7},{7,6},{8,9},{9,8},{10,11... | collective-permute-start | bytes 786440 | tf_op jit(solution)/shard_map/ppermute | solution.py:22
  65.6 6.4 %collective-permute-start.10 = (bf16[2,2,16,1024]{3,2,1,0:T(8,128)(2,1)S(1)}, bf16[2,2,16,1024]{3,2,1,0:T(8,128)(2,1)S(1)}, u32[]{:S(2)}, u32[]{:S(2)}) collective-permute-start(bf16[2,2,16,1024]{3,2,1,0:T(8,128)(2,1)S(1)} %slice.256), channel_id=1, source_target_pairs={{0,2},{1,3},{2,0},{3,1},{4,6},{5,7},{6,4},{7,5},{8,10},{9,11},{10,... | collective-permute-start | bytes 393224 | tf_op jit(solution)/shard_map/ppermute | solution.py:22
  67.7 7.8 %collective-permute-start.16 = (bf16[2,2,16,1024]{3,2,1,0:T(8,128)(2,1)S(1)}, bf16[2,2,16,1024]{3,2,1,0:T(8,128)(2,1)S(1)}, u32[]{:S(2)}, u32[]{:S(2)}) collective-permute-start(bf16[2,2,16,1024]{3,2,1,0:T(8,128)(2,1)S(1)} %slice.262), channel_id=1, source_target_pairs={{0,2},{1,3},{2,0},{3,1},{4,6},{5,7},{6,4},{7,5},{8,10},{9,11},{10,... | collective-permute-start | bytes 393224 | tf_op jit(solution)/shard_map/ppermute | solution.py:22
  67.9 11.1 %collective-permute-start.22 = (bf16[2,2,16,1024]{3,2,1,0:T(8,128)(2,1)S(1)}, bf16[2,2,16,1024]{3,2,1,0:T(8,128)(2,1)S(1)}, u32[]{:S(2)}, u32[]{:S(2)}) collective-permute-start(bf16[2,2,16,1024]{3,2,1,0:T(8,128)(2,1)S(1)} %slice.268), channel_id=1, source_target_pairs={{0,2},{1,3},{2,0},{3,1},{4,6},{5,7},{6,4},{7,5},{8,10},{9,11},{10,... | collective-permute-start | bytes 393224 | tf_op jit(solution)/shard_map/ppermute | solution.py:22
  72.0 7.3 %collective-permute-start.11 = (bf16[2,1,16,1024]{3,2,1,0:T(8,128)(2,1)S(1)}, bf16[2,1,16,1024]{3,2,1,0:T(8,128)(2,1)S(1)}, u32[]{:S(2)}, u32[]{:S(2)}) collective-permute-start(bf16[2,1,16,1024]{3,2,1,0:T(8,128)(2,1)S(1)} %get-tuple-element.53), channel_id=1, source_target_pairs={{0,4},{1,5},{2,6},{3,7},{4,0},{5,1},{6,2},{7,3},{8,12},{9,13},{10,... | collective-permute-start | bytes 196616 | tf_op jit(solution)/shard_map/ppermute | solution.py:22
  75.6 7.2 %collective-permute-start.17 = (bf16[2,1,16,1024]{3,2,1,0:T(8,128)(2,1)S(1)}, bf16[2,1,16,1024]{3,2,1,0:T(8,128)(2,1)S(1)}, u32[]{:S(2)}, u32[]{:S(2)}) collective-permute-start(bf16[2,1,16,1024]{3,2,1,0:T(8,128)(2,1)S(1)} %get-tuple-element.51), channel_id=1, source_target_pairs={{0,4},{1,5},{2,6},{3,7},{4,0},{5,1},{6,2},{7,3},{8,12},{9,13},{10,... | collective-permute-start | bytes 196616 | tf_op jit(solution)/shard_map/ppermute | solution.py:22
  79.0 8.3 %collective-permute-start.23 = (bf16[2,1,16,1024]{3,2,1,0:T(8,128)(2,1)S(1)}, bf16[2,1,16,1024]{3,2,1,0:T(8,128)(2,1)S(1)}, u32[]{:S(2)}, u32[]{:S(2)}) collective-permute-start(bf16[2,1,16,1024]{3,2,1,0:T(8,128)(2,1)S(1)} %get-tuple-element.49), channel_id=1, source_target_pairs={{0,4},{1,5},{2,6},{3,7},{4,0},{5,1},{6,2},{7,3},{8,12},{9,13},{10,... | collective-permute-start | bytes 196616 | tf_op jit(solution)/shard_map/ppermute | solution.py:22
  80.0 8.7 %collective-permute-start.12 = (bf16[2,1,16,1024]{3,2,1,0:T(8,128)(2,1)S(1)}, bf16[2,1,16,1024]{3,2,1,0:T(8,128)(2,1)S(1)}, u32[]{:S(2)}, u32[]{:S(2)}) collective-permute-start(bf16[2,1,16,1024]{3,2,1,0:T(8,128)(2,1)S(1)} %get-tuple-element.11), channel_id=1, source_target_pairs={{0,4},{1,5},{2,6},{3,7},{4,0},{5,1},{6,2},{7,3},{8,12},{9,13},{10,... | collective-permute-start | bytes 196616 | tf_op jit(solution)/shard_map/ppermute | solution.py:22
  83.5 9.1 %collective-permute-start.18 = (bf16[2,1,16,1024]{3,2,1,0:T(8,128)(2,1)S(1)}, bf16[2,1,16,1024]{3,2,1,0:T(8,128)(2,1)S(1)}, u32[]{:S(2)}, u32[]{:S(2)}) collective-permute-start(bf16[2,1,16,1024]{3,2,1,0:T(8,128)(2,1)S(1)} %get-tuple-element.12), channel_id=1, source_target_pairs={{0,4},{1,5},{2,6},{3,7},{4,0},{5,1},{6,2},{7,3},{8,12},{9,13},{10,... | collective-permute-start | bytes 196616 | tf_op jit(solution)/shard_map/ppermute | solution.py:22
  88.7 11.7 %collective-permute-start.13 = (bf16[2,2,16,1024]{3,2,1,0:T(8,128)(2,1)S(1)}, bf16[2,2,16,1024]{3,2,1,0:T(8,128)(2,1)S(1)}, u32[]{:S(2)}, u32[]{:S(2)}) collective-permute-start(bf16[2,2,16,1024]{3,2,1,0:T(8,128)(2,1)S(1)} %pad_maximum_fusion.10), channel_id=1, source_target_pairs={{0,2},{1,3},{2,0},{3,1},{4,6},{5,7},{6,4},{7,5},{8,10},{9,11},{10,... | collective-permute-start | bytes 393224 | tf_op jit(solution)/shard_map/ppermute | solution.py:22
  92.6 7.2 %collective-permute-start.19 = (bf16[2,2,16,1024]{3,2,1,0:T(8,128)(2,1)S(1)}, bf16[2,2,16,1024]{3,2,1,0:T(8,128)(2,1)S(1)}, u32[]{:S(2)}, u32[]{:S(2)}) collective-permute-start(bf16[2,2,16,1024]{3,2,1,0:T(8,128)(2,1)S(1)} %pad_maximum_fusion.11), channel_id=1, source_target_pairs={{0,2},{1,3},{2,0},{3,1},{4,6},{5,7},{6,4},{7,5},{8,10},{9,11},{10,... | collective-permute-start | bytes 393224 | tf_op jit(solution)/shard_map/ppermute | solution.py:22
  93.3 6.4 %collective-permute-start.25 = (bf16[2,2,16,1024]{3,2,1,0:T(8,128)(2,1)S(1)}, bf16[2,2,16,1024]{3,2,1,0:T(8,128)(2,1)S(1)}, u32[]{:S(2)}, u32[]{:S(2)}) collective-permute-start(bf16[2,2,16,1024]{3,2,1,0:T(8,128)(2,1)S(1)} %pad_maximum_fusion.12), channel_id=1, source_target_pairs={{0,2},{1,3},{2,0},{3,1},{4,6},{5,7},{6,4},{7,5},{8,10},{9,11},{10,... | collective-permute-start | bytes 393224 | tf_op jit(solution)/shard_map/ppermute | solution.py:22
  99.8 6.3 %collective-permute-start.20 = (bf16[2,4,16,1024]{3,2,1,0:T(8,128)(2,1)S(1)}, bf16[2,4,16,1024]{3,2,1,0:T(8,128)(2,1)S(1)}, u32[]{:S(2)}, u32[]{:S(2)}) collective-permute-start(bf16[2,4,16,1024]{3,2,1,0:T(8,128)(2,1)S(1)} %constant_dynamic-update-slice_fusion.3.kept_ref), channel_id=1, source_target_pairs={{0,1},{1,0},{2,3},{3,2},{4,5},{5,4},{6,7},{7,6},{8,9},{9,8},{10,11... | collective-permute-start | bytes 786440 | tf_op jit(solution)/shard_map/ppermute | solution.py:22
  100.4 10.6 %collective-permute-start.14 = (bf16[2,4,16,1024]{3,2,1,0:T(8,128)(2,1)S(1)}, bf16[2,4,16,1024]{3,2,1,0:T(8,128)(2,1)S(1)}, u32[]{:S(2)}, u32[]{:S(2)}) collective-permute-start(bf16[2,4,16,1024]{3,2,1,0:T(8,128)(2,1)S(1)} %constant_dynamic-update-slice_fusion.kept_ref), channel_id=1, source_target_pairs={{0,1},{1,0},{2,3},{3,2},{4,5},{5,4},{6,7},{7,6},{8,9},{9,8},{10,11... | collective-permute-start | bytes 786440 | tf_op jit(solution)/shard_map/ppermute | solution.py:22
  121.4 6.4 %collective-permute-start.31 = (bf16[4,2,16,512]{3,2,0,1:T(8,128)(2,1)S(1)}, bf16[4,2,16,512]{3,2,0,1:T(8,128)(2,1)S(1)}, u32[]{:S(2)}, u32[]{:S(2)}) collective-permute-start(bf16[4,2,16,512]{3,2,0,1:T(8,128)(2,1)S(1)} %slice.280), channel_id=1, source_target_pairs={{0,2},{1,3},{2,0},{3,1},{4,6},{5,7},{6,4},{7,5},{8,10},{9,11},{10,... | collective-permute-start | bytes 393224 | tf_op jit(solution)/shard_map/ppermute | solution.py:22
  122.5 7.5 %collective-permute-start.28 = (bf16[4,2,16,512]{3,2,1,0:T(8,128)(2,1)S(1)}, bf16[4,2,16,512]{3,2,1,0:T(8,128)(2,1)S(1)}, u32[]{:S(2)}, u32[]{:S(2)}) collective-permute-start(bf16[4,2,16,512]{3,2,1,0:T(8,128)(2,1)S(1)} %slice.274), channel_id=1, source_target_pairs={{0,2},{1,3},{2,0},{3,1},{4,6},{5,7},{6,4},{7,5},{8,10},{9,11},{10,... | collective-permute-start | bytes 393224 | tf_op jit(solution)/shard_map/ppermute | solution.py:22
  127.8 7.0 %collective-permute-start.32 = (bf16[4,1,16,512]{3,2,0,1:T(8,128)(2,1)S(1)}, bf16[4,1,16,512]{3,2,0,1:T(8,128)(2,1)S(1)}, u32[]{:S(2)}, u32[]{:S(2)}) collective-permute-start(bf16[4,1,16,512]{3,2,0,1:T(8,128)(2,1)S(1)} %slice.282), channel_id=1, source_target_pairs={{0,4},{1,5},{2,6},{3,7},{4,0},{5,1},{6,2},{7,3},{8,12},{9,13},{10,... | collective-permute-start | bytes 196616 | tf_op jit(solution)/shard_map/ppermute | solution.py:22
  (21 other events, 210.6 us)

commit v2 on v0

v2 whole, which is shorter than its diff:
```python
import functools
import math

import jax
import jax.numpy as jnp
from jax import lax
from jax.experimental import pallas as pl
from jax.experimental.pallas import tpu as pltpu
from jax.sharding import PartitionSpec as P

HEAD = 128
MIB = 1024 * 1024


def rms_norm(values, gain):
    spread = jnp.mean(values * values, -1, keepdims=True)
    return values * lax.rsqrt(spread + 1e-06) * gain


def swap(values, bit, axis):
    count = lax.axis_size(axis)
    return lax.ppermute(values, axis, [(i, i ^ bit) for i in range(count)])


def gather_blocks(values, bits):
    for bit in bits:
        values = jnp.concatenate([values, swap(values, bit, "tensor")], 1)
    return values


def halve(values, bit):
    half = values.shape[1] // 2
    return values[:, :half], swap(values[:, half:], bit, "tensor")


def kernel_call(kernel, name, operands, out_shape, scratch=(), smem=(), out_smem=(), limit=16, flops=0, moved=0, exps=0):
    space = lambda yes: pl.BlockSpec(memory_space=pltpu.SMEM if yes else pltpu.VMEM)
    return pl.pallas_call(
        kernel,
        out_shape=out_shape,
        in_specs=[space(i in smem) for i in range(len(operands))],
        out_specs=[space(i in out_smem) for i in range(len(out_shape))],
        scratch_shapes=list(scratch),
        compiler_params=pltpu.CompilerParams(vmem_limit_bytes=limit * MIB),
        cost_estimate=pl.CostEstimate(flops=flops, bytes_accessed=moved, transcendentals=exps),
        name=name,
    )(*operands)


def bf16(*shape):
    return jax.ShapeDtypeStruct(shape, jnp.bfloat16)


def start_kernel(slots, route_ref, len_ref, list_ref, docs_ref, queries_ref, gain_ref, meta_ref, early_ref, *send_refs):
    owners = route_ref.shape[0]
    doc_count, doc_rows, width = docs_ref.shape
    me = lax.axis_index("pair")
    for k in range(owners):
        picked = docs_ref[jnp.maximum(route_ref[me, me ^ k], 0)]
        send_refs[k][...] = picked
        if k == 0 and slots == owners:
            own = picked.astype(jnp.float32)
            early_ref[1, 0] = rms_norm(own, gain_ref[...]).astype(jnp.bfloat16)
    tokens = queries_ref[...].astype(jnp.float32).reshape(early_ref.shape[2], width)
    early_ref[0, 0] = rms_norm(tokens, gain_ref[...]).astype(jnp.bfloat16)
    for p in range(list_ref.shape[0]):
        meta_ref[p, 0] = list_ref[p, 0]
        for role in range(2):
            source = list_ref[p, 1 + role]
            if slots == owners:
                slot = source ^ me
            else:
                slot = jnp.int32(0)
                for j in range(owners):
                    slot = slot + jnp.where((j < source) & (route_ref[j, me] >= 0), 1, 0)
            meta_ref[p, 1 + role] = slot
            meta_ref[p, 3 + role] = len_ref[source * doc_count + jnp.maximum(route_ref[source, me], 0)]
        meta_ref[p, 5] = lax.axis_index("tensor")


def late_kernel(count, *refs):
    arrived, gain_ref = refs[:count], refs[count]
    raw_ref, late_ref = refs[count + 1 :]
    skip = count - late_ref.shape[0]
    for k in range(count):
        raw_ref[k] = arrived[k][...]
        if k >= skip:
            late_ref[k - skip, 0] = rms_norm(arrived[k][...].astype(jnp.float32), gain_ref[...]).astype(jnp.bfloat16)


def project_kernel(lead, kept_ref, came_ref, wq_ref, wk_ref, wv_ref, *refs):
    old, (q_ref, k_ref, v_ref) = refs[: len(refs) - 3], refs[len(refs) - 3 :]
    slots, half, rows, width = kept_ref.shape
    group = half * rows
    tall = slots * group
    tokens = jnp.concatenate([kept_ref[...].reshape(tall, width), came_ref[...].reshape(tall, width)], 0)
    scale = math.log2(math.e) / math.sqrt(HEAD)
    base_q, base_kv = 0, 0
    if old:
        base_q, base_kv = old[0].shape[0] if len(old) == 3 else 0, old[-1].shape[0]
        for ref, new_ref in zip(old, (q_ref, k_ref, v_ref)[3 - len(old) :]):
            new_ref[: ref.shape[0]] = ref[...]

    def store(ref, values, first, base):
        count = slots - first
        for part in range(2):
            for s in range(count):
                begin = part * count * group + s * group
                ref[base + s, part * half : (part + 1) * half] = (
                    values[begin : begin + group].astype(jnp.bfloat16).reshape(half, rows, values.shape[1])
                )

    if lead == slots:
        q_ref[...] = jnp.zeros_like(q_ref)
    else:
        asking = tokens
        if lead:
            asking = jnp.concatenate([tokens[lead * group : tall], tokens[tall + lead * group :]], 0)
        store(q_ref, jnp.dot(asking, wq_ref[...], preferred_element_type=jnp.float32) * scale, lead, base_q)
    store(k_ref, jnp.dot(tokens, wk_ref[...], preferred_element_type=jnp.float32), 0, base_kv)
    store(v_ref, jnp.dot(tokens, wv_ref[...], preferred_element_type=jnp.float32), 0, base_kv)


def project(name, lead, kept, came, weights, old):
    slots, half, rows, width = kept.shape
    wide = weights[0].shape[1]
    have_q = old[0].shape[0] if len(old) == 3 else 0
    have_kv = old[-1].shape[0] if old else 0
    nq, nkv = max(have_q + slots - lead, 1), have_kv + slots
    shape = lambda n: bf16(n, 2 * half, rows, wide)
    return kernel_call(
        functools.partial(project_kernel, lead),
        name,
        (kept, came, *weights, *old),
        [shape(nq), shape(nkv), shape(nkv)],
        limit=32,
        flops=2 * 2 * half * rows * width * wide * (3 * slots - lead),
        moved=6 * width * wide,
    )


def attend_kernel(pair, bits, query_rows, meta, q_ref, k_ref, v_ref, wo_ref, out_ref, next_ref, ctx_ref):
    _, blocks, rows, width = q_ref.shape
    keys = blocks * rows
    for a in range(meta.shape[0]):
        for b in range(meta.shape[1]):
            next_ref[a, b] = meta[a, b]
    my_slice, query = meta[0, 5], meta[pair, 0]
    first, second = meta[pair, 1], meta[pair, 2]
    lane = lax.broadcasted_iota(jnp.int32, (1, keys), 1)
    block, row = lane // rows, lane % rows
    origin = jnp.zeros_like(lane)
    for place, bit in enumerate(bits):
        origin = origin + ((block >> place) & 1) * bit
    position = (origin ^ my_slice) * rows + row
    keep = lambda yes: jnp.where(yes, 0.0, jnp.float32(-1e30))
    bias = jnp.concatenate(
        [
            keep(position < meta[pair, 3]),
            keep(position < meta[pair, 4]),
            keep((row >= query * query_rows) & (row < (query + 1) * query_rows)),
        ],
        1,
    )

    def rows_of(ref, places, at):
        return jnp.concatenate([ref[place, :, :, at].reshape(keys, HEAD) for place in places], 0)

    ones = jnp.ones((3 * keys, HEAD), jnp.bfloat16)
    for head in range(width // HEAD):
        at = slice(head * HEAD, (head + 1) * HEAD)
        qs = rows_of(q_ref, (first, second), at)
        ks = rows_of(k_ref, (first + 1, second + 1, 0), at)
        vs = rows_of(v_ref, (first + 1, second + 1, 0), at)
        scores = lax.dot_general(qs, ks, (((1,), (1,)), ((), ())), preferred_element_type=jnp.float32) + bias
        top = jnp.max(scores, -1, keepdims=True)
        expo = jnp.exp2(scores - top).astype(jnp.bfloat16)
        mixed = jnp.dot(expo, jnp.concatenate([vs, ones], 1), preferred_element_type=jnp.float32)
        ctx_ref[:, at] = (mixed[:, :HEAD] / mixed[:, HEAD:]).astype(jnp.bfloat16)
    product = jnp.dot(ctx_ref[...], wo_ref[...], preferred_element_type=jnp.float32)
    out_ref[...] = product.astype(jnp.bfloat16).reshape(out_ref.shape)


def attend(pair, bits, query_rows, meta, q, k, v, w_output):
    _, blocks, rows, width = q.shape
    model = w_output.shape[1]
    tall = 2 * blocks * rows
    return kernel_call(
        functools.partial(attend_kernel, pair, bits, query_rows),
        "attend",
        (meta, q, k, v, w_output),
        [bf16(2, blocks, rows, model), jax.ShapeDtypeStruct(meta.shape, jnp.int32)],
        scratch=[pltpu.VMEM((tall, width), jnp.bfloat16)],
        smem=(0,),
        out_smem=(1,),
        flops=2 * tall * width * (model + 3 * tall),
        moved=2 * model * width,
        exps=width // HEAD * tall * tall * 3 // 2,
    )


def settle_kernel(pair, meta, kept_ref, came_ref, rows_ref, gain_ref, hidden_ref, ffn_ref):
    for role in range(2):
        slot = meta[pair, 1 + role]
        summed = kept_ref[role, 0].astype(jnp.float32) + came_ref[role, 0].astype(jnp.float32)
        hidden = rows_ref[slot].astype(jnp.float32) + summed
        hidden_ref[role] = hidden
        ffn_ref[role, 0] = rms_norm(hidden, gain_ref[...]).astype(jnp.bfloat16)


def settle(pair, meta, kept, came, rows, gain):
    _, _, count, width = kept.shape
    return kernel_call(
        functools.partial(settle_kernel, pair),
        "settle",
        (meta, kept, came, rows, gain),
        [jax.ShapeDtypeStruct((2, count, width), jnp.float32), bf16(2, 1, count, width)],
        smem=(0,),
    )


def expand_kernel(pair, tile, meta, kept_ref, came_ref, w_ref, *rest):
    old_ref, (out_ref,) = (rest[0] if len(rest) == 2 else None), rest[-1:]
    _, half, rows, width = kept_ref.shape
    group = half * rows
    tokens = jnp.concatenate(
        [ref[role].reshape(group, width) for role in range(2) for ref in (kept_ref, came_ref)], 0
    )

    def step(i, carry):
        at = pl.ds(pl.multiple_of(i * tile, tile), tile)
        units = jnp.maximum(jnp.dot(tokens, w_ref[:, at], preferred_element_type=jnp.float32), 0.0)
        units = units.astype(jnp.bfloat16)
        if old_ref is None:
            out_ref[:, :, at] = jnp.zeros((out_ref.shape[0], 2 * group, tile), jnp.bfloat16)
        else:
            out_ref[:, :, at] = old_ref[:, :, at]
        for role in range(2):
            slot = meta[pair, 1 + role]
            out_ref[slot, :, at] = out_ref[slot, :, at] + units[role * 2 * group : (role + 1) * 2 * group]
        return carry

    lax.fori_loop(0, w_ref.shape[1] // tile, step, 0)


def expand(pair, meta, kept, came, w_in, slots, old):
    _, half, rows, width = kept.shape
    units = w_in.shape[1]
    return kernel_call(
        functools.partial(expand_kernel, pair, min(512, units)),
        "expand",
        (meta, kept, came, w_in) + (() if old is None else (old,)),
        [bf16(slots, 2 * half * rows, units)],
        smem=(0,),
        limit=32,
        flops=2 * 4 * half * rows * width * units,
        moved=2 * width * units,
    )[0]


def shrink_kernel(begin, units_ref, w_ref, out_ref):
    slots, tall, depth = units_ref.shape
    step = out_ref.shape[-1]
    product = jnp.dot(
        units_ref[...].reshape(slots * tall, depth),
        w_ref[:, begin : begin + step],
        preferred_element_type=jnp.float32,
    )
    out_ref[...] = product.astype(jnp.bfloat16).reshape(out_ref.shape)


def shrink(begin, step, units, w_down, blocks):
    slots, tall, depth = units.shape
    return kernel_call(
        functools.partial(shrink_kernel, begin),
        "shrink",
        (units, w_down),
        [bf16(slots, blocks, tall // blocks, step)],
        limit=32,
        flops=2 * slots * tall * depth * step,
        moved=2 * depth * step,
    )[0]


def finish_kernel(pairs, columns, meta, *refs):
    hidden_refs, pieces = refs[:pairs], refs[pairs : pairs + 2 * columns]
    out_refs, acc_ref = refs[pairs + 2 * columns : -1], refs[-1]
    slots, rows, width = acc_ref.shape
    step = width // columns
    for c in range(columns):
        acc_ref[:, :, c * step : (c + 1) * step] = pieces[2 * c][:, 0].astype(jnp.float32) + pieces[2 * c + 1][
            :, 0
        ].astype(jnp.float32)
    lengths = [jnp.int32(0)] * slots
    for p in range(pairs):
        for role in range(2):
            slot = meta[p, 1 + role]
            acc_ref[slot] = acc_ref[slot] + hidden_refs[p][role]
            lengths = [jnp.where(slot == s, meta[p, 3 + role], old) for s, old in enumerate(lengths)]
    position = meta[0, 5] * rows + lax.broadcasted_iota(jnp.int32, (rows, width), 0)
    for s in range(slots):
        out_refs[s][...] = jnp.where(position < lengths[s], acc_ref[s], 0.0).astype(jnp.bfloat16)


def home_kernel(route_ref, *refs):
    blocks, out_ref, acc_ref = refs[:-2], refs[-2], refs[-1]
    me = lax.axis_index("pair")
    acc_ref[...] = jnp.zeros_like(acc_ref)
    for k, block in enumerate(blocks):
        doc = route_ref[me, me ^ k]

        @pl.when(doc >= 0)
        def add():
            acc_ref[doc] = acc_ref[doc] + block[...].astype(jnp.float32)

    out_ref[...] = acc_ref[...].astype(jnp.bfloat16)


def local(
    queries,
    documents,
    doc_len,
    route,
    pair_list,
    attn_gain,
    w_query,
    w_key,
    w_value,
    w_output,
    ffn_gain,
    w_in,
    w_down,
):
    owners = lax.axis_size("pair")
    slices = lax.axis_size("tensor")
    doc_count, doc_rows, width = documents.shape
    query_count, query_rows, _ = queries.shape
    assert query_count * query_rows == doc_rows
    pairs = pair_list.shape[0]
    slots = min(2 * pairs, owners)
    direct = slots == owners
    down_bits = [1 << i for i in range(slices.bit_length() - 1)]
    up_bits = down_bits[::-1]
    attn_gain, ffn_gain = attn_gain.reshape(1, width), ffn_gain.reshape(1, width)
    weights = (w_query, w_key, w_value)

    meta, early, *arrived = kernel_call(
        functools.partial(start_kernel, slots),
        "start",
        (route, doc_len, pair_list, documents, queries, attn_gain),
        [jax.ShapeDtypeStruct((pairs, 6), jnp.int32), bf16(1 + direct, 1, doc_rows, width)]
        + [bf16(doc_rows, width)] * owners,
        smem=(0, 1, 2),
        out_smem=(0,),
    )
    arrived = [block if k == 0 else swap(block, k, "pair") for k, block in enumerate(arrived)]
    if not direct:
        me = lax.axis_index("pair")
        taken = lax.dynamic_slice_in_dim(route, me, 1, 1)[:, 0] >= 0
        source = me ^ jnp.arange(owners, dtype=jnp.int32)
        other = jnp.arange(owners, dtype=jnp.int32)
        slot_of = jnp.sum(jnp.where((other[None, :] < source[:, None]) & taken[None, :], 1, 0), 1)
        is_taken = jnp.sum(jnp.where((other[None, :] == source[:, None]) & taken[None, :], 1, 0), 1)
        place = jnp.where(is_taken > 0, slot_of, -1)
        table = (other[:slots, None] == place[None, :]).astype(jnp.bfloat16)
        packed = jnp.einsum("sk,krd->srd", table, jnp.stack(arrived), preferred_element_type=jnp.float32)
        arrived = [packed[s].astype(jnp.bfloat16) for s in range(slots)]
    rows_own, late = kernel_call(
        functools.partial(late_kernel, slots),
        "late",
        (*arrived, attn_gain),
        [bf16(slots, doc_rows, width), bf16(slots - direct, 1, doc_rows, width)],
    )

    def spread(values):
        kept = gather_blocks(values, up_bits[:-1])
        return kept, swap(kept, up_bits[-1], "tensor")

    first = project("project_early", 1, *spread(early), weights, ())
    q, k, v = project("project_late", 0, *spread(late), weights, first if direct else first[1:])

    hidden, units = [], None
    for pair in range(pairs):
        part, meta = attend(pair, up_bits, query_rows, meta, q, k, v, w_output)
        for bit in down_bits:
            kept, came = halve(part, bit)
            if bit != down_bits[-1]:
                part = kept + came
        own, ffn = settle(pair, meta, kept, came, rows_own, ffn_gain)
        hidden.append(own)
        units = expand(pair, meta, *spread(ffn), w_in, slots, units)

    columns = 2
    step = width // columns
    pieces = []
    for c in range(columns):
        part = shrink(c * step, step, units, w_down, slices)
        for bit in down_bits:
            kept, came = halve(part, bit)
            if bit != down_bits[-1]:
                part = kept + came
        pieces += [kept, came]
    blocks = kernel_call(
        functools.partial(finish_kernel, pairs, columns),
        "finish",
        (meta, *hidden, *pieces),
        [bf16(doc_rows, width)] * slots,
        scratch=[pltpu.VMEM((slots, doc_rows, width), jnp.float32)],
        smem=(0,),
    )
    if not direct:
        packed = jnp.einsum("sk,srd->krd", table, jnp.stack(blocks), preferred_element_type=jnp.float32)
        blocks = [packed[s].astype(jnp.bfloat16) for s in range(owners)]
    blocks = [block if k == 0 else swap(block, k, "pair") for k, block in enumerate(blocks)]
    return kernel_call(
        home_kernel,
        "home",
        (route, *blocks),
        [bf16(doc_count, doc_rows, width)],
        scratch=[pltpu.VMEM((doc_count, doc_rows, width), jnp.float32)],
        smem=(0,),
    )[0]


def solution(mesh):
    placed = (
        P("pair", "tensor", None),
        P("pair", "tensor", None),
        P(),
        P(),
        P("pair", None),
        P(),
        P(None, "tensor"),
        P(None, "tensor"),
        P(None, "tensor"),
        P("tensor", None),
        P(),
        P(None, "tensor"),
        P("tensor", None),
    )
    return jax.shard_map(
        local, mesh=mesh, in_specs=placed, out_specs=P("pair", "tensor", None), check_vma=False
    )
```

time: 268 us -> 127 us (0.47)
  waiting for transfers between devices: 156 us -> 38.1 us
  matrix products: 53.4 us -> 0 us
  starting transfers between devices: 5.25 us -> 42.7 us
  Pallas kernels: 0 us -> 37.3 us
  other arithmetic: 26.5 us -> 0.47 us
  between operations: 13.3 us -> 0.56 us
  blocking collectives: 8.42 us -> 0 us
  local copies, waits for them, and re-layouts: 4.11 us -> 8.06 us
    psum x2 -> x0, waiting for transfers between devices: 127 us -> none  [the longest x1 63.6 us: local(): lax.psum(jnp.einsum('pre,ed->prd', context, w_output, preferred_element_t...]
    dot_general x14 -> x0, matrix products: 53.4 us -> none  [the longest x1 24.9 us: local(): jnp.einsum('prf,fd->prd', units, w_down, preferred_element_type=jnp.float32)]
    ppermute x0 -> x36, starting transfers between devices: none -> 42.7 us  [swap(): return lax.ppermute(values, axis, [(i, i ^ bit) for i in range(count)])]
    ppermute x0 -> x36, waiting for transfers between devices: none -> 38.1 us  [swap(): return lax.ppermute(values, axis, [(i, i ^ bit) for i in range(count)])]
    pallas_call x0 -> x17, Pallas kernels: none -> 37.3 us  [kernel_call(): pl.pallas_call(kernel, out_shape=out_shape, in_specs=[space(i in smem) fo...]
    all_gather x1 -> x0, waiting for transfers between devices: 25.9 us -> none  [local(): tokens_all = lax.all_gather(own_tokens, 'tensor', axis=1, tiled=True)]
    sub x2 -> x0, other arithmetic: 17 us -> none  [the longest x1 17 us: local(): expo = jnp.exp(scores - top)]
    all_to_all x1 -> x0, blocking collectives: 8.42 us -> none  [local(): lax.all_to_all(back.astype(jnp.bfloat16), 'pair', split_axis=0, concat_ax...]
  transfers between devices with their start and end apart: 4 -> 36, of which waited for: 4 -> 21; matrix products, arithmetic and copies ran while one was open for 2% -> 1% of each run, Pallas kernels for 0% -> 17%
where the time goes in v2:
time: 127 us
  starting transfers between devices  42.7 us (34%)
  waiting for transfers between devices  38.1 us (30%)
  Pallas kernels  37.3 us (29%)
  local copies, waits for them, and re-layouts  8.06 us (6%)
    ppermute x36, starting transfers between devices, swap(): return lax.ppermute(values, axis, [(i, i ^ bit) for i in range(count)])  42.7 us
    ppermute x36, waiting for transfers between devices, swap(): return lax.ppermute(values, axis, [(i, i ^ bit) for i in range(count)])  38.1 us
    pallas_call x17, Pallas kernels, kernel_call(): pl.pallas_call(kernel, out_shape=out_shape, in_specs=[space(i in smem) fo...  37.3 us
    unnamed x42, local copies, waits for them, and re-layouts  7.81 us
  transfers between devices with their start and end apart: 36, of which 21 were waited for; matrix products, arithmetic and copies ran while one was open for 1% of the time, Pallas kernels for 17%

profile of v2, /device:TPU:0, one launch (start us, length us, event | category | flops | bytes accessed | tf_op | source)
XLA Modules:
  0.0 127.2 jit_solution(4979740997638082215)
XLA Ops:
  5.8 3.0 %collective-permute-start = (bf16[16,1024]{1,0:T(8,128)(2,1)S(1)}, bf16[16,1024]{1,0:T(8,128)(2,1)S(1)}, u32[]{:S(2)}, u32[]{:S(2)}) collective-permute-start(bf16[16,1024]{1,0:T(8,128)(2,1)S(1)} %get-tuple-element.37), channel_id=1, source_target_pairs={{0,8},{8,0},{16,24},{24,16},{1,9},{9,1},{17,25},{25,17},{2,10},{10... | collective-permute-start | bytes 98312 | tf_op jit(solution)/shard_map/ppermute | solution.py:22
  10.3 3.0 %collective-permute-start.6 = (bf16[2,1,16,1024]{3,2,1,0:T(8,128)(2,1)S(1)}, bf16[2,1,16,1024]{3,2,1,0:T(8,128)(2,1)S(1)}, u32[]{:S(2)}, u32[]{:S(2)}) collective-permute-start(bf16[2,1,16,1024]{3,2,1,0:T(8,128)(2,1)S(1)} %get-tuple-element.41), channel_id=1, source_target_pairs={{0,4},{1,5},{2,6},{3,7},{4,0},{5,1},{6,2},{7,3},{8,12},{9,13},{10,... | collective-permute-start | bytes 196616 | tf_op jit(solution)/shard_map/ppermute | solution.py:22
  15.3 2.7 %collective-permute-start.3 = (bf16[3,1,16,1024]{3,2,1,0:T(8,128)(2,1)S(1)}, bf16[3,1,16,1024]{3,2,1,0:T(8,128)(2,1)S(1)}, u32[]{:S(2)}, u32[]{:S(2)}) collective-permute-start(bf16[3,1,16,1024]{3,2,1,0:T(8,128)(2,1)S(1)} %get-tuple-element.40), channel_id=1, source_target_pairs={{0,4},{1,5},{2,6},{3,7},{4,0},{5,1},{6,2},{7,3},{8,12},{9,13},{10,... | collective-permute-start | bytes 294920 | tf_op jit(solution)/shard_map/ppermute | solution.py:22
  22.7 4.0 %collective-permute-done.4 = bf16[3,2,16,1024]{3,2,1,0:T(8,128)(2,1)S(1)} collective-permute-done((bf16[3,2,16,1024]{3,2,1,0:T(8,128)(2,1)S(1)}, bf16[3,2,16,1024]{3,2,1,0:T(8,128)(2,1)S(1)}, u32[]{:S(2)}, u32[]{:S(2)}) %collective-permute-start.4) | collective-permute-done | bytes 196640 | tf_op jit(solution)/shard_map/ppermute | solution.py:22
  33.6 2.6 %project_late.1 = (bf16[4,8,16,1024]{3,2,1,0:T(8,128)(2,1)S(1)}, bf16[5,8,16,1024]{3,2,1,0:T(8,128)(2,1)S(1)}, bf16[5,8,16,1024]{3,2,1,0:T(8,128)(2,1)S(1)}) custom-call(bf16[3,4,16,1024]{3,2,1,0:T(8,128)(2,1)S(1)} %constant_dynamic-update-slice_fusion.kept_ref, bf16[3,4,16,1024]{3,2,1,0:T(8,128)(2,1)S(1)} %collective-permute-done.5.came_ref, ...), custom_call_target="tpu_custom_call" | custom-call | flops 2415919104 | bytes 6291456 | tf_op jit(solution)/shard_map/project_late/pallas_call | solution.py:38
  36.2 3.4 %attend.3 = (bf16[2,8,16,1024]{3,2,1,0:T(8,128)(2,1)S(1)}, s32[3,6]{1,0:T(4,128)S(1)}) custom-call(s32[3,6]{1,0:T(4,128)S(1)} %get-tuple-element.35.meta, bf16[4,8,16,1024]{3,2,1,0:T(8,128)(2,1)S(1)} %get-tuple-element.45.q_ref, bf16[5,8,16,1024]{3,2,1,0:T(8,128)(2,1)S(1)} %get-tuple-element.46.k_ref, bf16[5,8,16,1024]{3,2,1,0:T(8,128)(2,1)S(1)} %get-tuple-element.47.v_ref, ...), custom_call_target="tpu_custom_call" | custom-call | flops 939524096 | bytes 2097152 | tf_op jit(solution)/shard_map/attend/pallas_call | solution.py:38
  39.9 3.4 %attend.4 = (bf16[2,8,16,1024]{3,2,1,0:T(8,128)(2,1)S(1)}, s32[3,6]{1,0:T(4,128)S(1)}) custom-call(s32[3,6]{1,0:T(4,128)S(1)} %get-tuple-element.48.meta, bf16[4,8,16,1024]{3,2,1,0:T(8,128)(2,1)S(1)} %get-tuple-element.45.q_ref, bf16[5,8,16,1024]{3,2,1,0:T(8,128)(2,1)S(1)} %get-tuple-element.46.k_ref, bf16[5,8,16,1024]{3,2,1,0:T(8,128)(2,1)S(1)} %get-tuple-element.47.v_ref, ...), custom_call_target="tpu_custom_call" | custom-call | flops 939524096 | bytes 2097152 | tf_op jit(solution)/shard_map/attend/pallas_call | solution.py:38
  43.8 3.4 %attend.5 = (bf16[2,8,16,1024]{3,2,1,0:T(8,128)(2,1)S(1)}, s32[3,6]{1,0:T(4,128)S(1)}) custom-call(s32[3,6]{1,0:T(4,128)S(1)} %get-tuple-element.49.meta, bf16[4,8,16,1024]{3,2,1,0:T(8,128)(2,1)S(1)} %get-tuple-element.45.q_ref, bf16[5,8,16,1024]{3,2,1,0:T(8,128)(2,1)S(1)} %get-tuple-element.46.k_ref, bf16[5,8,16,1024]{3,2,1,0:T(8,128)(2,1)S(1)} %get-tuple-element.47.v_ref, ...), custom_call_target="tpu_custom_call" | custom-call | flops 939524096 | bytes 2097152 | tf_op jit(solution)/shard_map/attend/pallas_call | solution.py:38
  51.5 2.4 %collective-permute-done.10 = bf16[2,2,16,1024]{3,2,1,0:T(8,128)(2,1)S(1)} collective-permute-done((bf16[2,2,16,1024]{3,2,1,0:T(8,128)(2,1)S(1)}, bf16[2,2,16,1024]{3,2,1,0:T(8,128)(2,1)S(1)}, u32[]{:S(2)}, u32[]{:S(2)}) %collective-permute-start.10) | collective-permute-done | bytes 131104 | tf_op jit(solution)/shard_map/ppermute | solution.py:22
  53.9 3.3 %collective-permute-start.11 = (bf16[2,1,16,1024]{3,2,1,0:T(8,128)(2,1)S(1)}, bf16[2,1,16,1024]{3,2,1,0:T(8,128)(2,1)S(1)}, u32[]{:S(2)}, u32[]{:S(2)}) collective-permute-start(bf16[2,1,16,1024]{3,2,1,0:T(8,128)(2,1)S(1)} %get-tuple-element.73), channel_id=1, source_target_pairs={{0,4},{1,5},{2,6},{3,7},{4,0},{5,1},{6,2},{7,3},{8,12},{9,13},{10,... | collective-permute-start | bytes 196616 | tf_op jit(solution)/shard_map/ppermute | solution.py:22
  57.3 2.8 %collective-permute-start.14 = (bf16[2,1,16,1024]{3,2,1,0:T(8,128)(2,1)S(1)}, bf16[2,1,16,1024]{3,2,1,0:T(8,128)(2,1)S(1)}, u32[]{:S(2)}, u32[]{:S(2)}) collective-permute-start(bf16[2,1,16,1024]{3,2,1,0:T(8,128)(2,1)S(1)} %get-tuple-element.71), channel_id=1, source_target_pairs={{0,4},{1,5},{2,6},{3,7},{4,0},{5,1},{6,2},{7,3},{8,12},{9,13},{10,... | collective-permute-start | bytes 196616 | tf_op jit(solution)/shard_map/ppermute | solution.py:22
  67.3 3.2 %collective-permute-done.17.came_ref = bf16[2,1,16,1024]{3,2,1,0:T(8,128)(2,1)S(1)} collective-permute-done((bf16[2,1,16,1024]{3,2,1,0:T(8,128)(2,1)S(1)}, bf16[2,1,16,1024]{3,2,1,0:T(8,128)(2,1)S(1)}, u32[]{:S(2)}, u32[]{:S(2)}) %collective-permute-start.17) | collective-permute-done | bytes 65568 | tf_op jit(solution)/shard_map/ppermute | solution.py:22
  71.9 3.8 %collective-permute-start.25 = (bf16[2,2,16,1024]{3,2,1,0:T(8,128)(2,1)S(1)}, bf16[2,2,16,1024]{3,2,1,0:T(8,128)(2,1)S(1)}, u32[]{:S(2)}, u32[]{:S(2)}) collective-permute-start(bf16[2,2,16,1024]{3,2,1,0:T(8,128)(2,1)S(1)} %pad_maximum_fusion.4), channel_id=1, source_target_pairs={{0,2},{1,3},{2,0},{3,1},{4,6},{5,7},{6,4},{7,5},{8,10},{9,11},{10,... | collective-permute-start | bytes 393224 | tf_op jit(solution)/shard_map/ppermute | solution.py:22
  76.7 2.1 %collective-permute-start.19 = (bf16[2,2,16,1024]{3,2,1,0:T(8,128)(2,1)S(1)}, bf16[2,2,16,1024]{3,2,1,0:T(8,128)(2,1)S(1)}, u32[]{:S(2)}, u32[]{:S(2)}) collective-permute-start(bf16[2,2,16,1024]{3,2,1,0:T(8,128)(2,1)S(1)} %pad_maximum_fusion.2), channel_id=1, source_target_pairs={{0,2},{1,3},{2,0},{3,1},{4,6},{5,7},{6,4},{7,5},{8,10},{9,11},{10,... | collective-permute-start | bytes 393224 | tf_op jit(solution)/shard_map/ppermute | solution.py:22
  80.2 2.5 %collective-permute-done.22 = bf16[2,2,16,1024]{3,2,1,0:T(8,128)(2,1)S(1)} collective-permute-done((bf16[2,2,16,1024]{3,2,1,0:T(8,128)(2,1)S(1)}, bf16[2,2,16,1024]{3,2,1,0:T(8,128)(2,1)S(1)}, u32[]{:S(2)}, u32[]{:S(2)}) %collective-permute-start.22) | collective-permute-done | bytes 131104 | tf_op jit(solution)/shard_map/ppermute | solution.py:22
  84.2 4.3 %expand.3.rest_0_ = bf16[4,128,4096]{2,1,0:T(8,128)(2,1)S(1)} custom-call(s32[3,6]{1,0:T(4,128)S(1)} %get-tuple-element.48.meta, bf16[2,4,16,1024]{3,2,1,0:T(8,128)(2,1)S(1)} %constant_dynamic-update-slice_fusion.12.kept_ref, bf16[2,4,16,1024]{3,2,1,0:T(8,128)(2,1)S(1)} %collective-permute-done.26.came_ref, bf16[1024,4096]{1,0:T(8,128)(2,1)S(1)} %bitcast.3), custom_call_target="tpu_custom_call" | custom-call | flops 2147483648 | bytes 8388608 | tf_op jit(solution)/shard_map/expand/pallas_call | solution.py:38
  88.5 4.3 %expand.4.rest_0_ = bf16[4,128,4096]{2,1,0:T(8,128)(2,1)S(1)} custom-call(s32[3,6]{1,0:T(4,128)S(1)} %get-tuple-element.49.meta, bf16[2,4,16,1024]{3,2,1,0:T(8,128)(2,1)S(1)} %constant_dynamic-update-slice_fusion.9.kept_ref, bf16[2,4,16,1024]{3,2,1,0:T(8,128)(2,1)S(1)} %collective-permute-done.23.came_ref, bf16[1024,4096]{1,0:T(8,128)(2,1)S(1)} %bitcast.3, ...), custom_call_target="tpu_custom_call" | custom-call | flops 2147483648 | bytes 8388608 | tf_op jit(solution)/shard_map/expand/pallas_call | solution.py:38
  92.8 4.3 %expand.5.units_ref = bf16[4,128,4096]{2,1,0:T(8,128)(2,1)S(1)} custom-call(s32[3,6]{1,0:T(4,128)S(1)} %get-tuple-element.50.meta, bf16[2,4,16,1024]{3,2,1,0:T(8,128)(2,1)S(1)} %constant_dynamic-update-slice_fusion.6.kept_ref, bf16[2,4,16,1024]{3,2,1,0:T(8,128)(2,1)S(1)} %collective-permute-done.20.came_ref, bf16[1024,4096]{1,0:T(8,128)(2,1)S(1)} %bitcast.3, ...), custom_call_target="tpu_custom_call" | custom-call | flops 2147483648 | bytes 8388608 | tf_op jit(solution)/shard_map/expand/pallas_call | solution.py:38
  97.1 2.3 %shrink.3 = bf16[4,8,16,512]{3,2,1,0:T(8,128)(2,1)S(1)} custom-call(bf16[4,128,4096]{2,1,0:T(8,128)(2,1)S(1)} %expand.5.units_ref, bf16[4096,1024]{1,0:T(8,128)(2,1)S(1)} %bitcast.5), custom_call_target="tpu_custom_call" | custom-call | flops 2147483648 | bytes 4194304 | tf_op jit(solution)/shard_map/shrink/pallas_call | solution.py:38
  100.0 2.3 %shrink.2 = bf16[4,8,16,512]{3,2,1,0:T(8,128)(2,1)S(1)} custom-call(bf16[4,128,4096]{2,1,0:T(8,128)(2,1)S(1)} %expand.5.units_ref, bf16[4096,1024]{1,0:T(8,128)(2,1)S(1)} %bitcast.5), custom_call_target="tpu_custom_call" | custom-call | flops 2147483648 | bytes 4194304 | tf_op jit(solution)/shard_map/shrink/pallas_call | solution.py:38
  104.8 4.2 %collective-permute-done.31 = bf16[4,2,16,512]{3,2,1,0:T(8,128)(2,1)S(1)} collective-permute-done((bf16[4,2,16,512]{3,2,1,0:T(8,128)(2,1)S(1)}, bf16[4,2,16,512]{3,2,1,0:T(8,128)(2,1)S(1)}, u32[]{:S(2)}, u32[]{:S(2)}) %collective-permute-start.31) | collective-permute-done | bytes 131104 | tf_op jit(solution)/shard_map/ppermute | solution.py:22
  114.6 2.8 %collective-permute-done.29.refs_4_ = bf16[4,1,16,512]{3,2,1,0:T(8,128)(2,1)S(1)} collective-permute-done((bf16[4,1,16,512]{3,2,1,0:T(8,128)(2,1)S(1)}, bf16[4,1,16,512]{3,2,1,0:T(8,128)(2,1)S(1)}, u32[]{:S(2)}, u32[]{:S(2)}) %collective-permute-start.29) | collective-permute-done | bytes 65568 | tf_op jit(solution)/shard_map/ppermute | solution.py:22
  119.0 2.0 %collective-permute-start.34 = (bf16[16,1024]{1,0:T(8,128)(2,1)S(1)}, bf16[16,1024]{1,0:T(8,128)(2,1)S(1)}, u32[]{:S(2)}, u32[]{:S(2)}) collective-permute-start(bf16[16,1024]{1,0:T(8,128)(2,1)S(1)} %get-tuple-element.63), channel_id=1, source_target_pairs={{0,16},{8,24},{16,0},{24,8},{1,17},{9,25},{17,1},{25,9},{2,18},{10... | collective-permute-start | bytes 98312 | tf_op jit(solution)/shard_map/ppermute | solution.py:22
  123.0 2.9 %collective-permute-done.35.refs_3_ = bf16[16,1024]{1,0:T(8,128)(2,1)S(1)} collective-permute-done((bf16[16,1024]{1,0:T(8,128)(2,1)S(1)}, bf16[16,1024]{1,0:T(8,128)(2,1)S(1)}, u32[]{:S(2)}, u32[]{:S(2)}) %collective-permute-start.35) | collective-permute-done | bytes 32800 | tf_op jit(solution)/shard_map/ppermute | solution.py:22
  (144 shorter events, 51.8 us)
Async XLA Ops:
  5.8 7.6 %collective-permute-start = (bf16[16,1024]{1,0:T(8,128)(2,1)S(1)}, bf16[16,1024]{1,0:T(8,128)(2,1)S(1)}, u32[]{:S(2)}, u32[]{:S(2)}) collective-permute-start(bf16[16,1024]{1,0:T(8,128)(2,1)S(1)} %get-tuple-element.37), channel_id=1, source_target_pairs={{0,8},{8,0},{16,24},{24,16},{1,9},{9,1},{17,25},{25,17},{2,10},{10... | collective-permute-start | bytes 98312 | tf_op jit(solution)/shard_map/ppermute | solution.py:22
  10.3 7.6 %collective-permute-start.6 = (bf16[2,1,16,1024]{3,2,1,0:T(8,128)(2,1)S(1)}, bf16[2,1,16,1024]{3,2,1,0:T(8,128)(2,1)S(1)}, u32[]{:S(2)}, u32[]{:S(2)}) collective-permute-start(bf16[2,1,16,1024]{3,2,1,0:T(8,128)(2,1)S(1)} %get-tuple-element.41), channel_id=1, source_target_pairs={{0,4},{1,5},{2,6},{3,7},{4,0},{5,1},{6,2},{7,3},{8,12},{9,13},{10,... | collective-permute-start | bytes 196616 | tf_op jit(solution)/shard_map/ppermute | solution.py:22
  15.3 5.7 %collective-permute-start.3 = (bf16[3,1,16,1024]{3,2,1,0:T(8,128)(2,1)S(1)}, bf16[3,1,16,1024]{3,2,1,0:T(8,128)(2,1)S(1)}, u32[]{:S(2)}, u32[]{:S(2)}) collective-permute-start(bf16[3,1,16,1024]{3,2,1,0:T(8,128)(2,1)S(1)} %get-tuple-element.40), channel_id=1, source_target_pairs={{0,4},{1,5},{2,6},{3,7},{4,0},{5,1},{6,2},{7,3},{8,12},{9,13},{10,... | collective-permute-start | bytes 294920 | tf_op jit(solution)/shard_map/ppermute | solution.py:22
  17.9 8.8 %collective-permute-start.7 = (bf16[2,2,16,1024]{3,2,1,0:T(8,128)(2,1)S(1)}, bf16[2,2,16,1024]{3,2,1,0:T(8,128)(2,1)S(1)}, u32[]{:S(2)}, u32[]{:S(2)}) collective-permute-start(bf16[2,2,16,1024]{3,2,1,0:T(8,128)(2,1)S(1)} %pad_maximum_fusion.1), channel_id=1, source_target_pairs={{0,2},{1,3},{2,0},{3,1},{4,6},{5,7},{6,4},{7,5},{8,10},{9,11},{10,... | collective-permute-start | bytes 393224 | tf_op jit(solution)/shard_map/ppermute | solution.py:22
  20.9 5.7 %collective-permute-start.4 = (bf16[3,2,16,1024]{3,2,1,0:T(8,128)(2,1)S(1)}, bf16[3,2,16,1024]{3,2,1,0:T(8,128)(2,1)S(1)}, u32[]{:S(2)}, u32[]{:S(2)}) collective-permute-start(bf16[3,2,16,1024]{3,2,1,0:T(8,128)(2,1)S(1)} %pad_maximum_fusion), channel_id=1, source_target_pairs={{0,2},{1,3},{2,0},{3,1},{4,6},{5,7},{6,4},{7,5},{8,10},{9,11},{10,... | collective-permute-start | bytes 589832 | tf_op jit(solution)/shard_map/ppermute | solution.py:22
  26.7 6.9 %collective-permute-start.5 = (bf16[3,4,16,1024]{3,2,1,0:T(8,128)(2,1)S(1)}, bf16[3,4,16,1024]{3,2,1,0:T(8,128)(2,1)S(1)}, u32[]{:S(2)}, u32[]{:S(2)}) collective-permute-start(bf16[3,4,16,1024]{3,2,1,0:T(8,128)(2,1)S(1)} %constant_dynamic-update-slice_fusion.kept_ref), channel_id=1, source_target_pairs={{0,1},{1,0},{2,3},{3,2},{4,5},{5,4},{6,7},{7,6},{8,9},{9,8},{10,11... | collective-permute-start | bytes 1179656 | tf_op jit(solution)/shard_map/ppermute | solution.py:22
  39.7 7.8 %collective-permute-start.9 = (bf16[2,4,16,1024]{3,2,1,0:T(8,128)(2,1)S(1)}, bf16[2,4,16,1024]{3,2,1,0:T(8,128)(2,1)S(1)}, u32[]{:S(2)}, u32[]{:S(2)}) collective-permute-start(bf16[2,4,16,1024]{3,2,1,0:T(8,128)(2,1)S(1)} %slice.91), channel_id=1, source_target_pairs={{0,1},{1,0},{2,3},{3,2},{4,5},{5,4},{6,7},{7,6},{8,9},{9,8},{10,11... | collective-permute-start | bytes 786440 | tf_op jit(solution)/shard_map/ppermute | solution.py:22
  43.4 5.9 %collective-permute-start.12 = (bf16[2,4,16,1024]{3,2,1,0:T(8,128)(2,1)S(1)}, bf16[2,4,16,1024]{3,2,1,0:T(8,128)(2,1)S(1)}, u32[]{:S(2)}, u32[]{:S(2)}) collective-permute-start(bf16[2,4,16,1024]{3,2,1,0:T(8,128)(2,1)S(1)} %slice.97), channel_id=1, source_target_pairs={{0,1},{1,0},{2,3},{3,2},{4,5},{5,4},{6,7},{7,6},{8,9},{9,8},{10,11... | collective-permute-start | bytes 786440 | tf_op jit(solution)/shard_map/ppermute | solution.py:22
  47.5 6.4 %collective-permute-start.10 = (bf16[2,2,16,1024]{3,2,1,0:T(8,128)(2,1)S(1)}, bf16[2,2,16,1024]{3,2,1,0:T(8,128)(2,1)S(1)}, u32[]{:S(2)}, u32[]{:S(2)}) collective-permute-start(bf16[2,2,16,1024]{3,2,1,0:T(8,128)(2,1)S(1)} %slice.121), channel_id=1, source_target_pairs={{0,2},{1,3},{2,0},{3,1},{4,6},{5,7},{6,4},{7,5},{8,10},{9,11},{10,... | collective-permute-start | bytes 393224 | tf_op jit(solution)/shard_map/ppermute | solution.py:22
  49.3 7.9 %collective-permute-start.13 = (bf16[2,2,16,1024]{3,2,1,0:T(8,128)(2,1)S(1)}, bf16[2,2,16,1024]{3,2,1,0:T(8,128)(2,1)S(1)}, u32[]{:S(2)}, u32[]{:S(2)}) collective-permute-start(bf16[2,2,16,1024]{3,2,1,0:T(8,128)(2,1)S(1)} %slice.125), channel_id=1, source_target_pairs={{0,2},{1,3},{2,0},{3,1},{4,6},{5,7},{6,4},{7,5},{8,10},{9,11},{10,... | collective-permute-start | bytes 393224 | tf_op jit(solution)/shard_map/ppermute | solution.py:22
  49.8 11.4 %collective-permute-start.16 = (bf16[2,2,16,1024]{3,2,1,0:T(8,128)(2,1)S(1)}, bf16[2,2,16,1024]{3,2,1,0:T(8,128)(2,1)S(1)}, u32[]{:S(2)}, u32[]{:S(2)}) collective-permute-start(bf16[2,2,16,1024]{3,2,1,0:T(8,128)(2,1)S(1)} %slice.129), channel_id=1, source_target_pairs={{0,2},{1,3},{2,0},{3,1},{4,6},{5,7},{6,4},{7,5},{8,10},{9,11},{10,... | collective-permute-start | bytes 393224 | tf_op jit(solution)/shard_map/ppermute | solution.py:22
  53.9 8.9 %collective-permute-start.11 = (bf16[2,1,16,1024]{3,2,1,0:T(8,128)(2,1)S(1)}, bf16[2,1,16,1024]{3,2,1,0:T(8,128)(2,1)S(1)}, u32[]{:S(2)}, u32[]{:S(2)}) collective-permute-start(bf16[2,1,16,1024]{3,2,1,0:T(8,128)(2,1)S(1)} %get-tuple-element.73), channel_id=1, source_target_pairs={{0,4},{1,5},{2,6},{3,7},{4,0},{5,1},{6,2},{7,3},{8,12},{9,13},{10,... | collective-permute-start | bytes 196616 | tf_op jit(solution)/shard_map/ppermute | solution.py:22
  57.3 9.0 %collective-permute-start.14 = (bf16[2,1,16,1024]{3,2,1,0:T(8,128)(2,1)S(1)}, bf16[2,1,16,1024]{3,2,1,0:T(8,128)(2,1)S(1)}, u32[]{:S(2)}, u32[]{:S(2)}) collective-permute-start(bf16[2,1,16,1024]{3,2,1,0:T(8,128)(2,1)S(1)} %get-tuple-element.71), channel_id=1, source_target_pairs={{0,4},{1,5},{2,6},{3,7},{4,0},{5,1},{6,2},{7,3},{8,12},{9,13},{10,... | collective-permute-start | bytes 196616 | tf_op jit(solution)/shard_map/ppermute | solution.py:22
  61.2 9.3 %collective-permute-start.17 = (bf16[2,1,16,1024]{3,2,1,0:T(8,128)(2,1)S(1)}, bf16[2,1,16,1024]{3,2,1,0:T(8,128)(2,1)S(1)}, u32[]{:S(2)}, u32[]{:S(2)}) collective-permute-start(bf16[2,1,16,1024]{3,2,1,0:T(8,128)(2,1)S(1)} %get-tuple-element.69), channel_id=1, source_target_pairs={{0,4},{1,5},{2,6},{3,7},{4,0},{5,1},{6,2},{7,3},{8,12},{9,13},{10,... | collective-permute-start | bytes 196616 | tf_op jit(solution)/shard_map/ppermute | solution.py:22
  63.5 8.4 %collective-permute-start.24 = (bf16[2,1,16,1024]{3,2,1,0:T(8,128)(2,1)S(1)}, bf16[2,1,16,1024]{3,2,1,0:T(8,128)(2,1)S(1)}, u32[]{:S(2)}, u32[]{:S(2)}) collective-permute-start(bf16[2,1,16,1024]{3,2,1,0:T(8,128)(2,1)S(1)} %get-tuple-element.60), channel_id=1, source_target_pairs={{0,4},{1,5},{2,6},{3,7},{4,0},{5,1},{6,2},{7,3},{8,12},{9,13},{10,... | collective-permute-start | bytes 196616 | tf_op jit(solution)/shard_map/ppermute | solution.py:22
  67.0 8.7 %collective-permute-start.21 = (bf16[2,1,16,1024]{3,2,1,0:T(8,128)(2,1)S(1)}, bf16[2,1,16,1024]{3,2,1,0:T(8,128)(2,1)S(1)}, u32[]{:S(2)}, u32[]{:S(2)}) collective-permute-start(bf16[2,1,16,1024]{3,2,1,0:T(8,128)(2,1)S(1)} %get-tuple-element.59), channel_id=1, source_target_pairs={{0,4},{1,5},{2,6},{3,7},{4,0},{5,1},{6,2},{7,3},{8,12},{9,13},{10,... | collective-permute-start | bytes 196616 | tf_op jit(solution)/shard_map/ppermute | solution.py:22
  71.9 8.2 %collective-permute-start.25 = (bf16[2,2,16,1024]{3,2,1,0:T(8,128)(2,1)S(1)}, bf16[2,2,16,1024]{3,2,1,0:T(8,128)(2,1)S(1)}, u32[]{:S(2)}, u32[]{:S(2)}) collective-permute-start(bf16[2,2,16,1024]{3,2,1,0:T(8,128)(2,1)S(1)} %pad_maximum_fusion.4), channel_id=1, source_target_pairs={{0,2},{1,3},{2,0},{3,1},{4,6},{5,7},{6,4},{7,5},{8,10},{9,11},{10,... | collective-permute-start | bytes 393224 | tf_op jit(solution)/shard_map/ppermute | solution.py:22
  75.7 7.0 %collective-permute-start.22 = (bf16[2,2,16,1024]{3,2,1,0:T(8,128)(2,1)S(1)}, bf16[2,2,16,1024]{3,2,1,0:T(8,128)(2,1)S(1)}, u32[]{:S(2)}, u32[]{:S(2)}) collective-permute-start(bf16[2,2,16,1024]{3,2,1,0:T(8,128)(2,1)S(1)} %pad_maximum_fusion.3), channel_id=1, source_target_pairs={{0,2},{1,3},{2,0},{3,1},{4,6},{5,7},{6,4},{7,5},{8,10},{9,11},{10,... | collective-permute-start | bytes 393224 | tf_op jit(solution)/shard_map/ppermute | solution.py:22
  76.7 7.4 %collective-permute-start.19 = (bf16[2,2,16,1024]{3,2,1,0:T(8,128)(2,1)S(1)}, bf16[2,2,16,1024]{3,2,1,0:T(8,128)(2,1)S(1)}, u32[]{:S(2)}, u32[]{:S(2)}) collective-permute-start(bf16[2,2,16,1024]{3,2,1,0:T(8,128)(2,1)S(1)} %pad_maximum_fusion.2), channel_id=1, source_target_pairs={{0,2},{1,3},{2,0},{3,1},{4,6},{5,7},{6,4},{7,5},{8,10},{9,11},{10,... | collective-permute-start | bytes 393224 | tf_op jit(solution)/shard_map/ppermute | solution.py:22
  82.7 5.8 %collective-permute-start.23 = (bf16[2,4,16,1024]{3,2,1,0:T(8,128)(2,1)S(1)}, bf16[2,4,16,1024]{3,2,1,0:T(8,128)(2,1)S(1)}, u32[]{:S(2)}, u32[]{:S(2)}) collective-permute-start(bf16[2,4,16,1024]{3,2,1,0:T(8,128)(2,1)S(1)} %constant_dynamic-update-slice_fusion.9.kept_ref), channel_id=1, source_target_pairs={{0,1},{1,0},{2,3},{3,2},{4,5},{5,4},{6,7},{7,6},{8,9},{9,8},{10,11... | collective-permute-start | bytes 786440 | tf_op jit(solution)/shard_map/ppermute | solution.py:22
  84.1 8.7 %collective-permute-start.20 = (bf16[2,4,16,1024]{3,2,1,0:T(8,128)(2,1)S(1)}, bf16[2,4,16,1024]{3,2,1,0:T(8,128)(2,1)S(1)}, u32[]{:S(2)}, u32[]{:S(2)}) collective-permute-start(bf16[2,4,16,1024]{3,2,1,0:T(8,128)(2,1)S(1)} %constant_dynamic-update-slice_fusion.6.kept_ref), channel_id=1, source_target_pairs={{0,1},{1,0},{2,3},{3,2},{4,5},{5,4},{6,7},{7,6},{8,9},{9,8},{10,11... | collective-permute-start | bytes 786440 | tf_op jit(solution)/shard_map/ppermute | solution.py:22
  102.6 6.4 %collective-permute-start.31 = (bf16[4,2,16,512]{3,2,1,0:T(8,128)(2,1)S(1)}, bf16[4,2,16,512]{3,2,1,0:T(8,128)(2,1)S(1)}, u32[]{:S(2)}, u32[]{:S(2)}) collective-permute-start(bf16[4,2,16,512]{3,2,1,0:T(8,128)(2,1)S(1)} %slice.141), channel_id=1, source_target_pairs={{0,2},{1,3},{2,0},{3,1},{4,6},{5,7},{6,4},{7,5},{8,10},{9,11},{10,... | collective-permute-start | bytes 393224 | tf_op jit(solution)/shard_map/ppermute | solution.py:22
  104.1 7.3 %collective-permute-start.28 = (bf16[4,2,16,512]{3,2,1,0:T(8,128)(2,1)S(1)}, bf16[4,2,16,512]{3,2,1,0:T(8,128)(2,1)S(1)}, u32[]{:S(2)}, u32[]{:S(2)}) collective-permute-start(bf16[4,2,16,512]{3,2,1,0:T(8,128)(2,1)S(1)} %slice.135), channel_id=1, source_target_pairs={{0,2},{1,3},{2,0},{3,1},{4,6},{5,7},{6,4},{7,5},{8,10},{9,11},{10,... | collective-permute-start | bytes 393224 | tf_op jit(solution)/shard_map/ppermute | solution.py:22
  111.4 6.1 %collective-permute-start.29 = (bf16[4,1,16,512]{3,2,1,0:T(8,128)(2,1)S(1)}, bf16[4,1,16,512]{3,2,1,0:T(8,128)(2,1)S(1)}, u32[]{:S(2)}, u32[]{:S(2)}) collective-permute-start(bf16[4,1,16,512]{3,2,1,0:T(8,128)(2,1)S(1)} %get-tuple-element.67), channel_id=1, source_target_pairs={{0,4},{1,5},{2,6},{3,7},{4,0},{5,1},{6,2},{7,3},{8,12},{9,13},{10,... | collective-permute-start | bytes 196616 | tf_op jit(solution)/shard_map/ppermute | solution.py:22
  (28 other events, 215.4 us)

commit v3 on v2

v3 whole, which is shorter than its diff:
```python
import functools
import math

import jax
import jax.numpy as jnp
from jax import lax
from jax.experimental import pallas as pl
from jax.experimental.pallas import tpu as pltpu
from jax.sharding import PartitionSpec as P

HEAD = 128
MIB = 1024 * 1024


def rms_norm(values, gain):
    spread = jnp.mean(values * values, -1, keepdims=True)
    return values * lax.rsqrt(spread + 1e-06) * gain


def swap(values, bit, axis):
    count = lax.axis_size(axis)
    return lax.ppermute(values, axis, [(i, i ^ bit) for i in range(count)])


def gather_blocks(values, bits):
    for bit in bits:
        values = jnp.concatenate([values, swap(values, bit, "tensor")], 1)
    return values


def halve(values, bit):
    half = values.shape[1] // 2
    return values[:, :half], swap(values[:, half:], bit, "tensor")


def tie(first, second):
    return lax.optimization_barrier((first, second))


def ignoring(kernel, at, count, *refs):
    return kernel(*refs[:at], *refs[at + count :])


def kernel_call(
    kernel, name, operands, out_shape, scratch=(), smem=(), out_smem=(), hbm=(), limit=16, flops=0, moved=0, exps=0, after=()
):
    if after:
        kernel = functools.partial(ignoring, kernel, len(operands), len(after))
    anywhere = [pl.BlockSpec(memory_space=pl.ANY)] * len(after)
    space = lambda yes, far=False: pl.BlockSpec(
        memory_space=pltpu.HBM if far else pltpu.SMEM if yes else pltpu.VMEM
    )
    return pl.pallas_call(
        kernel,
        out_shape=out_shape,
        in_specs=[space(i in smem, i in hbm) for i in range(len(operands))] + anywhere,
        out_specs=[space(i in out_smem) for i in range(len(out_shape))],
        scratch_shapes=list(scratch),
        compiler_params=pltpu.CompilerParams(vmem_limit_bytes=limit * MIB),
        cost_estimate=pl.CostEstimate(flops=flops, bytes_accessed=moved, transcendentals=exps),
        name=name,
    )(*operands, *after)


def bf16(*shape):
    return jax.ShapeDtypeStruct(shape, jnp.bfloat16)


def start_kernel(slots, route_hbm, len_hbm, list_hbm, docs_hbm, queries_hbm, meta_ref, early_ref, *refs):
    route_ref, len_ref, list_ref, docs_ref, queries_ref, sems = refs[-6:]
    send_refs = refs[:-6]
    pieces = (
        (route_hbm, route_ref),
        (docs_hbm, docs_ref),
        (queries_hbm, queries_ref),
        (len_hbm, len_ref),
        (list_hbm, list_ref),
    )
    copies = [pltpu.make_async_copy(a, b, sems.at[i]) for i, (a, b) in enumerate(pieces)]
    for copy in copies:
        copy.start()
    owners = route_ref.shape[0]
    doc_count, doc_rows, width = docs_ref.shape
    me = lax.axis_index("pair")
    copies[0].wait()
    copies[1].wait()
    for k in range(owners):
        picked = docs_ref[jnp.maximum(route_ref[me, me ^ k], 0)]
        send_refs[k][...] = picked
        if k == 0 and slots == owners:
            early_ref[1, 0] = picked
    copies[2].wait()
    asked = queries_ref[...].astype(jnp.float32).reshape(doc_rows, width)
    early_ref[0, 0] = asked.astype(jnp.bfloat16)
    copies[3].wait()
    copies[4].wait()
    for p in range(list_ref.shape[0]):
        meta_ref[p, 0] = list_ref[p, 0]
        for role in range(2):
            source = list_ref[p, 1 + role]
            if slots == owners:
                slot = source ^ me
            else:
                slot = jnp.int32(0)
                for j in range(owners):
                    slot = slot + jnp.where((j < source) & (route_ref[j, me] >= 0), 1, 0)
            meta_ref[p, 1 + role] = slot
            meta_ref[p, 3 + role] = len_ref[source * doc_count + jnp.maximum(route_ref[source, me], 0)]
        meta_ref[p, 5] = lax.axis_index("tensor")
    for k in range(owners):
        meta_ref[list_ref.shape[0], k] = route_ref[me, me ^ k]


def normed(values, gain):
    return rms_norm(values.astype(jnp.float32), gain).astype(jnp.bfloat16)


def early_kernel(kept_ref, came_ref, gain_ref, out_ref):
    for s in range(kept_ref.shape[0]):
        out_ref[s, 0] = normed(kept_ref[s, 0], gain_ref[...])
        out_ref[s, 1] = normed(came_ref[s, 0], gain_ref[...])


def late_kernel(extra, kept_ref, came_ref, *refs):
    gain_ref, raw_ref, out_ref = refs[-3:]
    for s in range(extra):
        raw_ref[s, 0] = refs[0][s + 1, 0]
        raw_ref[s, 1] = refs[1][s + 1, 0]
    for s in range(kept_ref.shape[0]):
        for part, ref in enumerate((kept_ref, came_ref)):
            raw_ref[extra + s, part] = ref[s, 0]
            out_ref[s, part] = normed(ref[s, 0], gain_ref[...])


def project_kernel(lead, kept_ref, came_ref, wq_ref, wk_ref, wv_ref, *refs):
    old, (q_ref, k_ref, v_ref) = refs[: len(refs) - 3], refs[len(refs) - 3 :]
    slots, half, rows, width = kept_ref.shape
    group = half * rows
    tall = slots * group
    tokens = jnp.concatenate([kept_ref[...].reshape(tall, width), came_ref[...].reshape(tall, width)], 0)
    scale = math.log2(math.e) / math.sqrt(HEAD)
    base_q, base_kv = 0, 0
    if old:
        base_q, base_kv = old[0].shape[0] if len(old) == 3 else 0, old[-1].shape[0]
        for ref, new_ref in zip(old, (q_ref, k_ref, v_ref)[3 - len(old) :]):
            new_ref[: ref.shape[0]] = ref[...]

    def store(ref, values, first, base):
        count = slots - first
        for part in range(2):
            for s in range(count):
                begin = part * count * group + s * group
                ref[base + s, part * half : (part + 1) * half] = (
                    values[begin : begin + group].astype(jnp.bfloat16).reshape(half, rows, values.shape[1])
                )

    if lead == slots:
        q_ref[...] = jnp.zeros_like(q_ref)
    else:
        asking = tokens
        if lead:
            asking = jnp.concatenate([tokens[lead * group : tall], tokens[tall + lead * group :]], 0)
        store(q_ref, jnp.dot(asking, wq_ref[...], preferred_element_type=jnp.float32) * scale, lead, base_q)
    store(k_ref, jnp.dot(tokens, wk_ref[...], preferred_element_type=jnp.float32), 0, base_kv)
    store(v_ref, jnp.dot(tokens, wv_ref[...], preferred_element_type=jnp.float32), 0, base_kv)


def project(name, lead, kept, came, weights, old):
    slots, half, rows, width = kept.shape
    wide = weights[0].shape[1]
    have_q = old[0].shape[0] if len(old) == 3 else 0
    have_kv = old[-1].shape[0] if old else 0
    nq, nkv = max(have_q + slots - lead, 1), have_kv + slots
    shape = lambda n: bf16(n, 2 * half, rows, wide)
    return kernel_call(
        functools.partial(project_kernel, lead),
        name,
        (kept, came, *weights, *old),
        [shape(nq), shape(nkv), shape(nkv)],
        limit=32,
        flops=2 * 2 * half * rows * width * wide * (3 * slots - lead),
        moved=6 * width * wide,
    )


def attend_kernel(bits, query_rows, owners, meta, q_ref, k_ref, v_ref, wo_ref, raw_ref, *refs):
    out_ref, rest_ref, mine_ref, role_ref, valid_ref, home_ref, ctx_ref, expo_ref = refs
    _, blocks, rows, width = q_ref.shape
    pairs = meta.shape[0] - 1
    slots = valid_ref.shape[0]
    flag = lambda yes: jnp.full((8, 128), yes.astype(jnp.float32), jnp.float32)
    place = lax.broadcasted_iota(jnp.int32, (rows, 128), 0) + meta[0, 5] * rows
    lengths = [jnp.int32(0)] * slots
    for p in range(pairs):
        for role in range(2):
            slot = meta[p, 1 + role]
            mine_ref[p, role] = raw_ref[slot]
            for s in range(slots):
                role_ref[2 * p + role, s] = flag(slot == s)
                lengths[s] = jnp.where(slot == s, meta[p, 3 + role], lengths[s])
    for s in range(slots):
        valid_ref[s] = (place < lengths[s]).astype(jnp.float32)
    for d in range(home_ref.shape[0]):
        for k in range(owners):
            home_ref[d, k] = flag(meta[pairs, k] == d)
    keys = blocks * rows
    heads = width // HEAD
    lane = lax.broadcasted_iota(jnp.int32, (1, keys), 1)
    block, row = lane // rows, lane % rows
    origin = jnp.zeros_like(lane)
    for place, bit in enumerate(bits):
        origin = origin + ((block >> place) & 1) * bit
    position = (origin ^ meta[0, 5]) * rows + row
    keep = lambda yes: jnp.where(yes, 0.0, jnp.float32(-1e30))
    ones = jnp.ones((3 * keys, HEAD), jnp.bfloat16)

    def rows_of(ref, places, at):
        return jnp.concatenate([ref[place, :, :, at].reshape(keys, HEAD) for place in places], 0)

    def one_pair(pair, carry):
        query, first, second = meta[pair, 0], meta[pair, 1], meta[pair, 2]
        bias = jnp.concatenate(
            [
                keep(position < meta[pair, 3]),
                keep(position < meta[pair, 4]),
                keep((row >= query * query_rows) & (row < (query + 1) * query_rows)),
            ],
            1,
        )
        for head in range(heads):
            at = slice(head * HEAD, (head + 1) * HEAD)
            qs = rows_of(q_ref, (first, second), at)
            ks = rows_of(k_ref, (first + 1, second + 1, 0), at)
            scores = lax.dot_general(qs, ks, (((1,), (1,)), ((), ())), preferred_element_type=jnp.float32) + bias
            top = jnp.max(scores, -1, keepdims=True)
            expo_ref[head] = jnp.exp2(scores - top).astype(jnp.bfloat16)
        for head in range(heads):
            at = slice(head * HEAD, (head + 1) * HEAD)
            vs = rows_of(v_ref, (first + 1, second + 1, 0), at)
            mixed = jnp.dot(expo_ref[head], jnp.concatenate([vs, ones], 1), preferred_element_type=jnp.float32)
            ctx_ref[pl.ds(pl.multiple_of(pair * 2 * keys, 2 * keys), 2 * keys), at] = (
                mixed[:, :HEAD] / mixed[:, HEAD:]
            ).astype(jnp.bfloat16)
        return carry

    lax.fori_loop(0, pairs, one_pair, 0)
    begin = out_ref.shape[0] * keys
    product = jnp.dot(ctx_ref[:begin], wo_ref[...], preferred_element_type=jnp.float32)
    out_ref[...] = product.astype(jnp.bfloat16).reshape(out_ref.shape)
    if begin < ctx_ref.shape[0]:
        rest_ref[...] = ctx_ref[begin:]


def attend(lead, bits, query_rows, doc_count, owners, meta, q, k, v, w_output, raw):
    _, blocks, rows, width = q.shape
    pairs, model, slots = meta.shape[0] - 1, w_output.shape[1], raw.shape[0]
    f32 = lambda *shape: jax.ShapeDtypeStruct(shape, jnp.float32)
    tall = 2 * blocks * rows
    return kernel_call(
        functools.partial(attend_kernel, bits, query_rows, owners),
        "attend",
        (meta, q, k, v, w_output, raw),
        [
            bf16(2 * lead, blocks, rows, model),
            bf16(max(pairs - lead, 1) * tall, width),
            bf16(pairs, 2, *raw.shape[1:]),
            f32(2 * pairs, slots, 8, 128),
            f32(slots, rows, 128),
            f32(doc_count, owners, 8, 128),
        ],
        scratch=[
            pltpu.VMEM((pairs * tall, width), jnp.bfloat16),
            pltpu.VMEM((width // HEAD, tall, tall * 3 // 2), jnp.bfloat16),
        ],
        smem=(0,),
        flops=2 * tall * width * (model + 3 * pairs * tall),
        moved=2 * model * width,
        exps=pairs * width // HEAD * tall * tall * 3 // 2,
    )


def output_kernel(groups, ctx_ref, wo_ref, *out_refs):
    product = jnp.dot(ctx_ref[...], wo_ref[...], preferred_element_type=jnp.float32).astype(jnp.bfloat16)
    tall = ctx_ref.shape[0] // sum(groups)
    for i, out_ref in enumerate(out_refs):
        begin = sum(groups[:i])
        out_ref[...] = product[begin * tall : (begin + groups[i]) * tall].reshape(out_ref.shape)


def settle_kernel(pair, kept_ref, came_ref, mine_ref, gain_ref, hidden_ref, ffn_ref):
    for role in range(kept_ref.shape[0]):
        for part in range(2):
            summed = kept_ref[role, part].astype(jnp.float32) + came_ref[role, 1 - part].astype(jnp.float32)
            hidden = mine_ref[pair + role // 2, role % 2, part].astype(jnp.float32) + summed
            if part == 0:
                hidden_ref[role] = hidden
            ffn_ref[role, part] = rms_norm(hidden, gain_ref[...]).astype(jnp.bfloat16)


def settle(pair, kept, came, mine, gain):
    roles, _, count, width = kept.shape
    return kernel_call(
        functools.partial(settle_kernel, pair),
        "settle",
        (kept, came, mine, gain),
        [jax.ShapeDtypeStruct((roles, count, width), jnp.float32), bf16(roles, 2, count, width)],
    )


def expand_kernel(pairs, tile, meta, w_ref, *refs):
    pieces, out_ref = refs[:-1], refs[-1]
    _, half, rows, width = pieces[0].shape
    group = half * rows
    tokens = jnp.concatenate(
        [
            pieces[i + part][role].reshape(group, width)
            for i in range(0, len(pieces), 2)
            for role in range(pieces[i].shape[0])
            for part in range(2)
        ],
        0,
    )

    def step(i, carry):
        at = pl.ds(pl.multiple_of(i * tile, tile), tile)
        units = jnp.maximum(jnp.dot(tokens, w_ref[:, at], preferred_element_type=jnp.float32), 0.0)
        units = units.astype(jnp.bfloat16)
        out_ref[:, :, at] = jnp.zeros((out_ref.shape[0], 2 * group, tile), jnp.bfloat16)
        for r in range(2 * pairs):
            slot = meta[r // 2, 1 + r % 2]
            out_ref[slot, :, at] = out_ref[slot, :, at] + units[r * 2 * group : (r + 1) * 2 * group]
        return carry

    lax.fori_loop(0, w_ref.shape[1] // tile, step, 0, unroll=2)


def expand(meta, pieces, w_in, slots):
    _, half, rows, width = pieces[0].shape
    units = w_in.shape[1]
    pairs = sum(piece.shape[0] for piece in pieces) // 4
    return kernel_call(
        functools.partial(expand_kernel, pairs, min(512, units)),
        "expand",
        (meta, w_in, *pieces),
        [bf16(slots, 2 * half * rows, units)],
        smem=(0,),
        limit=24,
        flops=2 * pairs * 4 * half * rows * width * units,
        moved=2 * width * units,
    )[0]


def shrink_kernel(low, high, begin, units_ref, w_ref, out_ref):
    _, tall, depth = units_ref.shape
    step = out_ref.shape[-1]
    product = jnp.dot(
        units_ref[low:high].reshape((high - low) * tall, depth),
        w_ref[:, begin : begin + step],
        preferred_element_type=jnp.float32,
    )
    out_ref[...] = product.astype(jnp.bfloat16).reshape(out_ref.shape)


def shrink(low, high, begin, step, units, w_down, blocks, after):
    _, tall, depth = units.shape
    return kernel_call(
        functools.partial(shrink_kernel, low, high, begin),
        "shrink",
        (units, w_down),
        [bf16(high - low, blocks, tall // blocks, step)],
        limit=24,
        flops=2 * (high - low) * tall * depth * step,
        moved=2 * depth * step,
        after=after,
    )[0]


def wide(flags, width):
    return jnp.concatenate([flags] * (width // 128), 1)


def finish_kernel(low, columns, role_ref, valid_ref, hidden_ref, *refs):
    pieces, out_refs = refs[: 2 * columns], refs[2 * columns :]
    roles, rows, width = hidden_ref.shape
    for i, out_ref in enumerate(out_refs):
        total = jnp.concatenate(
            [
                pieces[2 * c][i, 0].astype(jnp.float32) + pieces[2 * c + 1][i, 0].astype(jnp.float32)
                for c in range(columns)
            ],
            1,
        )
        for r in range(roles):
            chosen = jnp.concatenate([wide(role_ref[r, low + i], width)] * (rows // 8), 0)
            total = total + jnp.where(chosen > 0.0, hidden_ref[r], 0.0)
        valid = wide(valid_ref[low + i], width) > 0.0
        out_ref[...] = jnp.where(valid, total, 0.0).astype(jnp.bfloat16)


def home_kernel(home_ref, *refs):
    blocks, out_ref = refs[:-1], refs[-1]
    rows, width = blocks[0].shape
    for d in range(out_ref.shape[0]):
        total = jnp.zeros((rows, width), jnp.float32)
        for k, block in enumerate(blocks):
            chosen = jnp.concatenate([wide(home_ref[d, k], width)] * (rows // 8), 0)
            total = total + jnp.where(chosen > 0.0, block[...].astype(jnp.float32), 0.0)
        out_ref[d] = total.astype(jnp.bfloat16)


def local(
    queries,
    documents,
    doc_len,
    route,
    pair_list,
    attn_gain,
    w_query,
    w_key,
    w_value,
    w_output,
    ffn_gain,
    w_in,
    w_down,
):
    owners = lax.axis_size("pair")
    slices = lax.axis_size("tensor")
    doc_count, doc_rows, width = documents.shape
    query_count, query_rows, _ = queries.shape
    assert query_count * query_rows == doc_rows
    pairs = pair_list.shape[0]
    slots = min(2 * pairs, owners)
    direct = slots == owners
    down_bits = [1 << i for i in range(slices.bit_length() - 1)]
    up_bits = down_bits[::-1]
    attn_gain, ffn_gain = attn_gain.reshape(1, width), ffn_gain.reshape(1, width)
    weights = (w_query, w_key, w_value)

    meta, early, *arrived = kernel_call(
        functools.partial(start_kernel, slots),
        "start",
        (route, doc_len, pair_list, documents, queries),
        [jax.ShapeDtypeStruct((pairs + 1, max(6, owners)), jnp.int32), bf16(1 + direct, 1, doc_rows, width)]
        + [bf16(doc_rows, width)] * owners,
        scratch=[
            pltpu.SMEM(route.shape, jnp.int32),
            pltpu.SMEM(doc_len.shape, jnp.int32),
            pltpu.SMEM(pair_list.shape, jnp.int32),
            pltpu.VMEM(documents.shape, jnp.bfloat16),
            pltpu.VMEM(queries.shape, jnp.bfloat16),
            pltpu.SemaphoreType.DMA((5,)),
        ],
        hbm=(0, 1, 2, 3, 4),
        out_smem=(0,),
        limit=63,
        flops=8 * 10**9,
    )
    arrived = [block if k == 0 else swap(block, k, "pair") for k, block in enumerate(arrived)]
    if not direct:
        me = lax.axis_index("pair")
        taken = lax.dynamic_slice_in_dim(route, me, 1, 1)[:, 0] >= 0
        source = me ^ jnp.arange(owners, dtype=jnp.int32)
        other = jnp.arange(owners, dtype=jnp.int32)
        slot_of = jnp.sum(jnp.where((other[None, :] < source[:, None]) & taken[None, :], 1, 0), 1)
        is_taken = jnp.sum(jnp.where((other[None, :] == source[:, None]) & taken[None, :], 1, 0), 1)
        place = jnp.where(is_taken > 0, slot_of, -1)
        table = (other[:slots, None] == place[None, :]).astype(jnp.bfloat16)
        packed = jnp.einsum("sk,krd->srd", table, jnp.stack(arrived), preferred_element_type=jnp.float32)
        arrived = [packed[s].astype(jnp.bfloat16) for s in range(slots)]
    top = up_bits[0]
    pairwise = lambda a: bf16(a.shape[0], 2, doc_rows, width)
    early_came = swap(early, top, "tensor")
    early_norm = kernel_call(early_kernel, "early", (early, early_came, attn_gain), [pairwise(early)], flops=8 * 10**9)[0]
    late = jnp.stack(arrived[direct:])[:, None]
    late, early_norm = tie(late, early_norm)
    late_came = swap(late, top, "tensor")
    more = (early, early_came) if direct else ()
    rows_own, late_norm = kernel_call(
        functools.partial(late_kernel, int(direct)),
        "late",
        (late, late_came, *more, attn_gain),
        [bf16(slots, 2, doc_rows, width), pairwise(late)],
        flops=8 * 10**9,
    )

    def spread(kept):
        return kept, swap(kept, up_bits[-1], "tensor")

    early_kept = gather_blocks(early_norm, up_bits[1:-1])
    first = project("project_early", 1, *spread(early_kept), weights, ())
    late_kept = gather_blocks(late_norm, up_bits[1:-1])
    late_kept, first = tie(late_kept, first)
    q, k, v = project("project_late", 0, *spread(late_kept), weights, first if direct else first[1:])

    groups = [1] * pairs
    part, rest, mine, roles, valid, homes = attend(
        groups[0], up_bits, query_rows, doc_count, owners, meta, q, k, v, w_output, rows_own
    )
    parts = [part]
    if groups[1:]:
        parts += kernel_call(
            functools.partial(output_kernel, groups[1:]),
            "output",
            (rest, w_output),
            [bf16(2 * n, *part.shape[1:]) for n in groups[1:]],
            flops=2 * rest.size * width,
            moved=2 * w_output.size,
        )
    hidden, pieces = [], []
    for group, part in enumerate(parts):
        for bit in down_bits[:-1]:
            kept, came = halve(part, bit)
            part = kept + came
        came = swap(part, down_bits[-1], "tensor")
        own, ffn = settle(sum(groups[:group]), part, came, mine, ffn_gain)
        hidden.append(own)
        pieces += spread(gather_blocks(ffn, up_bits[1:-1]))
    units = expand(meta, pieces, w_in, slots)
    hidden = jnp.concatenate(hidden, 0)

    def shrunk(low, high, columns, after=()):
        step = width // columns
        return [shrink(low, high, c * step, step, units, w_down, slices, after) for c in range(columns)]

    def reduce(parts, low, high):
        columns = len(parts)
        pieces = []
        for part in parts:
            for bit in down_bits:
                kept, came = halve(part, bit)
                if bit != down_bits[-1]:
                    part = kept + came
            pieces += [kept, came]
        return kernel_call(
            functools.partial(finish_kernel, low, columns),
            "finish",
            (roles, valid, hidden, *pieces),
            [bf16(doc_rows, width)] * (high - low),
        )

    blocks = reduce(shrunk(0, slots, 2), 0, slots)
    if not direct:
        packed = jnp.einsum("sk,srd->krd", table, jnp.stack(blocks), preferred_element_type=jnp.float32)
        blocks = [packed[s].astype(jnp.bfloat16) for s in range(owners)]
    blocks = [block if k == 0 else swap(block, k, "pair") for k, block in enumerate(blocks)]
    return kernel_call(home_kernel, "home", (homes, *blocks), [bf16(doc_count, doc_rows, width)])[0]


def solution(mesh):
    placed = (
        P("pair", "tensor", None),
        P("pair", "tensor", None),
        P(),
        P(),
        P("pair", None),
        P(),
        P(None, "tensor"),
        P(None, "tensor"),
        P(None, "tensor"),
        P("tensor", None),
        P(),
        P(None, "tensor"),
        P("tensor", None),
    )
    return jax.shard_map(
        local, mesh=mesh, in_specs=placed, out_specs=P("pair", "tensor", None), check_vma=False
    )
```

time: 127 us -> 111 us (0.87)
  Pallas kernels: 37.3 us -> 26.9 us
  local copies, waits for them, and re-layouts: 8.06 us -> 1.14 us
  starting transfers between devices: 42.7 us -> 45.9 us
  waiting for transfers between devices: 38.1 us -> 36.2 us
    pallas_call x17 -> x15, Pallas kernels: 37.3 us -> 26.9 us  [kernel_call(): pl.pallas_call(kernel, out_shape=out_shape, in_specs=[space(i in smem, i...]
    unnamed x42 -> x28, local copies, waits for them, and re-layouts: 7.81 us -> 0.93 us
    ppermute x36 -> x33, starting transfers between devices: 42.7 us -> 45.9 us  [swap(): return lax.ppermute(values, axis, [(i, i ^ bit) for i in range(count)])]
    ppermute x36 -> x33, waiting for transfers between devices: 38.1 us -> 36.2 us  [swap(): return lax.ppermute(values, axis, [(i, i ^ bit) for i in range(count)])]
  transfers between devices with their start and end apart: 36 -> 33, of which waited for: 21 -> 22; matrix products, arithmetic and copies ran while one was open for 1% -> 0% of each run, Pallas kernels for 17% -> 4%
where the time goes in v3:
time: 111 us
  starting transfers between devices  45.9 us (41%)
  waiting for transfers between devices  36.2 us (33%)
  Pallas kernels  26.9 us (24%)
  local copies, waits for them, and re-layouts  1.14 us (1%)
    ppermute x33, starting transfers between devices, swap(): return lax.ppermute(values, axis, [(i, i ^ bit) for i in range(count)])  45.9 us
    ppermute x33, waiting for transfers between devices, swap(): return lax.ppermute(values, axis, [(i, i ^ bit) for i in range(count)])  36.2 us
    pallas_call x15, Pallas kernels, kernel_call(): pl.pallas_call(kernel, out_shape=out_shape, in_specs=[space(i in smem, i...  26.9 us
  transfers between devices with their start and end apart: 33, of which 22 were waited for; matrix products, arithmetic and copies ran while one was open for 0% of the time, Pallas kernels for 4%

profile of v3, /device:TPU:0, one launch (start us, length us, event | category | flops | bytes accessed | tf_op | source)
XLA Modules:
  0.0 110.8 jit_solution(10164104793591022209)
XLA Ops:
  1.7 3.0 %collective-permute-start = (bf16[16,1024]{1,0:T(8,128)(2,1)}, bf16[16,1024]{1,0:T(8,128)(2,1)S(1)}, u32[]{:S(2)}, u32[]{:S(2)}) collective-permute-start(bf16[16,1024]{1,0:T(8,128)(2,1)} %get-tuple-element.43), channel_id=1, source_target_pairs={{0,8},{8,0},{16,24},{24,16},{1,9},{9,1},{17,25},{25,17},{2,10},{10... | collective-permute-start | bytes 98312 | tf_op jit(solution)/shard_map/ppermute | solution.py:22
  6.2 3.0 %collective-permute-start.3 = (bf16[2,1,16,1024]{3,2,1,0:T(8,128)(2,1)}, bf16[2,1,16,1024]{3,2,1,0:T(8,128)(2,1)S(1)}, u32[]{:S(2)}, u32[]{:S(2)}) collective-permute-start(bf16[2,1,16,1024]{3,2,1,0:T(8,128)(2,1)} %get-tuple-element.46.kept_ref.refs_0_), channel_id=1, source_target_pairs={{0,4},{1,5},{2,6},{3,7},{4,0},{5,1},{6,2},{7,3},{8,12},{9,13},{10,... | collective-permute-start | bytes 196616 | tf_op jit(solution)/shard_map/ppermute | solution.py:22
  9.3 2.0 %collective-permute-done.2 = bf16[16,1024]{1,0:T(8,128)(2,1)S(1)} collective-permute-done((bf16[16,1024]{1,0:T(8,128)(2,1)}, bf16[16,1024]{1,0:T(8,128)(2,1)S(1)}, u32[]{:S(2)}, u32[]{:S(2)}) %collective-permute-start.2) | collective-permute-done | bytes 32800 | tf_op jit(solution)/shard_map/ppermute | solution.py:22
  12.8 3.0 %collective-permute-start.4 = (bf16[3,1,16,1024]{3,2,1,0:T(8,128)(2,1)S(1)}, bf16[3,1,16,1024]{3,2,1,0:T(8,128)(2,1)S(1)}, u32[]{:S(2)}, u32[]{:S(2)}) collective-permute-start(bf16[3,1,16,1024]{3,2,1,0:T(8,128)(2,1)S(1)} %maximum_bitcast_fusion.kept_ref), channel_id=1, source_target_pairs={{0,4},{1,5},{2,6},{3,7},{4,0},{5,1},{6,2},{7,3},{8,12},{9,13},{10,... | collective-permute-start | bytes 294920 | tf_op jit(solution)/shard_map/ppermute | solution.py:22
  15.8 2.1 %collective-permute-start.6 = (bf16[2,2,16,1024]{3,2,1,0:T(8,128)(2,1)S(1)}, bf16[2,2,16,1024]{3,2,1,0:T(8,128)(2,1)S(1)}, u32[]{:S(2)}, u32[]{:S(2)}) collective-permute-start(bf16[2,2,16,1024]{3,2,1,0:T(8,128)(2,1)S(1)} %early.1), channel_id=1, source_target_pairs={{0,2},{1,3},{2,0},{3,1},{4,6},{5,7},{6,4},{7,5},{8,10},{9,11},{10,... | collective-permute-start | bytes 393224 | tf_op jit(solution)/shard_map/ppermute | solution.py:22
  18.6 2.1 %collective-permute-start.5 = (bf16[3,2,16,1024]{3,2,1,0:T(8,128)(2,1)S(1)}, bf16[3,2,16,1024]{3,2,1,0:T(8,128)(2,1)S(1)}, u32[]{:S(2)}, u32[]{:S(2)}) collective-permute-start(bf16[3,2,16,1024]{3,2,1,0:T(8,128)(2,1)S(1)} %get-tuple-element.48), channel_id=1, source_target_pairs={{0,2},{1,3},{2,0},{3,1},{4,6},{5,7},{6,4},{7,5},{8,10},{9,11},{10,... | collective-permute-start | bytes 589832 | tf_op jit(solution)/shard_map/ppermute | solution.py:22
  22.3 2.0 %collective-permute-done.5 = bf16[3,2,16,1024]{3,2,1,0:T(8,128)(2,1)S(1)} collective-permute-done((bf16[3,2,16,1024]{3,2,1,0:T(8,128)(2,1)S(1)}, bf16[3,2,16,1024]{3,2,1,0:T(8,128)(2,1)S(1)}, u32[]{:S(2)}, u32[]{:S(2)}) %collective-permute-start.5) | collective-permute-done | bytes 196640 | tf_op jit(solution)/shard_map/ppermute | solution.py:22
  27.8 2.6 %project_late.1 = (bf16[4,8,16,1024]{3,2,1,0:T(8,128)(2,1)S(1)}, bf16[5,8,16,1024]{3,2,1,0:T(8,128)(2,1)S(1)}, bf16[5,8,16,1024]{3,2,1,0:T(8,128)(2,1)S(1)}) custom-call(bf16[3,4,16,1024]{3,2,1,0:T(8,128)(2,1)S(1)} %pad_maximum_fusion.kept_ref, bf16[3,4,16,1024]{3,2,1,0:T(8,128)(2,1)S(1)} %collective-permute-done.8.came_ref, bf16[1024,1024]{1,0:T(8,128)(2,1)S(1)} %copy-done, ...), custom_call_target="tpu_custom_call" | custom-call | flops 2415919104 | bytes 6291456 | tf_op jit(solution)/shard_map/project_late/pallas_call | solution.py:53
  30.5 5.5 %attend.1 = (bf16[2,8,16,1024]{3,2,1,0:T(8,128)(2,1)S(1)}, bf16[512,1024]{1,0:T(8,128)(2,1)S(1)}, bf16[3,2,2,16,1024]{4,3,2,1,0:T(8,128)(2,1)S(1)}, f32[6,4,8,12...) custom-call(s32[4,6]{1,0:T(4,128)S(1)} %copy-done.7, ...), custom_call_target="tpu_custom_call" | custom-call | flops 1744830464 | bytes 2097152 | tf_op jit(solution)/shard_map/attend/pallas_call | solution.py:53
  38.2 2.1 %collective-permute-start.10 = (bf16[2,2,16,1024]{3,2,1,0:T(8,128)(2,1)S(1)}, bf16[2,2,16,1024]{3,2,1,0:T(8,128)(2,1)S(1)}, u32[]{:S(2)}, u32[]{:S(2)}) collective-permute-start(bf16[2,2,16,1024]{3,2,1,0:T(8,128)(2,1)S(1)} %slice.97), channel_id=1, source_target_pairs={{0,2},{1,3},{2,0},{3,1},{4,6},{5,7},{6,4},{7,5},{8,10},{9,11},{10,... | collective-permute-start | bytes 393224 | tf_op jit(solution)/shard_map/ppermute | solution.py:22
  42.5 2.1 %collective-permute-done.10 = bf16[2,2,16,1024]{3,2,1,0:T(8,128)(2,1)S(1)} collective-permute-done((bf16[2,2,16,1024]{3,2,1,0:T(8,128)(2,1)S(1)}, bf16[2,2,16,1024]{3,2,1,0:T(8,128)(2,1)S(1)}, u32[]{:S(2)}, u32[]{:S(2)}) %collective-permute-start.10) | collective-permute-done | bytes 131104 | tf_op jit(solution)/shard_map/ppermute | solution.py:22
  44.6 3.6 %collective-permute-start.11 = (bf16[2,2,16,1024]{3,2,1,0:T(8,128)(2,1)S(1)}, bf16[2,2,16,1024]{3,2,1,0:T(8,128)(2,1)S(1)}, u32[]{:S(2)}, u32[]{:S(2)}) collective-permute-start(bf16[2,2,16,1024]{3,2,1,0:T(8,128)(2,1)S(1)} %slice_add_fusion.9.kept_ref), channel_id=1, source_target_pairs={{0,4},{1,5},{2,6},{3,7},{4,0},{5,1},{6,2},{7,3},{8,12},{9,13},{10,... | collective-permute-start | bytes 393224 | tf_op jit(solution)/shard_map/ppermute | solution.py:22
  48.2 2.8 %collective-permute-start.17 = (bf16[2,2,16,1024]{3,2,1,0:T(8,128)(2,1)S(1)}, bf16[2,2,16,1024]{3,2,1,0:T(8,128)(2,1)S(1)}, u32[]{:S(2)}, u32[]{:S(2)}) collective-permute-start(bf16[2,2,16,1024]{3,2,1,0:T(8,128)(2,1)S(1)} %slice_add_fusion.7.kept_ref), channel_id=1, source_target_pairs={{0,4},{1,5},{2,6},{3,7},{4,0},{5,1},{6,2},{7,3},{8,12},{9,13},{10,... | collective-permute-start | bytes 393224 | tf_op jit(solution)/shard_map/ppermute | solution.py:22
  51.0 3.3 %collective-permute-done.13 = bf16[2,2,16,1024]{3,2,1,0:T(8,128)(2,1)S(1)} collective-permute-done((bf16[2,2,16,1024]{3,2,1,0:T(8,128)(2,1)S(1)}, bf16[2,2,16,1024]{3,2,1,0:T(8,128)(2,1)S(1)}, u32[]{:S(2)}, u32[]{:S(2)}) %collective-permute-start.13) | collective-permute-done | bytes 131104 | tf_op jit(solution)/shard_map/ppermute | solution.py:22
  54.6 7.5 %collective-permute-start.18 = (bf16[2,2,16,1024]{3,2,1,0:T(8,128)(2,1)S(1)}, bf16[2,2,16,1024]{3,2,1,0:T(8,128)(2,1)S(1)}, u32[]{:S(2)}, u32[]{:S(2)}) collective-permute-start(bf16[2,2,16,1024]{3,2,1,0:T(8,128)(2,1)S(1)} %get-tuple-element.72), channel_id=1, source_target_pairs={{0,2},{1,3},{2,0},{3,1},{4,6},{5,7},{6,4},{7,5},{8,10},{9,11},{10,... | collective-permute-start | bytes 393224 | tf_op jit(solution)/shard_map/ppermute | solution.py:22
  68.3 2.7 %collective-permute-done.22 = bf16[2,2,16,1024]{3,2,1,0:T(8,128)(2,1)S(1)} collective-permute-done((bf16[2,2,16,1024]{3,2,1,0:T(8,128)(2,1)S(1)}, bf16[2,2,16,1024]{3,2,1,0:T(8,128)(2,1)S(1)}, u32[]{:S(2)}, u32[]{:S(2)}) %collective-permute-start.22) | collective-permute-done | bytes 131104 | tf_op jit(solution)/shard_map/ppermute | solution.py:22
  74.1 8.1 %expand.1.units_ref = bf16[4,128,4096]{2,1,0:T(8,128)(2,1)S(1)} custom-call(s32[4,6]{1,0:T(4,128)S(1)} %copy-done.7, bf16[1024,4096]{1,0:T(8,128)(2,1)S(1)} %bitcast.13, bf16[2,4,16,1024]{3,2,1,0:T(8,128)(2,1)S(1)} %constant_dynamic-update-slice_fusion.2.refs_0_, bf16[2,4,16,1024]{3,2,1,0:T(8,128)(2,1)S(1)} %collective-permute-done.19.refs_1_, ...), custom_call_target="tpu_custom_call" | custom-call | flops 6442450944 | bytes 8388608 | tf_op jit(solution)/shard_map/expand/pallas_call | solution.py:53
  82.1 2.3 %shrink.3 = bf16[4,8,16,512]{3,2,1,0:T(8,128)(2,1)S(1)} custom-call(bf16[4,128,4096]{2,1,0:T(8,128)(2,1)S(1)} %expand.1.units_ref, bf16[4096,1024]{1,0:T(8,128)(2,1)S(1)} %bitcast.8), custom_call_target="tpu_custom_call" | custom-call | flops 2147483648 | bytes 4194304 | tf_op jit(solution)/shard_map/shrink/pallas_call | solution.py:53
  84.7 2.3 %shrink.2 = bf16[4,8,16,512]{3,2,1,0:T(8,128)(2,1)S(1)} custom-call(bf16[4,128,4096]{2,1,0:T(8,128)(2,1)S(1)} %expand.1.units_ref, bf16[4096,1024]{1,0:T(8,128)(2,1)S(1)} %bitcast.8), custom_call_target="tpu_custom_call" | custom-call | flops 2147483648 | bytes 4194304 | tf_op jit(solution)/shard_map/shrink/pallas_call | solution.py:53
  89.8 4.2 %collective-permute-done.28 = bf16[4,2,16,512]{3,2,1,0:T(8,128)(2,1)S(1)} collective-permute-done((bf16[4,2,16,512]{3,2,1,0:T(8,128)(2,1)S(1)}, bf16[4,2,16,512]{3,2,1,0:T(8,128)(2,1)S(1)}, u32[]{:S(2)}, u32[]{:S(2)}) %collective-permute-start.28) | collective-permute-done | bytes 131104 | tf_op jit(solution)/shard_map/ppermute | solution.py:22
  94.0 2.1 %collective-permute-start.29 = (bf16[4,1,16,512]{3,2,1,0:T(8,128)(2,1)S(1)}, bf16[4,1,16,512]{3,2,1,0:T(8,128)(2,1)S(1)}, u32[]{:S(2)}, u32[]{:S(2)}) collective-permute-start(bf16[4,1,16,512]{3,2,1,0:T(8,128)(2,1)S(1)} %get-tuple-element.79), channel_id=1, source_target_pairs={{0,4},{1,5},{2,6},{3,7},{4,0},{5,1},{6,2},{7,3},{8,12},{9,13},{10,... | collective-permute-start | bytes 196616 | tf_op jit(solution)/shard_map/ppermute | solution.py:22
  96.1 2.8 %collective-permute-start.26 = (bf16[4,1,16,512]{3,2,1,0:T(8,128)(2,1)S(1)}, bf16[4,1,16,512]{3,2,1,0:T(8,128)(2,1)S(1)}, u32[]{:S(2)}, u32[]{:S(2)}) collective-permute-start(bf16[4,1,16,512]{3,2,1,0:T(8,128)(2,1)S(1)} %get-tuple-element.81), channel_id=1, source_target_pairs={{0,4},{1,5},{2,6},{3,7},{4,0},{5,1},{6,2},{7,3},{8,12},{9,13},{10,... | collective-permute-start | bytes 196616 | tf_op jit(solution)/shard_map/ppermute | solution.py:22
  98.9 2.0 %collective-permute-done.29.refs_3_ = bf16[4,1,16,512]{3,2,1,0:T(8,128)(2,1)S(1)} collective-permute-done((bf16[4,1,16,512]{3,2,1,0:T(8,128)(2,1)S(1)}, bf16[4,1,16,512]{3,2,1,0:T(8,128)(2,1)S(1)}, u32[]{:S(2)}, u32[]{:S(2)}) %collective-permute-start.29) | collective-permute-done | bytes 65568 | tf_op jit(solution)/shard_map/ppermute | solution.py:22
  107.7 2.4 %collective-permute-done.32.refs_3_ = bf16[16,1024]{1,0:T(8,128)(2,1)S(1)} collective-permute-done((bf16[16,1024]{1,0:T(8,128)(2,1)S(1)}, bf16[16,1024]{1,0:T(8,128)(2,1)S(1)}, u32[]{:S(2)}, u32[]{:S(2)}) %collective-permute-start.32) | collective-permute-done | bytes 32800 | tf_op jit(solution)/shard_map/ppermute | solution.py:22
  (116 shorter events, 34.9 us)
Async XLA Ops:
  1.7 7.6 %collective-permute-start = (bf16[16,1024]{1,0:T(8,128)(2,1)}, bf16[16,1024]{1,0:T(8,128)(2,1)S(1)}, u32[]{:S(2)}, u32[]{:S(2)}) collective-permute-start(bf16[16,1024]{1,0:T(8,128)(2,1)} %get-tuple-element.43), channel_id=1, source_target_pairs={{0,8},{8,0},{16,24},{24,16},{1,9},{9,1},{17,25},{25,17},{2,10},{10... | collective-permute-start | bytes 98312 | tf_op jit(solution)/shard_map/ppermute | solution.py:22
  4.7 4.6 %collective-permute-start.1 = (bf16[16,1024]{1,0:T(8,128)(2,1)}, bf16[16,1024]{1,0:T(8,128)(2,1)S(1)}, u32[]{:S(2)}, u32[]{:S(2)}) collective-permute-start(bf16[16,1024]{1,0:T(8,128)(2,1)} %get-tuple-element.44), channel_id=1, source_target_pairs={{0,16},{8,24},{16,0},{24,8},{1,17},{9,25},{17,1},{25,9},{2,18},{10... | collective-permute-start | bytes 98312 | tf_op jit(solution)/shard_map/ppermute | solution.py:22
  6.2 5.0 %collective-permute-start.2 = (bf16[16,1024]{1,0:T(8,128)(2,1)}, bf16[16,1024]{1,0:T(8,128)(2,1)S(1)}, u32[]{:S(2)}, u32[]{:S(2)}) collective-permute-start(bf16[16,1024]{1,0:T(8,128)(2,1)} %get-tuple-element.45), channel_id=1, source_target_pairs={{0,24},{8,16},{16,8},{24,0},{1,25},{9,17},{17,9},{25,1},{2,26},{10... | collective-permute-start | bytes 98312 | tf_op jit(solution)/shard_map/ppermute | solution.py:22
  6.2 5.6 %collective-permute-start.3 = (bf16[2,1,16,1024]{3,2,1,0:T(8,128)(2,1)}, bf16[2,1,16,1024]{3,2,1,0:T(8,128)(2,1)S(1)}, u32[]{:S(2)}, u32[]{:S(2)}) collective-permute-start(bf16[2,1,16,1024]{3,2,1,0:T(8,128)(2,1)} %get-tuple-element.46.kept_ref.refs_0_), channel_id=1, source_target_pairs={{0,4},{1,5},{2,6},{3,7},{4,0},{5,1},{6,2},{7,3},{8,12},{9,13},{10,... | collective-permute-start | bytes 196616 | tf_op jit(solution)/shard_map/ppermute | solution.py:22
  12.8 5.7 %collective-permute-start.4 = (bf16[3,1,16,1024]{3,2,1,0:T(8,128)(2,1)S(1)}, bf16[3,1,16,1024]{3,2,1,0:T(8,128)(2,1)S(1)}, u32[]{:S(2)}, u32[]{:S(2)}) collective-permute-start(bf16[3,1,16,1024]{3,2,1,0:T(8,128)(2,1)S(1)} %maximum_bitcast_fusion.kept_ref), channel_id=1, source_target_pairs={{0,4},{1,5},{2,6},{3,7},{4,0},{5,1},{6,2},{7,3},{8,12},{9,13},{10,... | collective-permute-start | bytes 294920 | tf_op jit(solution)/shard_map/ppermute | solution.py:22
  15.8 6.5 %collective-permute-start.6 = (bf16[2,2,16,1024]{3,2,1,0:T(8,128)(2,1)S(1)}, bf16[2,2,16,1024]{3,2,1,0:T(8,128)(2,1)S(1)}, u32[]{:S(2)}, u32[]{:S(2)}) collective-permute-start(bf16[2,2,16,1024]{3,2,1,0:T(8,128)(2,1)S(1)} %early.1), channel_id=1, source_target_pairs={{0,2},{1,3},{2,0},{3,1},{4,6},{5,7},{6,4},{7,5},{8,10},{9,11},{10,... | collective-permute-start | bytes 393224 | tf_op jit(solution)/shard_map/ppermute | solution.py:22
  18.6 5.8 %collective-permute-start.5 = (bf16[3,2,16,1024]{3,2,1,0:T(8,128)(2,1)S(1)}, bf16[3,2,16,1024]{3,2,1,0:T(8,128)(2,1)S(1)}, u32[]{:S(2)}, u32[]{:S(2)}) collective-permute-start(bf16[3,2,16,1024]{3,2,1,0:T(8,128)(2,1)S(1)} %get-tuple-element.48), channel_id=1, source_target_pairs={{0,2},{1,3},{2,0},{3,1},{4,6},{5,7},{6,4},{7,5},{8,10},{9,11},{10,... | collective-permute-start | bytes 589832 | tf_op jit(solution)/shard_map/ppermute | solution.py:22
  38.2 6.5 %collective-permute-start.10 = (bf16[2,2,16,1024]{3,2,1,0:T(8,128)(2,1)S(1)}, bf16[2,2,16,1024]{3,2,1,0:T(8,128)(2,1)S(1)}, u32[]{:S(2)}, u32[]{:S(2)}) collective-permute-start(bf16[2,2,16,1024]{3,2,1,0:T(8,128)(2,1)S(1)} %slice.97), channel_id=1, source_target_pairs={{0,2},{1,3},{2,0},{3,1},{4,6},{5,7},{6,4},{7,5},{8,10},{9,11},{10,... | collective-permute-start | bytes 393224 | tf_op jit(solution)/shard_map/ppermute | solution.py:22
  40.3 7.9 %collective-permute-start.16 = (bf16[2,2,16,1024]{3,2,1,0:T(8,128)(2,1)S(1)}, bf16[2,2,16,1024]{3,2,1,0:T(8,128)(2,1)S(1)}, u32[]{:S(2)}, u32[]{:S(2)}) collective-permute-start(bf16[2,2,16,1024]{3,2,1,0:T(8,128)(2,1)S(1)} %slice.101), channel_id=1, source_target_pairs={{0,2},{1,3},{2,0},{3,1},{4,6},{5,7},{6,4},{7,5},{8,10},{9,11},{10,... | collective-permute-start | bytes 393224 | tf_op jit(solution)/shard_map/ppermute | solution.py:22
  41.3 13.0 %collective-permute-start.13 = (bf16[2,2,16,1024]{3,2,1,0:T(8,128)(2,1)S(1)}, bf16[2,2,16,1024]{3,2,1,0:T(8,128)(2,1)S(1)}, u32[]{:S(2)}, u32[]{:S(2)}) collective-permute-start(bf16[2,2,16,1024]{3,2,1,0:T(8,128)(2,1)S(1)} %slice.99), channel_id=1, source_target_pairs={{0,2},{1,3},{2,0},{3,1},{4,6},{5,7},{6,4},{7,5},{8,10},{9,11},{10,... | collective-permute-start | bytes 393224 | tf_op jit(solution)/shard_map/ppermute | solution.py:22
  44.6 9.8 %collective-permute-start.11 = (bf16[2,2,16,1024]{3,2,1,0:T(8,128)(2,1)S(1)}, bf16[2,2,16,1024]{3,2,1,0:T(8,128)(2,1)S(1)}, u32[]{:S(2)}, u32[]{:S(2)}) collective-permute-start(bf16[2,2,16,1024]{3,2,1,0:T(8,128)(2,1)S(1)} %slice_add_fusion.9.kept_ref), channel_id=1, source_target_pairs={{0,4},{1,5},{2,6},{3,7},{4,0},{5,1},{6,2},{7,3},{8,12},{9,13},{10,... | collective-permute-start | bytes 393224 | tf_op jit(solution)/shard_map/ppermute | solution.py:22
  48.2 15.7 %collective-permute-start.17 = (bf16[2,2,16,1024]{3,2,1,0:T(8,128)(2,1)S(1)}, bf16[2,2,16,1024]{3,2,1,0:T(8,128)(2,1)S(1)}, u32[]{:S(2)}, u32[]{:S(2)}) collective-permute-start(bf16[2,2,16,1024]{3,2,1,0:T(8,128)(2,1)S(1)} %slice_add_fusion.7.kept_ref), channel_id=1, source_target_pairs={{0,4},{1,5},{2,6},{3,7},{4,0},{5,1},{6,2},{7,3},{8,12},{9,13},{10,... | collective-permute-start | bytes 393224 | tf_op jit(solution)/shard_map/ppermute | solution.py:22
  54.3 11.2 %collective-permute-start.14 = (bf16[2,2,16,1024]{3,2,1,0:T(8,128)(2,1)S(1)}, bf16[2,2,16,1024]{3,2,1,0:T(8,128)(2,1)S(1)}, u32[]{:S(2)}, u32[]{:S(2)}) collective-permute-start(bf16[2,2,16,1024]{3,2,1,0:T(8,128)(2,1)S(1)} %slice_add_fusion.8.kept_ref), channel_id=1, source_target_pairs={{0,4},{1,5},{2,6},{3,7},{4,0},{5,1},{6,2},{7,3},{8,12},{9,13},{10,... | collective-permute-start | bytes 393224 | tf_op jit(solution)/shard_map/ppermute | solution.py:22
  54.6 13.7 %collective-permute-start.18 = (bf16[2,2,16,1024]{3,2,1,0:T(8,128)(2,1)S(1)}, bf16[2,2,16,1024]{3,2,1,0:T(8,128)(2,1)S(1)}, u32[]{:S(2)}, u32[]{:S(2)}) collective-permute-start(bf16[2,2,16,1024]{3,2,1,0:T(8,128)(2,1)S(1)} %get-tuple-element.72), channel_id=1, source_target_pairs={{0,2},{1,3},{2,0},{3,1},{4,6},{5,7},{6,4},{7,5},{8,10},{9,11},{10,... | collective-permute-start | bytes 393224 | tf_op jit(solution)/shard_map/ppermute | solution.py:22
  64.0 7.0 %collective-permute-start.22 = (bf16[2,2,16,1024]{3,2,1,0:T(8,128)(2,1)S(1)}, bf16[2,2,16,1024]{3,2,1,0:T(8,128)(2,1)S(1)}, u32[]{:S(2)}, u32[]{:S(2)}) collective-permute-start(bf16[2,2,16,1024]{3,2,1,0:T(8,128)(2,1)S(1)} %get-tuple-element.74), channel_id=1, source_target_pairs={{0,2},{1,3},{2,0},{3,1},{4,6},{5,7},{6,4},{7,5},{8,10},{9,11},{10,... | collective-permute-start | bytes 393224 | tf_op jit(solution)/shard_map/ppermute | solution.py:22
  65.7 6.8 %collective-permute-start.20 = (bf16[2,2,16,1024]{3,2,1,0:T(8,128)(2,1)S(1)}, bf16[2,2,16,1024]{3,2,1,0:T(8,128)(2,1)S(1)}, u32[]{:S(2)}, u32[]{:S(2)}) collective-permute-start(bf16[2,2,16,1024]{3,2,1,0:T(8,128)(2,1)S(1)} %get-tuple-element.73), channel_id=1, source_target_pairs={{0,2},{1,3},{2,0},{3,1},{4,6},{5,7},{6,4},{7,5},{8,10},{9,11},{10,... | collective-permute-start | bytes 393224 | tf_op jit(solution)/shard_map/ppermute | solution.py:22
  68.3 4.3 %collective-permute-start.19 = (bf16[2,4,16,1024]{3,2,1,0:T(8,128)(2,1)S(1)}, bf16[2,4,16,1024]{3,2,1,0:T(8,128)(2,1)S(1)}, u32[]{:S(2)}, u32[]{:S(2)}) collective-permute-start(bf16[2,4,16,1024]{3,2,1,0:T(8,128)(2,1)S(1)} %constant_dynamic-update-slice_fusion.2.refs_0_), channel_id=1, source_target_pairs={{0,1},{1,0},{2,3},{3,2},{4,5},{5,4},{6,7},{7,6},{8,9},{9,8},{10,11... | collective-permute-start | bytes 786440 | tf_op jit(solution)/shard_map/ppermute | solution.py:22
  87.6 6.4 %collective-permute-start.28 = (bf16[4,2,16,512]{3,2,1,0:T(8,128)(2,1)S(1)}, bf16[4,2,16,512]{3,2,1,0:T(8,128)(2,1)S(1)}, u32[]{:S(2)}, u32[]{:S(2)}) collective-permute-start(bf16[4,2,16,512]{3,2,1,0:T(8,128)(2,1)S(1)} %slice.111), channel_id=1, source_target_pairs={{0,2},{1,3},{2,0},{3,1},{4,6},{5,7},{6,4},{7,5},{8,10},{9,11},{10,... | collective-permute-start | bytes 393224 | tf_op jit(solution)/shard_map/ppermute | solution.py:22
  88.7 7.4 %collective-permute-start.25 = (bf16[4,2,16,512]{3,2,1,0:T(8,128)(2,1)S(1)}, bf16[4,2,16,512]{3,2,1,0:T(8,128)(2,1)S(1)}, u32[]{:S(2)}, u32[]{:S(2)}) collective-permute-start(bf16[4,2,16,512]{3,2,1,0:T(8,128)(2,1)S(1)} %slice.105), channel_id=1, source_target_pairs={{0,2},{1,3},{2,0},{3,1},{4,6},{5,7},{6,4},{7,5},{8,10},{9,11},{10,... | collective-permute-start | bytes 393224 | tf_op jit(solution)/shard_map/ppermute | solution.py:22
  94.0 7.0 %collective-permute-start.29 = (bf16[4,1,16,512]{3,2,1,0:T(8,128)(2,1)S(1)}, bf16[4,1,16,512]{3,2,1,0:T(8,128)(2,1)S(1)}, u32[]{:S(2)}, u32[]{:S(2)}) collective-permute-start(bf16[4,1,16,512]{3,2,1,0:T(8,128)(2,1)S(1)} %get-tuple-element.79), channel_id=1, source_target_pairs={{0,4},{1,5},{2,6},{3,7},{4,0},{5,1},{6,2},{7,3},{8,12},{9,13},{10,... | collective-permute-start | bytes 196616 | tf_op jit(solution)/shard_map/ppermute | solution.py:22
  96.1 5.9 %collective-permute-start.26 = (bf16[4,1,16,512]{3,2,1,0:T(8,128)(2,1)S(1)}, bf16[4,1,16,512]{3,2,1,0:T(8,128)(2,1)S(1)}, u32[]{:S(2)}, u32[]{:S(2)}) collective-permute-start(bf16[4,1,16,512]{3,2,1,0:T(8,128)(2,1)S(1)} %get-tuple-element.81), channel_id=1, source_target_pairs={{0,4},{1,5},{2,6},{3,7},{4,0},{5,1},{6,2},{7,3},{8,12},{9,13},{10,... | collective-permute-start | bytes 196616 | tf_op jit(solution)/shard_map/ppermute | solution.py:22
  102.2 4.0 %collective-permute-start.30 = (bf16[16,1024]{1,0:T(8,128)(2,1)S(1)}, bf16[16,1024]{1,0:T(8,128)(2,1)S(1)}, u32[]{:S(2)}, u32[]{:S(2)}) collective-permute-start(bf16[16,1024]{1,0:T(8,128)(2,1)S(1)} %get-tuple-element.76), channel_id=1, source_target_pairs={{0,8},{8,0},{16,24},{24,16},{1,9},{9,1},{17,25},{25,17},{2,10},{10... | collective-permute-start | bytes 98312 | tf_op jit(solution)/shard_map/ppermute | solution.py:22
  103.8 3.9 %collective-permute-start.31 = (bf16[16,1024]{1,0:T(8,128)(2,1)S(1)}, bf16[16,1024]{1,0:T(8,128)(2,1)S(1)}, u32[]{:S(2)}, u32[]{:S(2)}) collective-permute-start(bf16[16,1024]{1,0:T(8,128)(2,1)S(1)} %get-tuple-element.77), channel_id=1, source_target_pairs={{0,16},{8,24},{16,0},{24,8},{1,17},{9,25},{17,1},{25,9},{2,18},{10... | collective-permute-start | bytes 98312 | tf_op jit(solution)/shard_map/ppermute | solution.py:22
  105.3 4.8 %collective-permute-start.32 = (bf16[16,1024]{1,0:T(8,128)(2,1)S(1)}, bf16[16,1024]{1,0:T(8,128)(2,1)S(1)}, u32[]{:S(2)}, u32[]{:S(2)}) collective-permute-start(bf16[16,1024]{1,0:T(8,128)(2,1)S(1)} %get-tuple-element.78), channel_id=1, source_target_pairs={{0,24},{8,16},{16,8},{24,0},{1,25},{9,17},{17,9},{25,1},{2,26},{10... | collective-permute-start | bytes 98312 | tf_op jit(solution)/shard_map/ppermute | solution.py:22
  (21 other events, 183.8 us)

commit v4 on v3

--- a/solution.py
+++ b/solution.py
@@ -10,6 +10,7 @@
 
 HEAD = 128
 MIB = 1024 * 1024
+WAIT = 8 * 10**9
 
 
 def rms_norm(values, gain):
@@ -115,29 +116,28 @@
     return rms_norm(values.astype(jnp.float32), gain).astype(jnp.bfloat16)
 
 
-def early_kernel(kept_ref, came_ref, gain_ref, out_ref):
-    for s in range(kept_ref.shape[0]):
-        out_ref[s, 0] = normed(kept_ref[s, 0], gain_ref[...])
-        out_ref[s, 1] = normed(came_ref[s, 0], gain_ref[...])
-
-
-def late_kernel(extra, kept_ref, came_ref, *refs):
-    gain_ref, raw_ref, out_ref = refs[-3:]
-    for s in range(extra):
-        raw_ref[s, 0] = refs[0][s + 1, 0]
-        raw_ref[s, 1] = refs[1][s + 1, 0]
-    for s in range(kept_ref.shape[0]):
-        for part, ref in enumerate((kept_ref, came_ref)):
-            raw_ref[extra + s, part] = ref[s, 0]
-            out_ref[s, part] = normed(ref[s, 0], gain_ref[...])
-
-
-def project_kernel(lead, kept_ref, came_ref, wq_ref, wk_ref, wv_ref, *refs):
+def stack_kernel(*refs):
+    for i, ref in enumerate(refs[:-1]):
+        refs[-1][i, 0] = ref[...]
+
+
+def join_kernel(kept_ref, came_ref, out_ref):
+    out_ref[:, :1] = kept_ref[...]
+    out_ref[:, 1:] = came_ref[...]
+
+
+def join(kept, came):
+    slots, _, rows, width = kept.shape
+    return kernel_call(join_kernel, "join", (kept, came), [bf16(slots, 2, rows, width)], flops=WAIT)[0]
+
+
+def project_kernel(lead, kept_ref, came_ref, gain_ref, wq_ref, wk_ref, wv_ref, *refs):
     old, (q_ref, k_ref, v_ref) = refs[: len(refs) - 3], refs[len(refs) - 3 :]
     slots, half, rows, width = kept_ref.shape
     group = half * rows
     tall = slots * group
     tokens = jnp.concatenate([kept_ref[...].reshape(tall, width), came_ref[...].reshape(tall, width)], 0)
+    tokens = normed(tokens, gain_ref[...])
     scale = math.log2(math.e) / math.sqrt(HEAD)
     base_q, base_kv = 0, 0
     if old:
@@ -165,7 +165,7 @@
     store(v_ref, jnp.dot(tokens, wv_ref[...], preferred_element_type=jnp.float32), 0, base_kv)
 
 
-def project(name, lead, kept, came, weights, old):
+def project(name, lead, kept, came, gain, weights, old):
     slots, half, rows, width = kept.shape
     wide = weights[0].shape[1]
     have_q = old[0].shape[0] if len(old) == 3 else 0
@@ -175,7 +175,7 @@
     return kernel_call(
         functools.partial(project_kernel, lead),
         name,
-        (kept, came, *weights, *old),
+        (kept, came, gain, *weights, *old),
         [shape(nq), shape(nkv), shape(nkv)],
         limit=32,
         flops=2 * 2 * half * rows * width * wide * (3 * slots - lead),
@@ -183,7 +183,43 @@
     )
 
 
-def attend_kernel(bits, query_rows, owners, meta, q_ref, k_ref, v_ref, wo_ref, raw_ref, *refs):
+def project_part_kernel(scale, rows_ref, gain_ref, wq_ref, wk_ref, wv_ref, *refs):
+    olds, outs = refs[:-3], refs[-3:]
+    slots, half, rows, width = rows_ref.shape
+    tokens = normed(rows_ref[...].reshape(slots * half * rows, width), gain_ref[...])
+    kept, ahead = olds[:3], (None,) * (6 - len(olds)) + olds[3:] if olds else ()
+    for i, (w_ref, out_ref) in enumerate(zip((wq_ref, wk_ref, wv_ref), outs)):
+        values = jnp.dot(tokens, w_ref[...], preferred_element_type=jnp.float32)
+        if i == 0:
+            values = values * scale
+        values = values.astype(jnp.bfloat16).reshape(slots, half, rows, values.shape[1])
+        if not olds:
+            out_ref[...] = values
+            continue
+        base = out_ref.shape[0] - slots
+        if base:
+            out_ref[:base] = ahead[i][...]
+        out_ref[base:, :half] = kept[i][...]
+        out_ref[base:, half:] = values
+
+
+def project_part(name, rows_in, gain, weights, kept=(), ahead=()):
+    slots, half, rows, width = rows_in.shape
+    wide = weights[0].shape[1]
+    bases = (0,) * (3 - len(ahead)) + tuple(a.shape[0] for a in ahead)
+    return kernel_call(
+        functools.partial(project_part_kernel, math.log2(math.e) / math.sqrt(HEAD)),
+        name,
+        (rows_in, gain, *weights, *kept, *ahead),
+        [bf16(base + slots, half * (2 if kept else 1), rows, wide) for base in bases],
+        limit=24,
+        flops=6 * slots * half * rows * width * wide,
+        moved=6 * width * wide,
+    )
+
+
+def attend_kernel(bits, query_rows, owners, others, direct, meta, q_ref, k_ref, v_ref, wo_ref, late_ref, *refs):
+    early_ref, refs = (refs[0], refs[1:]) if direct else (None, refs)
     out_ref, rest_ref, mine_ref, role_ref, valid_ref, home_ref, ctx_ref, expo_ref = refs
     _, blocks, rows, width = q_ref.shape
     pairs = meta.shape[0] - 1
@@ -194,7 +230,12 @@
     for p in range(pairs):
         for role in range(2):
             slot = meta[p, 1 + role]
-            mine_ref[p, role] = raw_ref[slot]
+            for part, at in enumerate((0, others[p])):
+                if direct:
+                    chosen = late_ref[jnp.maximum(slot - 1, 0), at]
+                    mine_ref[p, role, part] = jnp.where(slot == 0, early_ref[1, at], chosen)
+                else:
+                    mine_ref[p, role, part] = late_ref[slot, at]
             for s in range(slots):
                 role_ref[2 * p + role, s] = flag(slot == s)
                 lengths[s] = jnp.where(slot == s, meta[p, 3 + role], lengths[s])
@@ -251,19 +292,20 @@
         rest_ref[...] = ctx_ref[begin:]
 
 
-def attend(lead, bits, query_rows, doc_count, owners, meta, q, k, v, w_output, raw):
+def attend(groups, swapped, bits, query_rows, doc_count, owners, meta, q, k, v, w_output, late, early):
     _, blocks, rows, width = q.shape
-    pairs, model, slots = meta.shape[0] - 1, w_output.shape[1], raw.shape[0]
+    pairs, model, slots, lead = meta.shape[0] - 1, w_output.shape[1], q.shape[0], groups[0]
+    others = [late.shape[1] // 2 if far else 1 for n, far in zip(groups, swapped) for _ in range(n)]
     f32 = lambda *shape: jax.ShapeDtypeStruct(shape, jnp.float32)
     tall = 2 * blocks * rows
     return kernel_call(
-        functools.partial(attend_kernel, bits, query_rows, owners),
+        functools.partial(attend_kernel, bits, query_rows, owners, others, early is not None),
         "attend",
-        (meta, q, k, v, w_output, raw),
+        (meta, q, k, v, w_output, late) + (() if early is None else (early,)),
         [
             bf16(2 * lead, blocks, rows, model),
             bf16(max(pairs - lead, 1) * tall, width),
-            bf16(pairs, 2, *raw.shape[1:]),
+            bf16(pairs, 2, 2, *late.shape[2:]),
             f32(2 * pairs, slots, 8, 128),
             f32(slots, rows, 128),
             f32(doc_count, owners, 8, 128),
@@ -279,12 +321,24 @@
     )
 
 
-def output_kernel(groups, ctx_ref, wo_ref, *out_refs):
+def turned(blocks):
+    bits = blocks.bit_length() - 1
+    return [sum(((b >> i) & 1) << (bits - 1 - i) for i in range(bits)) for b in range(blocks)]
+
+
+def output_kernel(groups, swapped, ctx_ref, wo_ref, *out_refs):
     product = jnp.dot(ctx_ref[...], wo_ref[...], preferred_element_type=jnp.float32).astype(jnp.bfloat16)
     tall = ctx_ref.shape[0] // sum(groups)
     for i, out_ref in enumerate(out_refs):
         begin = sum(groups[:i])
-        out_ref[...] = product[begin * tall : (begin + groups[i]) * tall].reshape(out_ref.shape)
+        values = product[begin * tall : (begin + groups[i]) * tall].reshape(out_ref.shape)
+        if not swapped[i]:
+            out_ref[...] = values
+            continue
+        half = out_ref.shape[1] // 2
+        for b, to in enumerate(turned(half)):
+            out_ref[:, to] = values[:, b]
+            out_ref[:, half + to] = values[:, half + b]
 
 
 def settle_kernel(pair, kept_ref, came_ref, mine_ref, gain_ref, hidden_ref, ffn_ref):
@@ -307,71 +361,75 @@
     )
 
 
-def expand_kernel(pairs, tile, meta, w_ref, *refs):
-    pieces, out_ref = refs[:-1], refs[-1]
+def expand_kernel(swapped, tile, meta, w_ref, *refs):
+    pieces, rest = refs[: len(swapped)], refs[len(swapped) :]
+    old_ref, out_ref = (rest[0] if len(rest) == 2 else None), rest[-1]
     _, half, rows, width = pieces[0].shape
     group = half * rows
-    tokens = jnp.concatenate(
-        [
-            pieces[i + part][role].reshape(group, width)
-            for i in range(0, len(pieces), 2)
-            for role in range(pieces[i].shape[0])
-            for part in range(2)
-        ],
-        0,
-    )
+    tokens = []
+    for piece, far in zip(pieces, swapped):
+        for r in range(piece.shape[0]):
+            if far:
+                tokens += [piece[r, b] for b in turned(half)]
+            else:
+                tokens.append(piece[r].reshape(group, width))
+    tokens = jnp.concatenate(tokens, 0)
+    last = out_ref.shape[0] - 1
 
     def step(i, carry):
         at = pl.ds(pl.multiple_of(i * tile, tile), tile)
         units = jnp.maximum(jnp.dot(tokens, w_ref[:, at], preferred_element_type=jnp.float32), 0.0)
         units = units.astype(jnp.bfloat16)
-        out_ref[:, :, at] = jnp.zeros((out_ref.shape[0], 2 * group, tile), jnp.bfloat16)
-        for r in range(2 * pairs):
+        if old_ref is not None:
+            out_ref[0, :, :, at] = old_ref[0, :, :, at]
+        out_ref[last, :, :, at] = jnp.zeros((out_ref.shape[1], group, tile), jnp.bfloat16)
+        for r in range(tokens.shape[0] // group):
             slot = meta[r // 2, 1 + r % 2]
-            out_ref[slot, :, at] = out_ref[slot, :, at] + units[r * 2 * group : (r + 1) * 2 * group]
+            out_ref[last, slot, :, at] = out_ref[last, slot, :, at] + units[r * group : (r + 1) * group]
         return carry
 
     lax.fori_loop(0, w_ref.shape[1] // tile, step, 0, unroll=2)
 
 
-def expand(meta, pieces, w_in, slots):
+def expand(meta, swapped, pieces, w_in, slots, old=()):
     _, half, rows, width = pieces[0].shape
     units = w_in.shape[1]
-    pairs = sum(piece.shape[0] for piece in pieces) // 4
+    roles = sum(piece.shape[0] for piece in pieces)
     return kernel_call(
-        functools.partial(expand_kernel, pairs, min(512, units)),
+        functools.partial(expand_kernel, swapped, min(512, units)),
         "expand",
-        (meta, w_in, *pieces),
-        [bf16(slots, 2 * half * rows, units)],
+        (meta, w_in, *pieces, *old),
+        [bf16(1 + len(old), slots, half * rows, units)],
         smem=(0,),
         limit=24,
-        flops=2 * pairs * 4 * half * rows * width * units,
+        flops=2 * roles * half * rows * width * units,
         moved=2 * width * units,
-    )[0]
-
-
-def shrink_kernel(low, high, begin, units_ref, w_ref, out_ref):
-    _, tall, depth = units_ref.shape
-    step = out_ref.shape[-1]
+    )
+
+
+def shrink_kernel(begin, units_ref, w_ref, out_ref):
+    parts, slots, tall, depth = units_ref.shape
+    _, blocks, rows, step = out_ref.shape
     product = jnp.dot(
-        units_ref[low:high].reshape((high - low) * tall, depth),
+        units_ref[...].reshape(parts * slots * tall, depth),
         w_ref[:, begin : begin + step],
         preferred_element_type=jnp.float32,
     )
-    out_ref[...] = product.astype(jnp.bfloat16).reshape(out_ref.shape)
-
-
-def shrink(low, high, begin, step, units, w_down, blocks, after):
-    _, tall, depth = units.shape
+    product = product.astype(jnp.bfloat16).reshape(parts, slots, blocks // parts, rows, step)
+    for part in range(parts):
+        out_ref[:, part * (blocks // parts) : (part + 1) * (blocks // parts)] = product[part]
+
+
+def shrink(begin, step, units, w_down, blocks):
+    parts, slots, tall, depth = units.shape
     return kernel_call(
-        functools.partial(shrink_kernel, low, high, begin),
+        functools.partial(shrink_kernel, begin),
         "shrink",
         (units, w_down),
-        [bf16(high - low, blocks, tall // blocks, step)],
+        [bf16(slots, blocks, parts * tall // blocks, step)],
         limit=24,
-        flops=2 * (high - low) * tall * depth * step,
+        flops=2 * parts * slots * tall * depth * step,
         moved=2 * depth * step,
-        after=after,
     )[0]
 
 
@@ -453,7 +511,7 @@
         hbm=(0, 1, 2, 3, 4),
         out_smem=(0,),
         limit=63,
-        flops=8 * 10**9,
+        flops=WAIT,
     )
     arrived = [block if k == 0 else swap(block, k, "pair") for k, block in enumerate(arrived)]
     if not direct:
@@ -467,39 +525,34 @@
         table = (other[:slots, None] == place[None, :]).astype(jnp.bfloat16)
         packed = jnp.einsum("sk,krd->srd", table, jnp.stack(arrived), preferred_element_type=jnp.float32)
         arrived = [packed[s].astype(jnp.bfloat16) for s in range(slots)]
-    top = up_bits[0]
-    pairwise = lambda a: bf16(a.shape[0], 2, doc_rows, width)
-    early_came = swap(early, top, "tensor")
-    early_norm = kernel_call(early_kernel, "early", (early, early_came, attn_gain), [pairwise(early)], flops=8 * 10**9)[0]
-    late = jnp.stack(arrived[direct:])[:, None]
-    late, early_norm = tie(late, early_norm)
-    late_came = swap(late, top, "tensor")
-    more = (early, early_came) if direct else ()
-    rows_own, late_norm = kernel_call(
-        functools.partial(late_kernel, int(direct)),
-        "late",
-        (late, late_came, *more, attn_gain),
-        [bf16(slots, 2, doc_rows, width), pairwise(late)],
-        flops=8 * 10**9,
-    )
-
     def spread(kept):
         return kept, swap(kept, up_bits[-1], "tensor")
 
-    early_kept = gather_blocks(early_norm, up_bits[1:-1])
-    first = project("project_early", 1, *spread(early_kept), weights, ())
-    late_kept = gather_blocks(late_norm, up_bits[1:-1])
-    late_kept, first = tie(late_kept, first)
-    q, k, v = project("project_late", 0, *spread(late_kept), weights, first if direct else first[1:])
+    top = up_bits[0]
+    early = join(early, swap(early, top, "tensor"))
+    late = kernel_call(
+        stack_kernel, "stack", arrived[direct:], [bf16(slots - direct, 1, doc_rows, width)], flops=WAIT
+    )[0]
+    late, early = tie(late, early)
+    early = gather_blocks(early, up_bits[1:-1])
+    first = project("project_early", 1, *spread(early), attn_gain, weights, ())
+    late = gather_blocks(join(late, swap(late, top, "tensor")), up_bits[1:-1])
+    late, first = tie(late, first)
+    late, late_other = spread(late)
+    half_done = project_part("project_kept", late, attn_gain, weights)
+    q, k, v = project_part(
+        "project_came", late_other, attn_gain, weights, tuple(half_done), tuple(first if direct else first[1:])
+    )
 
     groups = [1] * pairs
+    swapped = [len(groups) > 1 and g == len(groups) - 1 for g in range(len(groups))]
     part, rest, mine, roles, valid, homes = attend(
-        groups[0], up_bits, query_rows, doc_count, owners, meta, q, k, v, w_output, rows_own
+        groups, swapped, up_bits, query_rows, doc_count, owners, meta, q, k, v, w_output, late, early if direct else None
     )
     parts = [part]
     if groups[1:]:
         parts += kernel_call(
-            functools.partial(output_kernel, groups[1:]),
+            functools.partial(output_kernel, groups[1:], swapped[1:]),
             "output",
             (rest, w_output),
             [bf16(2 * n, *part.shape[1:]) for n in groups[1:]],
@@ -508,37 +561,34 @@
         )
     hidden, pieces = [], []
     for group, part in enumerate(parts):
-        for bit in down_bits[:-1]:
+        order = down_bits[:1] + (down_bits[:0:-1] if swapped[group] else down_bits[1:])
+        for bit in order[:-1]:
             kept, came = halve(part, bit)
             part = kept + came
-        came = swap(part, down_bits[-1], "tensor")
+        came = swap(part, order[-1], "tensor")
         own, ffn = settle(sum(groups[:group]), part, came, mine, ffn_gain)
         hidden.append(own)
-        pieces += spread(gather_blocks(ffn, up_bits[1:-1]))
-    units = expand(meta, pieces, w_in, slots)
+        pieces += spread(gather_blocks(ffn, order[1:-1][::-1]))
+    units = expand(meta, swapped, pieces[::2], w_in, slots)
+    units = expand(meta, swapped, pieces[1::2], w_in, slots, tuple(units))[0]
     hidden = jnp.concatenate(hidden, 0)
 
-    def shrunk(low, high, columns, after=()):
-        step = width // columns
-        return [shrink(low, high, c * step, step, units, w_down, slices, after) for c in range(columns)]
-
-    def reduce(parts, low, high):
-        columns = len(parts)
-        pieces = []
-        for part in parts:
-            for bit in down_bits:
-                kept, came = halve(part, bit)
-                if bit != down_bits[-1]:
-                    part = kept + came
-            pieces += [kept, came]
-        return kernel_call(
-            functools.partial(finish_kernel, low, columns),
-            "finish",
-            (roles, valid, hidden, *pieces),
-            [bf16(doc_rows, width)] * (high - low),
-        )
-
-    blocks = reduce(shrunk(0, slots, 2), 0, slots)
+    columns = 2
+    step = width // columns
+    pieces = []
+    for c in range(columns):
+        part = shrink(c * step, step, units, w_down, slices)
+        for bit in down_bits:
+            kept, came = halve(part, bit)
+            if bit != down_bits[-1]:
+                part = kept + came
+        pieces += [kept, came]
+    blocks = kernel_call(
+        functools.partial(finish_kernel, 0, columns),
+        "finish",
+        (roles, valid, hidden, *pieces),
+        [bf16(doc_rows, width)] * slots,
+    )
     if not direct:
         packed = jnp.einsum("sk,srd->krd", table, jnp.stack(blocks), preferred_element_type=jnp.float32)
         blocks = [packed[s].astype(jnp.bfloat16) for s in range(owners)]

time: 111 us -> 105 us (0.946)
  waiting for transfers between devices: 36.2 us -> 24.5 us
  starting transfers between devices: 45.9 us -> 50.8 us
  Pallas kernels: 26.9 us -> 28.9 us
    ppermute x33, waiting for transfers between devices: 36.2 us -> 24.5 us  [swap(): return lax.ppermute(values, axis, [(i, i ^ bit) for i in range(count)])]
    ppermute x33, starting transfers between devices: 45.9 us -> 50.8 us  [swap(): return lax.ppermute(values, axis, [(i, i ^ bit) for i in range(count)])]
    pallas_call x15 -> x18, Pallas kernels: 26.9 us -> 28.9 us  [kernel_call(): pl.pallas_call(kernel, out_shape=out_shape, in_specs=[space(i in smem, i...]
  transfers between devices with their start and end apart: 33 -> 33, of which waited for: 22 -> 17; matrix products, arithmetic and copies ran while one was open for 0% -> 1% of each run, Pallas kernels for 4% -> 10%
where the time goes in v4:
time: 105 us
  starting transfers between devices  50.8 us (48%)
  Pallas kernels  28.9 us (28%)
  waiting for transfers between devices  24.5 us (23%)
    ppermute x33, starting transfers between devices, swap(): return lax.ppermute(values, axis, [(i, i ^ bit) for i in range(count)])  50.8 us
    pallas_call x18, Pallas kernels, kernel_call(): pl.pallas_call(kernel, out_shape=out_shape, in_specs=[space(i in smem, i...  28.9 us
    ppermute x33, waiting for transfers between devices, swap(): return lax.ppermute(values, axis, [(i, i ^ bit) for i in range(count)])  24.5 us
  transfers between devices with their start and end apart: 33, of which 17 were waited for; matrix products, arithmetic and copies ran while one was open for 1% of the time, Pallas kernels for 10%

profile of v4, /device:TPU:0, one launch (start us, length us, event | category | flops | bytes accessed | tf_op | source)
XLA Modules:
  0.0 105.3 jit_solution(8502362614755764687)
XLA Ops:
  1.7 3.0 %collective-permute-start = (bf16[16,1024]{1,0:T(8,128)(2,1)}, bf16[16,1024]{1,0:T(8,128)(2,1)S(1)}, u32[]{:S(2)}, u32[]{:S(2)}) collective-permute-start(bf16[16,1024]{1,0:T(8,128)(2,1)} %get-tuple-element.44), channel_id=1, source_target_pairs={{0,8},{8,0},{16,24},{24,16},{1,9},{9,1},{17,25},{25,17},{2,10},{10... | collective-permute-start | bytes 98312 | tf_op jit(solution)/shard_map/ppermute | solution.py:23
  6.2 3.0 %collective-permute-start.3 = (bf16[2,1,16,1024]{3,2,1,0:T(8,128)(2,1)}, bf16[2,1,16,1024]{3,2,1,0:T(8,128)(2,1)S(1)}, u32[]{:S(2)}, u32[]{:S(2)}) collective-permute-start(bf16[2,1,16,1024]{3,2,1,0:T(8,128)(2,1)} %get-tuple-element.47.kept_ref), channel_id=1, source_target_pairs={{0,4},{1,5},{2,6},{3,7},{4,0},{5,1},{6,2},{7,3},{8,12},{9,13},{10,... | collective-permute-start | bytes 196616 | tf_op jit(solution)/shard_map/ppermute | solution.py:23
  9.3 1.9 %collective-permute-done.2.refs_2_ = bf16[16,1024]{1,0:T(8,128)(2,1)S(1)} collective-permute-done((bf16[16,1024]{1,0:T(8,128)(2,1)}, bf16[16,1024]{1,0:T(8,128)(2,1)S(1)}, u32[]{:S(2)}, u32[]{:S(2)}) %collective-permute-start.2) | collective-permute-done | bytes 32800 | tf_op jit(solution)/shard_map/ppermute | solution.py:23
  11.8 3.0 %collective-permute-start.4 = (bf16[3,1,16,1024]{3,2,1,0:T(8,128)(2,1)S(1)}, bf16[3,1,16,1024]{3,2,1,0:T(8,128)(2,1)S(1)}, u32[]{:S(2)}, u32[]{:S(2)}) collective-permute-start(bf16[3,1,16,1024]{3,2,1,0:T(8,128)(2,1)S(1)} %stack.1.kept_ref), channel_id=1, source_target_pairs={{0,4},{1,5},{2,6},{3,7},{4,0},{5,1},{6,2},{7,3},{8,12},{9,13},{10,... | collective-permute-start | bytes 294920 | tf_op jit(solution)/shard_map/ppermute | solution.py:23
  14.8 2.1 %collective-permute-start.6 = (bf16[2,2,16,1024]{3,2,1,0:T(8,128)(2,1)S(1)}, bf16[2,2,16,1024]{3,2,1,0:T(8,128)(2,1)S(1)}, u32[]{:S(2)}, u32[]{:S(2)}) collective-permute-start(bf16[2,2,16,1024]{3,2,1,0:T(8,128)(2,1)S(1)} %join.2), channel_id=1, source_target_pairs={{0,2},{1,3},{2,0},{3,1},{4,6},{5,7},{6,4},{7,5},{8,10},{9,11},{10,... | collective-permute-start | bytes 393224 | tf_op jit(solution)/shard_map/ppermute | solution.py:23
  17.5 2.1 %collective-permute-start.5 = (bf16[3,2,16,1024]{3,2,1,0:T(8,128)(2,1)S(1)}, bf16[3,2,16,1024]{3,2,1,0:T(8,128)(2,1)S(1)}, u32[]{:S(2)}, u32[]{:S(2)}) collective-permute-start(bf16[3,2,16,1024]{3,2,1,0:T(8,128)(2,1)S(1)} %join.3), channel_id=1, source_target_pairs={{0,2},{1,3},{2,0},{3,1},{4,6},{5,7},{6,4},{7,5},{8,10},{9,11},{10,... | collective-permute-start | bytes 589832 | tf_op jit(solution)/shard_map/ppermute | solution.py:23
  21.4 2.0 %collective-permute-done.5 = bf16[3,2,16,1024]{3,2,1,0:T(8,128)(2,1)S(1)} collective-permute-done((bf16[3,2,16,1024]{3,2,1,0:T(8,128)(2,1)S(1)}, bf16[3,2,16,1024]{3,2,1,0:T(8,128)(2,1)S(1)}, u32[]{:S(2)}, u32[]{:S(2)}) %collective-permute-start.5) | collective-permute-done | bytes 196640 | tf_op jit(solution)/shard_map/ppermute | solution.py:23
  28.5 5.7 %attend.1 = (bf16[2,8,16,1024]{3,2,1,0:T(8,128)(2,1)S(1)}, bf16[512,1024]{1,0:T(8,128)(2,1)S(1)}, bf16[3,2,2,16,1024]{4,3,2,1,0:T(8,128)(2,1)S(1)}, f32[6,4,8,12...) custom-call(s32[4,6]{1,0:T(4,128)S(1)} %copy-done.5, ...), custom_call_target="tpu_custom_call" | custom-call | flops 1744830464 | bytes 2097152 | tf_op jit(solution)/shard_map/attend/pallas_call | solution.py:54
  36.7 2.0 %collective-permute-start.10 = (bf16[2,2,16,1024]{3,2,1,0:T(8,128)(2,1)S(1)}, bf16[2,2,16,1024]{3,2,1,0:T(8,128)(2,1)S(1)}, u32[]{:S(2)}, u32[]{:S(2)}) collective-permute-start(bf16[2,2,16,1024]{3,2,1,0:T(8,128)(2,1)S(1)} %slice.97), channel_id=1, source_target_pairs={{0,2},{1,3},{2,0},{3,1},{4,6},{5,7},{6,4},{7,5},{8,10},{9,11},{10,... | collective-permute-start | bytes 393224 | tf_op jit(solution)/shard_map/ppermute | solution.py:23
  38.8 3.5 %collective-permute-start.16 = (bf16[2,2,16,1024]{3,2,1,0:T(8,128)(2,1)S(1)}, bf16[2,2,16,1024]{3,2,1,0:T(8,128)(2,1)S(1)}, u32[]{:S(2)}, u32[]{:S(2)}) collective-permute-start(bf16[2,2,16,1024]{3,2,1,0:T(8,128)(2,1)S(1)} %slice.101), channel_id=1, source_target_pairs={{0,4},{1,5},{2,6},{3,7},{4,0},{5,1},{6,2},{7,3},{8,12},{9,13},{10,... | collective-permute-start | bytes 393224 | tf_op jit(solution)/shard_map/ppermute | solution.py:23
  43.2 3.3 %collective-permute-start.11 = (bf16[2,2,16,1024]{3,2,1,0:T(8,128)(2,1)S(1)}, bf16[2,2,16,1024]{3,2,1,0:T(8,128)(2,1)S(1)}, u32[]{:S(2)}, u32[]{:S(2)}) collective-permute-start(bf16[2,2,16,1024]{3,2,1,0:T(8,128)(2,1)S(1)} %slice_add_fusion.9.kept_ref), channel_id=1, source_target_pairs={{0,4},{1,5},{2,6},{3,7},{4,0},{5,1},{6,2},{7,3},{8,12},{9,13},{10,... | collective-permute-start | bytes 393224 | tf_op jit(solution)/shard_map/ppermute | solution.py:23
  46.6 2.3 %collective-permute-done.16 = bf16[2,2,16,1024]{3,2,1,0:T(8,128)(2,1)S(1)} collective-permute-done((bf16[2,2,16,1024]{3,2,1,0:T(8,128)(2,1)S(1)}, bf16[2,2,16,1024]{3,2,1,0:T(8,128)(2,1)S(1)}, u32[]{:S(2)}, u32[]{:S(2)}) %collective-permute-start.16) | collective-permute-done | bytes 131104 | tf_op jit(solution)/shard_map/ppermute | solution.py:23
  50.1 3.9 %collective-permute-start.14 = (bf16[2,2,16,1024]{3,2,1,0:T(8,128)(2,1)S(1)}, bf16[2,2,16,1024]{3,2,1,0:T(8,128)(2,1)S(1)}, u32[]{:S(2)}, u32[]{:S(2)}) collective-permute-start(bf16[2,2,16,1024]{3,2,1,0:T(8,128)(2,1)S(1)} %slice_add_fusion.8.kept_ref), channel_id=1, source_target_pairs={{0,4},{1,5},{2,6},{3,7},{4,0},{5,1},{6,2},{7,3},{8,12},{9,13},{10,... | collective-permute-start | bytes 393224 | tf_op jit(solution)/shard_map/ppermute | solution.py:23
  56.0 3.9 %collective-permute-start.22 = (bf16[2,2,16,1024]{3,2,1,0:T(8,128)(2,1)S(1)}, bf16[2,2,16,1024]{3,2,1,0:T(8,128)(2,1)S(1)}, u32[]{:S(2)}, u32[]{:S(2)}) collective-permute-start(bf16[2,2,16,1024]{3,2,1,0:T(8,128)(2,1)S(1)} %get-tuple-element.76), channel_id=1, source_target_pairs={{0,4},{1,5},{2,6},{3,7},{4,0},{5,1},{6,2},{7,3},{8,12},{9,13},{10,... | collective-permute-start | bytes 393224 | tf_op jit(solution)/shard_map/ppermute | solution.py:23
  62.5 2.2 %collective-permute-done.22 = bf16[2,2,16,1024]{3,2,1,0:T(8,128)(2,1)S(1)} collective-permute-done((bf16[2,2,16,1024]{3,2,1,0:T(8,128)(2,1)S(1)}, bf16[2,2,16,1024]{3,2,1,0:T(8,128)(2,1)S(1)}, u32[]{:S(2)}, u32[]{:S(2)}) %collective-permute-start.22) | collective-permute-done | bytes 131104 | tf_op jit(solution)/shard_map/ppermute | solution.py:23
  66.1 4.6 %expand.2.refs_3_ = bf16[1,4,64,4096]{3,2,1,0:T(8,128)(2,1)S(1)} custom-call(s32[4,6]{1,0:T(4,128)S(1)} %copy-done.5, bf16[1024,4096]{1,0:T(8,128)(2,1)S(1)} %bitcast.5, bf16[2,4,16,1024]{3,2,1,0:T(8,128)(2,1)S(1)} %constant_dynamic-update-slice_fusion.2.refs_0_, bf16[2,4,16,1024]{3,2,1,0:T(8,128)(2,1)S(1)} %constant_dynamic-update-slice_fusion.4.refs_1_, ...), custom_call_target="tpu_custom_call" | custom-call | flops 3221225472 | bytes 8388608 | tf_op jit(solution)/shard_map/expand/pallas_call | solution.py:54
  70.7 4.8 %expand.3.units_ref = bf16[2,4,64,4096]{3,2,1,0:T(8,128)(2,1)S(1)} custom-call(s32[4,6]{1,0:T(4,128)S(1)} %copy-done.5, bf16[1024,4096]{1,0:T(8,128)(2,1)S(1)} %bitcast.5, bf16[2,4,16,1024]{3,2,1,0:T(8,128)(2,1)S(1)} %collective-permute-done.19.refs_0_, bf16[2,4,16,1024]{3,2,1,0:T(8,128)(2,1)S(1)} %collective-permute-done.21.refs_1_, ...), custom_call_target="tpu_custom_call" | custom-call | flops 3221225472 | bytes 8388608 | tf_op jit(solution)/shard_map/expand/pallas_call | solution.py:54
  75.6 2.3 %shrink.3 = bf16[4,8,16,512]{3,2,1,0:T(8,128)(2,1)S(1)} custom-call(bf16[2,4,64,4096]{3,2,1,0:T(8,128)(2,1)S(1)} %expand.3.units_ref, bf16[4096,1024]{1,0:T(8,128)(2,1)S(1)} %bitcast.3), custom_call_target="tpu_custom_call" | custom-call | flops 2147483648 | bytes 4194304 | tf_op jit(solution)/shard_map/shrink/pallas_call | solution.py:54
  78.5 2.3 %shrink.2 = bf16[4,8,16,512]{3,2,1,0:T(8,128)(2,1)S(1)} custom-call(bf16[2,4,64,4096]{3,2,1,0:T(8,128)(2,1)S(1)} %expand.3.units_ref, bf16[4096,1024]{1,0:T(8,128)(2,1)S(1)} %bitcast.3), custom_call_target="tpu_custom_call" | custom-call | flops 2147483648 | bytes 4194304 | tf_op jit(solution)/shard_map/shrink/pallas_call | solution.py:54
  83.9 3.4 %collective-permute-done.28 = bf16[4,2,16,512]{3,2,1,0:T(8,128)(2,1)S(1)} collective-permute-done((bf16[4,2,16,512]{3,2,1,0:T(8,128)(2,1)S(1)}, bf16[4,2,16,512]{3,2,1,0:T(8,128)(2,1)S(1)}, u32[]{:S(2)}, u32[]{:S(2)}) %collective-permute-start.28) | collective-permute-done | bytes 131104 | tf_op jit(solution)/shard_map/ppermute | solution.py:23
  87.4 3.3 %collective-permute-start.29 = (bf16[4,1,16,512]{3,2,1,0:T(8,128)(2,1)S(1)}, bf16[4,1,16,512]{3,2,1,0:T(8,128)(2,1)S(1)}, u32[]{:S(2)}, u32[]{:S(2)}) collective-permute-start(bf16[4,1,16,512]{3,2,1,0:T(8,128)(2,1)S(1)} %get-tuple-element.81), channel_id=1, source_target_pairs={{0,4},{1,5},{2,6},{3,7},{4,0},{5,1},{6,2},{7,3},{8,12},{9,13},{10,... | collective-permute-start | bytes 196616 | tf_op jit(solution)/shard_map/ppermute | solution.py:23
  90.8 2.8 %collective-permute-start.26 = (bf16[4,1,16,512]{3,2,1,0:T(8,128)(2,1)S(1)}, bf16[4,1,16,512]{3,2,1,0:T(8,128)(2,1)S(1)}, u32[]{:S(2)}, u32[]{:S(2)}) collective-permute-start(bf16[4,1,16,512]{3,2,1,0:T(8,128)(2,1)S(1)} %get-tuple-element.83), channel_id=1, source_target_pairs={{0,4},{1,5},{2,6},{3,7},{4,0},{5,1},{6,2},{7,3},{8,12},{9,13},{10,... | collective-permute-start | bytes 196616 | tf_op jit(solution)/shard_map/ppermute | solution.py:23
  94.4 2.1 %collective-permute-done.26.refs_1_ = bf16[4,1,16,512]{3,2,1,0:T(8,128)(2,1)S(1)} collective-permute-done((bf16[4,1,16,512]{3,2,1,0:T(8,128)(2,1)S(1)}, bf16[4,1,16,512]{3,2,1,0:T(8,128)(2,1)S(1)}, u32[]{:S(2)}, u32[]{:S(2)}) %collective-permute-start.26) | collective-permute-done | bytes 65568 | tf_op jit(solution)/shard_map/ppermute | solution.py:23
  102.2 2.4 %collective-permute-done.32.refs_3_ = bf16[16,1024]{1,0:T(8,128)(2,1)S(1)} collective-permute-done((bf16[16,1024]{1,0:T(8,128)(2,1)S(1)}, bf16[16,1024]{1,0:T(8,128)(2,1)S(1)}, u32[]{:S(2)}, u32[]{:S(2)}) %collective-permute-start.32) | collective-permute-done | bytes 32800 | tf_op jit(solution)/shard_map/ppermute | solution.py:23
  (118 shorter events, 32.6 us)
Async XLA Ops:
  1.7 7.6 %collective-permute-start = (bf16[16,1024]{1,0:T(8,128)(2,1)}, bf16[16,1024]{1,0:T(8,128)(2,1)S(1)}, u32[]{:S(2)}, u32[]{:S(2)}) collective-permute-start(bf16[16,1024]{1,0:T(8,128)(2,1)} %get-tuple-element.44), channel_id=1, source_target_pairs={{0,8},{8,0},{16,24},{24,16},{1,9},{9,1},{17,25},{25,17},{2,10},{10... | collective-permute-start | bytes 98312 | tf_op jit(solution)/shard_map/ppermute | solution.py:23
  6.2 5.0 %collective-permute-start.2 = (bf16[16,1024]{1,0:T(8,128)(2,1)}, bf16[16,1024]{1,0:T(8,128)(2,1)S(1)}, u32[]{:S(2)}, u32[]{:S(2)}) collective-permute-start(bf16[16,1024]{1,0:T(8,128)(2,1)} %get-tuple-element.46), channel_id=1, source_target_pairs={{0,24},{8,16},{16,8},{24,0},{1,25},{9,17},{17,9},{25,1},{2,26},{10... | collective-permute-start | bytes 98312 | tf_op jit(solution)/shard_map/ppermute | solution.py:23
  6.2 5.6 %collective-permute-start.3 = (bf16[2,1,16,1024]{3,2,1,0:T(8,128)(2,1)}, bf16[2,1,16,1024]{3,2,1,0:T(8,128)(2,1)S(1)}, u32[]{:S(2)}, u32[]{:S(2)}) collective-permute-start(bf16[2,1,16,1024]{3,2,1,0:T(8,128)(2,1)} %get-tuple-element.47.kept_ref), channel_id=1, source_target_pairs={{0,4},{1,5},{2,6},{3,7},{4,0},{5,1},{6,2},{7,3},{8,12},{9,13},{10,... | collective-permute-start | bytes 196616 | tf_op jit(solution)/shard_map/ppermute | solution.py:23
  11.8 5.7 %collective-permute-start.4 = (bf16[3,1,16,1024]{3,2,1,0:T(8,128)(2,1)S(1)}, bf16[3,1,16,1024]{3,2,1,0:T(8,128)(2,1)S(1)}, u32[]{:S(2)}, u32[]{:S(2)}) collective-permute-start(bf16[3,1,16,1024]{3,2,1,0:T(8,128)(2,1)S(1)} %stack.1.kept_ref), channel_id=1, source_target_pairs={{0,4},{1,5},{2,6},{3,7},{4,0},{5,1},{6,2},{7,3},{8,12},{9,13},{10,... | collective-permute-start | bytes 294920 | tf_op jit(solution)/shard_map/ppermute | solution.py:23
  14.8 6.5 %collective-permute-start.6 = (bf16[2,2,16,1024]{3,2,1,0:T(8,128)(2,1)S(1)}, bf16[2,2,16,1024]{3,2,1,0:T(8,128)(2,1)S(1)}, u32[]{:S(2)}, u32[]{:S(2)}) collective-permute-start(bf16[2,2,16,1024]{3,2,1,0:T(8,128)(2,1)S(1)} %join.2), channel_id=1, source_target_pairs={{0,2},{1,3},{2,0},{3,1},{4,6},{5,7},{6,4},{7,5},{8,10},{9,11},{10,... | collective-permute-start | bytes 393224 | tf_op jit(solution)/shard_map/ppermute | solution.py:23
  17.5 5.8 %collective-permute-start.5 = (bf16[3,2,16,1024]{3,2,1,0:T(8,128)(2,1)S(1)}, bf16[3,2,16,1024]{3,2,1,0:T(8,128)(2,1)S(1)}, u32[]{:S(2)}, u32[]{:S(2)}) collective-permute-start(bf16[3,2,16,1024]{3,2,1,0:T(8,128)(2,1)S(1)} %join.3), channel_id=1, source_target_pairs={{0,2},{1,3},{2,0},{3,1},{4,6},{5,7},{6,4},{7,5},{8,10},{9,11},{10,... | collective-permute-start | bytes 589832 | tf_op jit(solution)/shard_map/ppermute | solution.py:23
  36.3 6.0 %collective-permute-start.12 = (bf16[2,4,16,1024]{3,2,1,0:T(8,128)(2,1)S(1)}, bf16[2,4,16,1024]{3,2,1,0:T(8,128)(2,1)S(1)}, u32[]{:S(2)}, u32[]{:S(2)}) collective-permute-start(bf16[2,4,16,1024]{3,2,1,0:T(8,128)(2,1)S(1)} %slice.77), channel_id=1, source_target_pairs={{0,1},{1,0},{2,3},{3,2},{4,5},{5,4},{6,7},{7,6},{8,9},{9,8},{10,11... | collective-permute-start | bytes 786440 | tf_op jit(solution)/shard_map/ppermute | solution.py:23
  36.7 6.5 %collective-permute-start.10 = (bf16[2,2,16,1024]{3,2,1,0:T(8,128)(2,1)S(1)}, bf16[2,2,16,1024]{3,2,1,0:T(8,128)(2,1)S(1)}, u32[]{:S(2)}, u32[]{:S(2)}) collective-permute-start(bf16[2,2,16,1024]{3,2,1,0:T(8,128)(2,1)S(1)} %slice.97), channel_id=1, source_target_pairs={{0,2},{1,3},{2,0},{3,1},{4,6},{5,7},{6,4},{7,5},{8,10},{9,11},{10,... | collective-permute-start | bytes 393224 | tf_op jit(solution)/shard_map/ppermute | solution.py:23
  38.8 10.1 %collective-permute-start.16 = (bf16[2,2,16,1024]{3,2,1,0:T(8,128)(2,1)S(1)}, bf16[2,2,16,1024]{3,2,1,0:T(8,128)(2,1)S(1)}, u32[]{:S(2)}, u32[]{:S(2)}) collective-permute-start(bf16[2,2,16,1024]{3,2,1,0:T(8,128)(2,1)S(1)} %slice.101), channel_id=1, source_target_pairs={{0,4},{1,5},{2,6},{3,7},{4,0},{5,1},{6,2},{7,3},{8,12},{9,13},{10,... | collective-permute-start | bytes 393224 | tf_op jit(solution)/shard_map/ppermute | solution.py:23
  42.3 7.7 %collective-permute-start.13 = (bf16[2,2,16,1024]{3,2,1,0:T(8,128)(2,1)S(1)}, bf16[2,2,16,1024]{3,2,1,0:T(8,128)(2,1)S(1)}, u32[]{:S(2)}, u32[]{:S(2)}) collective-permute-start(bf16[2,2,16,1024]{3,2,1,0:T(8,128)(2,1)S(1)} %slice.99), channel_id=1, source_target_pairs={{0,2},{1,3},{2,0},{3,1},{4,6},{5,7},{6,4},{7,5},{8,10},{9,11},{10,... | collective-permute-start | bytes 393224 | tf_op jit(solution)/shard_map/ppermute | solution.py:23
  43.2 11.3 %collective-permute-start.11 = (bf16[2,2,16,1024]{3,2,1,0:T(8,128)(2,1)S(1)}, bf16[2,2,16,1024]{3,2,1,0:T(8,128)(2,1)S(1)}, u32[]{:S(2)}, u32[]{:S(2)}) collective-permute-start(bf16[2,2,16,1024]{3,2,1,0:T(8,128)(2,1)S(1)} %slice_add_fusion.9.kept_ref), channel_id=1, source_target_pairs={{0,4},{1,5},{2,6},{3,7},{4,0},{5,1},{6,2},{7,3},{8,12},{9,13},{10,... | collective-permute-start | bytes 393224 | tf_op jit(solution)/shard_map/ppermute | solution.py:23
  48.9 6.9 %collective-permute-start.17 = (bf16[2,2,16,1024]{3,2,1,0:T(8,128)(2,1)S(1)}, bf16[2,2,16,1024]{3,2,1,0:T(8,128)(2,1)S(1)}, u32[]{:S(2)}, u32[]{:S(2)}) collective-permute-start(bf16[2,2,16,1024]{3,2,1,0:T(8,128)(2,1)S(1)} %slice_add_fusion.7.kept_ref), channel_id=1, source_target_pairs={{0,2},{1,3},{2,0},{3,1},{4,6},{5,7},{6,4},{7,5},{8,10},{9,11},{10,... | collective-permute-start | bytes 393224 | tf_op jit(solution)/shard_map/ppermute | solution.py:23
  50.1 9.9 %collective-permute-start.14 = (bf16[2,2,16,1024]{3,2,1,0:T(8,128)(2,1)S(1)}, bf16[2,2,16,1024]{3,2,1,0:T(8,128)(2,1)S(1)}, u32[]{:S(2)}, u32[]{:S(2)}) collective-permute-start(bf16[2,2,16,1024]{3,2,1,0:T(8,128)(2,1)S(1)} %slice_add_fusion.8.kept_ref), channel_id=1, source_target_pairs={{0,4},{1,5},{2,6},{3,7},{4,0},{5,1},{6,2},{7,3},{8,12},{9,13},{10,... | collective-permute-start | bytes 393224 | tf_op jit(solution)/shard_map/ppermute | solution.py:23
  54.7 7.8 %collective-permute-start.18 = (bf16[2,2,16,1024]{3,2,1,0:T(8,128)(2,1)S(1)}, bf16[2,2,16,1024]{3,2,1,0:T(8,128)(2,1)S(1)}, u32[]{:S(2)}, u32[]{:S(2)}) collective-permute-start(bf16[2,2,16,1024]{3,2,1,0:T(8,128)(2,1)S(1)} %get-tuple-element.74), channel_id=1, source_target_pairs={{0,2},{1,3},{2,0},{3,1},{4,6},{5,7},{6,4},{7,5},{8,10},{9,11},{10,... | collective-permute-start | bytes 393224 | tf_op jit(solution)/shard_map/ppermute | solution.py:23
  56.0 8.8 %collective-permute-start.22 = (bf16[2,2,16,1024]{3,2,1,0:T(8,128)(2,1)S(1)}, bf16[2,2,16,1024]{3,2,1,0:T(8,128)(2,1)S(1)}, u32[]{:S(2)}, u32[]{:S(2)}) collective-permute-start(bf16[2,2,16,1024]{3,2,1,0:T(8,128)(2,1)S(1)} %get-tuple-element.76), channel_id=1, source_target_pairs={{0,4},{1,5},{2,6},{3,7},{4,0},{5,1},{6,2},{7,3},{8,12},{9,13},{10,... | collective-permute-start | bytes 393224 | tf_op jit(solution)/shard_map/ppermute | solution.py:23
  60.1 5.8 %collective-permute-start.20 = (bf16[2,2,16,1024]{3,2,1,0:T(8,128)(2,1)S(1)}, bf16[2,2,16,1024]{3,2,1,0:T(8,128)(2,1)S(1)}, u32[]{:S(2)}, u32[]{:S(2)}) collective-permute-start(bf16[2,2,16,1024]{3,2,1,0:T(8,128)(2,1)S(1)} %get-tuple-element.75), channel_id=1, source_target_pairs={{0,2},{1,3},{2,0},{3,1},{4,6},{5,7},{6,4},{7,5},{8,10},{9,11},{10,... | collective-permute-start | bytes 393224 | tf_op jit(solution)/shard_map/ppermute | solution.py:23
  62.5 8.3 %collective-permute-start.19 = (bf16[2,4,16,1024]{3,2,1,0:T(8,128)(2,1)S(1)}, bf16[2,4,16,1024]{3,2,1,0:T(8,128)(2,1)S(1)}, u32[]{:S(2)}, u32[]{:S(2)}) collective-permute-start(bf16[2,4,16,1024]{3,2,1,0:T(8,128)(2,1)S(1)} %constant_dynamic-update-slice_fusion.2.refs_0_), channel_id=1, source_target_pairs={{0,1},{1,0},{2,3},{3,2},{4,5},{5,4},{6,7},{7,6},{8,9},{9,8},{10,11... | collective-permute-start | bytes 786440 | tf_op jit(solution)/shard_map/ppermute | solution.py:23
  64.8 6.0 %collective-permute-start.23 = (bf16[2,4,16,1024]{3,2,1,0:T(8,128)(2,1)S(1)}, bf16[2,4,16,1024]{3,2,1,0:T(8,128)(2,1)S(1)}, u32[]{:S(2)}, u32[]{:S(2)}) collective-permute-start(bf16[2,4,16,1024]{3,2,1,0:T(8,128)(2,1)S(1)} %constant_dynamic-update-slice_fusion.6.refs_2_), channel_id=1, source_target_pairs={{0,1},{1,0},{2,3},{3,2},{4,5},{5,4},{6,7},{7,6},{8,9},{9,8},{10,11... | collective-permute-start | bytes 786440 | tf_op jit(solution)/shard_map/ppermute | solution.py:23
  65.9 4.8 %collective-permute-start.21 = (bf16[2,4,16,1024]{3,2,1,0:T(8,128)(2,1)S(1)}, bf16[2,4,16,1024]{3,2,1,0:T(8,128)(2,1)S(1)}, u32[]{:S(2)}, u32[]{:S(2)}) collective-permute-start(bf16[2,4,16,1024]{3,2,1,0:T(8,128)(2,1)S(1)} %constant_dynamic-update-slice_fusion.4.refs_1_), channel_id=1, source_target_pairs={{0,1},{1,0},{2,3},{3,2},{4,5},{5,4},{6,7},{7,6},{8,9},{9,8},{10,11... | collective-permute-start | bytes 786440 | tf_op jit(solution)/shard_map/ppermute | solution.py:23
  81.0 6.4 %collective-permute-start.28 = (bf16[4,2,16,512]{3,2,1,0:T(8,128)(2,1)S(1)}, bf16[4,2,16,512]{3,2,1,0:T(8,128)(2,1)S(1)}, u32[]{:S(2)}, u32[]{:S(2)}) collective-permute-start(bf16[4,2,16,512]{3,2,1,0:T(8,128)(2,1)S(1)} %slice.111), channel_id=1, source_target_pairs={{0,2},{1,3},{2,0},{3,1},{4,6},{5,7},{6,4},{7,5},{8,10},{9,11},{10,... | collective-permute-start | bytes 393224 | tf_op jit(solution)/shard_map/ppermute | solution.py:23
  82.7 8.1 %collective-permute-start.25 = (bf16[4,2,16,512]{3,2,1,0:T(8,128)(2,1)S(1)}, bf16[4,2,16,512]{3,2,1,0:T(8,128)(2,1)S(1)}, u32[]{:S(2)}, u32[]{:S(2)}) collective-permute-start(bf16[4,2,16,512]{3,2,1,0:T(8,128)(2,1)S(1)} %slice.105), channel_id=1, source_target_pairs={{0,2},{1,3},{2,0},{3,1},{4,6},{5,7},{6,4},{7,5},{8,10},{9,11},{10,... | collective-permute-start | bytes 393224 | tf_op jit(solution)/shard_map/ppermute | solution.py:23
  87.4 7.0 %collective-permute-start.29 = (bf16[4,1,16,512]{3,2,1,0:T(8,128)(2,1)S(1)}, bf16[4,1,16,512]{3,2,1,0:T(8,128)(2,1)S(1)}, u32[]{:S(2)}, u32[]{:S(2)}) collective-permute-start(bf16[4,1,16,512]{3,2,1,0:T(8,128)(2,1)S(1)} %get-tuple-element.81), channel_id=1, source_target_pairs={{0,4},{1,5},{2,6},{3,7},{4,0},{5,1},{6,2},{7,3},{8,12},{9,13},{10,... | collective-permute-start | bytes 196616 | tf_op jit(solution)/shard_map/ppermute | solution.py:23
  90.8 5.7 %collective-permute-start.26 = (bf16[4,1,16,512]{3,2,1,0:T(8,128)(2,1)S(1)}, bf16[4,1,16,512]{3,2,1,0:T(8,128)(2,1)S(1)}, u32[]{:S(2)}, u32[]{:S(2)}) collective-permute-start(bf16[4,1,16,512]{3,2,1,0:T(8,128)(2,1)S(1)} %get-tuple-element.83), channel_id=1, source_target_pairs={{0,4},{1,5},{2,6},{3,7},{4,0},{5,1},{6,2},{7,3},{8,12},{9,13},{10,... | collective-permute-start | bytes 196616 | tf_op jit(solution)/shard_map/ppermute | solution.py:23
  99.8 4.8 %collective-permute-start.32 = (bf16[16,1024]{1,0:T(8,128)(2,1)S(1)}, bf16[16,1024]{1,0:T(8,128)(2,1)S(1)}, u32[]{:S(2)}, u32[]{:S(2)}) collective-permute-start(bf16[16,1024]{1,0:T(8,128)(2,1)S(1)} %get-tuple-element.80), channel_id=1, source_target_pairs={{0,24},{8,16},{16,8},{24,0},{1,25},{9,17},{17,9},{25,1},{2,26},{10... | collective-permute-start | bytes 98312 | tf_op jit(solution)/shard_map/ppermute | solution.py:23
  (21 other events, 161.1 us)

commit v5 on v4

--- a/solution.py
+++ b/solution.py
@@ -268,23 +268,31 @@
             ],
             1,
         )
-        for head in range(heads):
+        def weigh(head):
             at = slice(head * HEAD, (head + 1) * HEAD)
             qs = rows_of(q_ref, (first, second), at)
             ks = rows_of(k_ref, (first + 1, second + 1, 0), at)
             scores = lax.dot_general(qs, ks, (((1,), (1,)), ((), ())), preferred_element_type=jnp.float32) + bias
             top = jnp.max(scores, -1, keepdims=True)
             expo_ref[head] = jnp.exp2(scores - top).astype(jnp.bfloat16)
-        for head in range(heads):
+
+        def mix(head):
             at = slice(head * HEAD, (head + 1) * HEAD)
             vs = rows_of(v_ref, (first + 1, second + 1, 0), at)
             mixed = jnp.dot(expo_ref[head], jnp.concatenate([vs, ones], 1), preferred_element_type=jnp.float32)
             ctx_ref[pl.ds(pl.multiple_of(pair * 2 * keys, 2 * keys), 2 * keys), at] = (
                 mixed[:, :HEAD] / mixed[:, HEAD:]
             ).astype(jnp.bfloat16)
+
+        ahead = min(3, heads)
+        for head in range(heads + ahead):
+            if head < heads:
+                weigh(head)
+            if head >= ahead:
+                mix(head - ahead)
         return carry
 
-    lax.fori_loop(0, pairs, one_pair, 0)
+    lax.fori_loop(0, pairs, one_pair, 0, unroll=True)
     begin = out_ref.shape[0] * keys
     product = jnp.dot(ctx_ref[:begin], wo_ref[...], preferred_element_type=jnp.float32)
     out_ref[...] = product.astype(jnp.bfloat16).reshape(out_ref.shape)
@@ -388,7 +396,7 @@
             out_ref[last, slot, :, at] = out_ref[last, slot, :, at] + units[r * group : (r + 1) * group]
         return carry
 
-    lax.fori_loop(0, w_ref.shape[1] // tile, step, 0, unroll=2)
+    lax.fori_loop(0, w_ref.shape[1] // tile, step, 0, unroll=4)
 
 
 def expand(meta, swapped, pieces, w_in, slots, old=()):

time: 105 us -> 104 us (level)
  Pallas kernels: 28.9 us -> 27.7 us
    pallas_call x18, Pallas kernels: 28.9 us -> 27.7 us  [kernel_call(): pl.pallas_call(kernel, out_shape=out_shape, in_specs=[space(i in smem, i...]
where the time goes in v5:
time: 104 us
  starting transfers between devices  50.8 us (49%)
  Pallas kernels  27.7 us (27%)
  waiting for transfers between devices  24.5 us (24%)
    ppermute x33, starting transfers between devices, swap(): return lax.ppermute(values, axis, [(i, i ^ bit) for i in range(count)])  50.8 us
    pallas_call x18, Pallas kernels, kernel_call(): pl.pallas_call(kernel, out_shape=out_shape, in_specs=[space(i in smem, i...  27.7 us
    ppermute x33, waiting for transfers between devices, swap(): return lax.ppermute(values, axis, [(i, i ^ bit) for i in range(count)])  24.5 us
  transfers between devices with their start and end apart: 33, of which 17 were waited for; matrix products, arithmetic and copies ran while one was open for 1% of the time, Pallas kernels for 10%

profile of v5, /device:TPU:0, one launch (start us, length us, event | category | flops | bytes accessed | tf_op | source)
XLA Modules:
  0.0 104.2 jit_solution(12996391123824509035)
XLA Ops:
  1.7 3.0 %collective-permute-start = (bf16[16,1024]{1,0:T(8,128)(2,1)}, bf16[16,1024]{1,0:T(8,128)(2,1)S(1)}, u32[]{:S(2)}, u32[]{:S(2)}) collective-permute-start(bf16[16,1024]{1,0:T(8,128)(2,1)} %get-tuple-element.44), channel_id=1, source_target_pairs={{0,8},{8,0},{16,24},{24,16},{1,9},{9,1},{17,25},{25,17},{2,10},{10... | collective-permute-start | bytes 98312 | tf_op jit(solution)/shard_map/ppermute | solution.py:23
  6.2 3.0 %collective-permute-start.3 = (bf16[2,1,16,1024]{3,2,1,0:T(8,128)(2,1)}, bf16[2,1,16,1024]{3,2,1,0:T(8,128)(2,1)S(1)}, u32[]{:S(2)}, u32[]{:S(2)}) collective-permute-start(bf16[2,1,16,1024]{3,2,1,0:T(8,128)(2,1)} %get-tuple-element.47.kept_ref), channel_id=1, source_target_pairs={{0,4},{1,5},{2,6},{3,7},{4,0},{5,1},{6,2},{7,3},{8,12},{9,13},{10,... | collective-permute-start | bytes 196616 | tf_op jit(solution)/shard_map/ppermute | solution.py:23
  9.3 1.9 %collective-permute-done.2.refs_2_ = bf16[16,1024]{1,0:T(8,128)(2,1)S(1)} collective-permute-done((bf16[16,1024]{1,0:T(8,128)(2,1)}, bf16[16,1024]{1,0:T(8,128)(2,1)S(1)}, u32[]{:S(2)}, u32[]{:S(2)}) %collective-permute-start.2) | collective-permute-done | bytes 32800 | tf_op jit(solution)/shard_map/ppermute | solution.py:23
  11.8 3.0 %collective-permute-start.4 = (bf16[3,1,16,1024]{3,2,1,0:T(8,128)(2,1)S(1)}, bf16[3,1,16,1024]{3,2,1,0:T(8,128)(2,1)S(1)}, u32[]{:S(2)}, u32[]{:S(2)}) collective-permute-start(bf16[3,1,16,1024]{3,2,1,0:T(8,128)(2,1)S(1)} %stack.1.kept_ref), channel_id=1, source_target_pairs={{0,4},{1,5},{2,6},{3,7},{4,0},{5,1},{6,2},{7,3},{8,12},{9,13},{10,... | collective-permute-start | bytes 294920 | tf_op jit(solution)/shard_map/ppermute | solution.py:23
  14.8 2.1 %collective-permute-start.6 = (bf16[2,2,16,1024]{3,2,1,0:T(8,128)(2,1)S(1)}, bf16[2,2,16,1024]{3,2,1,0:T(8,128)(2,1)S(1)}, u32[]{:S(2)}, u32[]{:S(2)}) collective-permute-start(bf16[2,2,16,1024]{3,2,1,0:T(8,128)(2,1)S(1)} %join.2), channel_id=1, source_target_pairs={{0,2},{1,3},{2,0},{3,1},{4,6},{5,7},{6,4},{7,5},{8,10},{9,11},{10,... | collective-permute-start | bytes 393224 | tf_op jit(solution)/shard_map/ppermute | solution.py:23
  17.5 2.1 %collective-permute-start.5 = (bf16[3,2,16,1024]{3,2,1,0:T(8,128)(2,1)S(1)}, bf16[3,2,16,1024]{3,2,1,0:T(8,128)(2,1)S(1)}, u32[]{:S(2)}, u32[]{:S(2)}) collective-permute-start(bf16[3,2,16,1024]{3,2,1,0:T(8,128)(2,1)S(1)} %join.3), channel_id=1, source_target_pairs={{0,2},{1,3},{2,0},{3,1},{4,6},{5,7},{6,4},{7,5},{8,10},{9,11},{10,... | collective-permute-start | bytes 589832 | tf_op jit(solution)/shard_map/ppermute | solution.py:23
  21.4 2.0 %collective-permute-done.5 = bf16[3,2,16,1024]{3,2,1,0:T(8,128)(2,1)S(1)} collective-permute-done((bf16[3,2,16,1024]{3,2,1,0:T(8,128)(2,1)S(1)}, bf16[3,2,16,1024]{3,2,1,0:T(8,128)(2,1)S(1)}, u32[]{:S(2)}, u32[]{:S(2)}) %collective-permute-start.5) | collective-permute-done | bytes 196640 | tf_op jit(solution)/shard_map/ppermute | solution.py:23
  28.5 5.0 %attend.1 = (bf16[2,8,16,1024]{3,2,1,0:T(8,128)(2,1)S(1)}, bf16[512,1024]{1,0:T(8,128)(2,1)S(1)}, bf16[3,2,2,16,1024]{4,3,2,1,0:T(8,128)(2,1)S(1)}, f32[6,4,8,12...) custom-call(s32[4,6]{1,0:T(4,128)S(1)} %copy-done.5, ...), custom_call_target="tpu_custom_call" | custom-call | flops 1744830464 | bytes 2097152 | tf_op jit(solution)/shard_map/attend/pallas_call | solution.py:54
  36.0 2.0 %collective-permute-start.10 = (bf16[2,2,16,1024]{3,2,1,0:T(8,128)(2,1)S(1)}, bf16[2,2,16,1024]{3,2,1,0:T(8,128)(2,1)S(1)}, u32[]{:S(2)}, u32[]{:S(2)}) collective-permute-start(bf16[2,2,16,1024]{3,2,1,0:T(8,128)(2,1)S(1)} %slice.97), channel_id=1, source_target_pairs={{0,2},{1,3},{2,0},{3,1},{4,6},{5,7},{6,4},{7,5},{8,10},{9,11},{10,... | collective-permute-start | bytes 393224 | tf_op jit(solution)/shard_map/ppermute | solution.py:23
  38.1 3.5 %collective-permute-start.16 = (bf16[2,2,16,1024]{3,2,1,0:T(8,128)(2,1)S(1)}, bf16[2,2,16,1024]{3,2,1,0:T(8,128)(2,1)S(1)}, u32[]{:S(2)}, u32[]{:S(2)}) collective-permute-start(bf16[2,2,16,1024]{3,2,1,0:T(8,128)(2,1)S(1)} %slice.101), channel_id=1, source_target_pairs={{0,4},{1,5},{2,6},{3,7},{4,0},{5,1},{6,2},{7,3},{8,12},{9,13},{10,... | collective-permute-start | bytes 393224 | tf_op jit(solution)/shard_map/ppermute | solution.py:23
  42.5 3.3 %collective-permute-start.11 = (bf16[2,2,16,1024]{3,2,1,0:T(8,128)(2,1)S(1)}, bf16[2,2,16,1024]{3,2,1,0:T(8,128)(2,1)S(1)}, u32[]{:S(2)}, u32[]{:S(2)}) collective-permute-start(bf16[2,2,16,1024]{3,2,1,0:T(8,128)(2,1)S(1)} %slice_add_fusion.9.kept_ref), channel_id=1, source_target_pairs={{0,4},{1,5},{2,6},{3,7},{4,0},{5,1},{6,2},{7,3},{8,12},{9,13},{10,... | collective-permute-start | bytes 393224 | tf_op jit(solution)/shard_map/ppermute | solution.py:23
  45.9 2.3 %collective-permute-done.16 = bf16[2,2,16,1024]{3,2,1,0:T(8,128)(2,1)S(1)} collective-permute-done((bf16[2,2,16,1024]{3,2,1,0:T(8,128)(2,1)S(1)}, bf16[2,2,16,1024]{3,2,1,0:T(8,128)(2,1)S(1)}, u32[]{:S(2)}, u32[]{:S(2)}) %collective-permute-start.16) | collective-permute-done | bytes 131104 | tf_op jit(solution)/shard_map/ppermute | solution.py:23
  49.4 3.9 %collective-permute-start.14 = (bf16[2,2,16,1024]{3,2,1,0:T(8,128)(2,1)S(1)}, bf16[2,2,16,1024]{3,2,1,0:T(8,128)(2,1)S(1)}, u32[]{:S(2)}, u32[]{:S(2)}) collective-permute-start(bf16[2,2,16,1024]{3,2,1,0:T(8,128)(2,1)S(1)} %slice_add_fusion.8.kept_ref), channel_id=1, source_target_pairs={{0,4},{1,5},{2,6},{3,7},{4,0},{5,1},{6,2},{7,3},{8,12},{9,13},{10,... | collective-permute-start | bytes 393224 | tf_op jit(solution)/shard_map/ppermute | solution.py:23
  55.3 3.9 %collective-permute-start.22 = (bf16[2,2,16,1024]{3,2,1,0:T(8,128)(2,1)S(1)}, bf16[2,2,16,1024]{3,2,1,0:T(8,128)(2,1)S(1)}, u32[]{:S(2)}, u32[]{:S(2)}) collective-permute-start(bf16[2,2,16,1024]{3,2,1,0:T(8,128)(2,1)S(1)} %get-tuple-element.76), channel_id=1, source_target_pairs={{0,4},{1,5},{2,6},{3,7},{4,0},{5,1},{6,2},{7,3},{8,12},{9,13},{10,... | collective-permute-start | bytes 393224 | tf_op jit(solution)/shard_map/ppermute | solution.py:23
  61.8 2.2 %collective-permute-done.22 = bf16[2,2,16,1024]{3,2,1,0:T(8,128)(2,1)S(1)} collective-permute-done((bf16[2,2,16,1024]{3,2,1,0:T(8,128)(2,1)S(1)}, bf16[2,2,16,1024]{3,2,1,0:T(8,128)(2,1)S(1)}, u32[]{:S(2)}, u32[]{:S(2)}) %collective-permute-start.22) | collective-permute-done | bytes 131104 | tf_op jit(solution)/shard_map/ppermute | solution.py:23
  65.4 4.5 %expand.2.refs_3_ = bf16[1,4,64,4096]{3,2,1,0:T(8,128)(2,1)S(1)} custom-call(s32[4,6]{1,0:T(4,128)S(1)} %copy-done.5, bf16[1024,4096]{1,0:T(8,128)(2,1)S(1)} %bitcast.5, bf16[2,4,16,1024]{3,2,1,0:T(8,128)(2,1)S(1)} %constant_dynamic-update-slice_fusion.2.refs_0_, bf16[2,4,16,1024]{3,2,1,0:T(8,128)(2,1)S(1)} %constant_dynamic-update-slice_fusion.4.refs_1_, ...), custom_call_target="tpu_custom_call" | custom-call | flops 3221225472 | bytes 8388608 | tf_op jit(solution)/shard_map/expand/pallas_call | solution.py:54
  69.9 4.5 %expand.3.units_ref = bf16[2,4,64,4096]{3,2,1,0:T(8,128)(2,1)S(1)} custom-call(s32[4,6]{1,0:T(4,128)S(1)} %copy-done.5, bf16[1024,4096]{1,0:T(8,128)(2,1)S(1)} %bitcast.5, bf16[2,4,16,1024]{3,2,1,0:T(8,128)(2,1)S(1)} %collective-permute-done.19.refs_0_, bf16[2,4,16,1024]{3,2,1,0:T(8,128)(2,1)S(1)} %collective-permute-done.21.refs_1_, ...), custom_call_target="tpu_custom_call" | custom-call | flops 3221225472 | bytes 8388608 | tf_op jit(solution)/shard_map/expand/pallas_call | solution.py:54
  74.5 2.3 %shrink.3 = bf16[4,8,16,512]{3,2,1,0:T(8,128)(2,1)S(1)} custom-call(bf16[2,4,64,4096]{3,2,1,0:T(8,128)(2,1)S(1)} %expand.3.units_ref, bf16[4096,1024]{1,0:T(8,128)(2,1)S(1)} %bitcast.3), custom_call_target="tpu_custom_call" | custom-call | flops 2147483648 | bytes 4194304 | tf_op jit(solution)/shard_map/shrink/pallas_call | solution.py:54
  77.3 2.3 %shrink.2 = bf16[4,8,16,512]{3,2,1,0:T(8,128)(2,1)S(1)} custom-call(bf16[2,4,64,4096]{3,2,1,0:T(8,128)(2,1)S(1)} %expand.3.units_ref, bf16[4096,1024]{1,0:T(8,128)(2,1)S(1)} %bitcast.3), custom_call_target="tpu_custom_call" | custom-call | flops 2147483648 | bytes 4194304 | tf_op jit(solution)/shard_map/shrink/pallas_call | solution.py:54
  82.8 3.5 %collective-permute-done.28 = bf16[4,2,16,512]{3,2,1,0:T(8,128)(2,1)S(1)} collective-permute-done((bf16[4,2,16,512]{3,2,1,0:T(8,128)(2,1)S(1)}, bf16[4,2,16,512]{3,2,1,0:T(8,128)(2,1)S(1)}, u32[]{:S(2)}, u32[]{:S(2)}) %collective-permute-start.28) | collective-permute-done | bytes 131104 | tf_op jit(solution)/shard_map/ppermute | solution.py:23
  86.3 3.3 %collective-permute-start.29 = (bf16[4,1,16,512]{3,2,1,0:T(8,128)(2,1)S(1)}, bf16[4,1,16,512]{3,2,1,0:T(8,128)(2,1)S(1)}, u32[]{:S(2)}, u32[]{:S(2)}) collective-permute-start(bf16[4,1,16,512]{3,2,1,0:T(8,128)(2,1)S(1)} %get-tuple-element.81), channel_id=1, source_target_pairs={{0,4},{1,5},{2,6},{3,7},{4,0},{5,1},{6,2},{7,3},{8,12},{9,13},{10,... | collective-permute-start | bytes 196616 | tf_op jit(solution)/shard_map/ppermute | solution.py:23
  89.7 2.8 %collective-permute-start.26 = (bf16[4,1,16,512]{3,2,1,0:T(8,128)(2,1)S(1)}, bf16[4,1,16,512]{3,2,1,0:T(8,128)(2,1)S(1)}, u32[]{:S(2)}, u32[]{:S(2)}) collective-permute-start(bf16[4,1,16,512]{3,2,1,0:T(8,128)(2,1)S(1)} %get-tuple-element.83), channel_id=1, source_target_pairs={{0,4},{1,5},{2,6},{3,7},{4,0},{5,1},{6,2},{7,3},{8,12},{9,13},{10,... | collective-permute-start | bytes 196616 | tf_op jit(solution)/shard_map/ppermute | solution.py:23
  93.3 2.1 %collective-permute-done.26.refs_1_ = bf16[4,1,16,512]{3,2,1,0:T(8,128)(2,1)S(1)} collective-permute-done((bf16[4,1,16,512]{3,2,1,0:T(8,128)(2,1)S(1)}, bf16[4,1,16,512]{3,2,1,0:T(8,128)(2,1)S(1)}, u32[]{:S(2)}, u32[]{:S(2)}) %collective-permute-start.26) | collective-permute-done | bytes 65568 | tf_op jit(solution)/shard_map/ppermute | solution.py:23
  101.0 2.4 %collective-permute-done.32.refs_3_ = bf16[16,1024]{1,0:T(8,128)(2,1)S(1)} collective-permute-done((bf16[16,1024]{1,0:T(8,128)(2,1)S(1)}, bf16[16,1024]{1,0:T(8,128)(2,1)S(1)}, u32[]{:S(2)}, u32[]{:S(2)}) %collective-permute-start.32) | collective-permute-done | bytes 32800 | tf_op jit(solution)/shard_map/ppermute | solution.py:23
  (118 shorter events, 32.5 us)
Async XLA Ops:
  1.7 7.6 %collective-permute-start = (bf16[16,1024]{1,0:T(8,128)(2,1)}, bf16[16,1024]{1,0:T(8,128)(2,1)S(1)}, u32[]{:S(2)}, u32[]{:S(2)}) collective-permute-start(bf16[16,1024]{1,0:T(8,128)(2,1)} %get-tuple-element.44), channel_id=1, source_target_pairs={{0,8},{8,0},{16,24},{24,16},{1,9},{9,1},{17,25},{25,17},{2,10},{10... | collective-permute-start | bytes 98312 | tf_op jit(solution)/shard_map/ppermute | solution.py:23
  6.2 5.0 %collective-permute-start.2 = (bf16[16,1024]{1,0:T(8,128)(2,1)}, bf16[16,1024]{1,0:T(8,128)(2,1)S(1)}, u32[]{:S(2)}, u32[]{:S(2)}) collective-permute-start(bf16[16,1024]{1,0:T(8,128)(2,1)} %get-tuple-element.46), channel_id=1, source_target_pairs={{0,24},{8,16},{16,8},{24,0},{1,25},{9,17},{17,9},{25,1},{2,26},{10... | collective-permute-start | bytes 98312 | tf_op jit(solution)/shard_map/ppermute | solution.py:23
  6.2 5.6 %collective-permute-start.3 = (bf16[2,1,16,1024]{3,2,1,0:T(8,128)(2,1)}, bf16[2,1,16,1024]{3,2,1,0:T(8,128)(2,1)S(1)}, u32[]{:S(2)}, u32[]{:S(2)}) collective-permute-start(bf16[2,1,16,1024]{3,2,1,0:T(8,128)(2,1)} %get-tuple-element.47.kept_ref), channel_id=1, source_target_pairs={{0,4},{1,5},{2,6},{3,7},{4,0},{5,1},{6,2},{7,3},{8,12},{9,13},{10,... | collective-permute-start | bytes 196616 | tf_op jit(solution)/shard_map/ppermute | solution.py:23
  11.8 5.7 %collective-permute-start.4 = (bf16[3,1,16,1024]{3,2,1,0:T(8,128)(2,1)S(1)}, bf16[3,1,16,1024]{3,2,1,0:T(8,128)(2,1)S(1)}, u32[]{:S(2)}, u32[]{:S(2)}) collective-permute-start(bf16[3,1,16,1024]{3,2,1,0:T(8,128)(2,1)S(1)} %stack.1.kept_ref), channel_id=1, source_target_pairs={{0,4},{1,5},{2,6},{3,7},{4,0},{5,1},{6,2},{7,3},{8,12},{9,13},{10,... | collective-permute-start | bytes 294920 | tf_op jit(solution)/shard_map/ppermute | solution.py:23
  14.8 6.5 %collective-permute-start.6 = (bf16[2,2,16,1024]{3,2,1,0:T(8,128)(2,1)S(1)}, bf16[2,2,16,1024]{3,2,1,0:T(8,128)(2,1)S(1)}, u32[]{:S(2)}, u32[]{:S(2)}) collective-permute-start(bf16[2,2,16,1024]{3,2,1,0:T(8,128)(2,1)S(1)} %join.2), channel_id=1, source_target_pairs={{0,2},{1,3},{2,0},{3,1},{4,6},{5,7},{6,4},{7,5},{8,10},{9,11},{10,... | collective-permute-start | bytes 393224 | tf_op jit(solution)/shard_map/ppermute | solution.py:23
  17.5 5.8 %collective-permute-start.5 = (bf16[3,2,16,1024]{3,2,1,0:T(8,128)(2,1)S(1)}, bf16[3,2,16,1024]{3,2,1,0:T(8,128)(2,1)S(1)}, u32[]{:S(2)}, u32[]{:S(2)}) collective-permute-start(bf16[3,2,16,1024]{3,2,1,0:T(8,128)(2,1)S(1)} %join.3), channel_id=1, source_target_pairs={{0,2},{1,3},{2,0},{3,1},{4,6},{5,7},{6,4},{7,5},{8,10},{9,11},{10,... | collective-permute-start | bytes 589832 | tf_op jit(solution)/shard_map/ppermute | solution.py:23
  35.6 6.0 %collective-permute-start.12 = (bf16[2,4,16,1024]{3,2,1,0:T(8,128)(2,1)S(1)}, bf16[2,4,16,1024]{3,2,1,0:T(8,128)(2,1)S(1)}, u32[]{:S(2)}, u32[]{:S(2)}) collective-permute-start(bf16[2,4,16,1024]{3,2,1,0:T(8,128)(2,1)S(1)} %slice.77), channel_id=1, source_target_pairs={{0,1},{1,0},{2,3},{3,2},{4,5},{5,4},{6,7},{7,6},{8,9},{9,8},{10,11... | collective-permute-start | bytes 786440 | tf_op jit(solution)/shard_map/ppermute | solution.py:23
  36.0 6.5 %collective-permute-start.10 = (bf16[2,2,16,1024]{3,2,1,0:T(8,128)(2,1)S(1)}, bf16[2,2,16,1024]{3,2,1,0:T(8,128)(2,1)S(1)}, u32[]{:S(2)}, u32[]{:S(2)}) collective-permute-start(bf16[2,2,16,1024]{3,2,1,0:T(8,128)(2,1)S(1)} %slice.97), channel_id=1, source_target_pairs={{0,2},{1,3},{2,0},{3,1},{4,6},{5,7},{6,4},{7,5},{8,10},{9,11},{10,... | collective-permute-start | bytes 393224 | tf_op jit(solution)/shard_map/ppermute | solution.py:23
  38.1 10.1 %collective-permute-start.16 = (bf16[2,2,16,1024]{3,2,1,0:T(8,128)(2,1)S(1)}, bf16[2,2,16,1024]{3,2,1,0:T(8,128)(2,1)S(1)}, u32[]{:S(2)}, u32[]{:S(2)}) collective-permute-start(bf16[2,2,16,1024]{3,2,1,0:T(8,128)(2,1)S(1)} %slice.101), channel_id=1, source_target_pairs={{0,4},{1,5},{2,6},{3,7},{4,0},{5,1},{6,2},{7,3},{8,12},{9,13},{10,... | collective-permute-start | bytes 393224 | tf_op jit(solution)/shard_map/ppermute | solution.py:23
  41.6 7.7 %collective-permute-start.13 = (bf16[2,2,16,1024]{3,2,1,0:T(8,128)(2,1)S(1)}, bf16[2,2,16,1024]{3,2,1,0:T(8,128)(2,1)S(1)}, u32[]{:S(2)}, u32[]{:S(2)}) collective-permute-start(bf16[2,2,16,1024]{3,2,1,0:T(8,128)(2,1)S(1)} %slice.99), channel_id=1, source_target_pairs={{0,2},{1,3},{2,0},{3,1},{4,6},{5,7},{6,4},{7,5},{8,10},{9,11},{10,... | collective-permute-start | bytes 393224 | tf_op jit(solution)/shard_map/ppermute | solution.py:23
  42.5 11.3 %collective-permute-start.11 = (bf16[2,2,16,1024]{3,2,1,0:T(8,128)(2,1)S(1)}, bf16[2,2,16,1024]{3,2,1,0:T(8,128)(2,1)S(1)}, u32[]{:S(2)}, u32[]{:S(2)}) collective-permute-start(bf16[2,2,16,1024]{3,2,1,0:T(8,128)(2,1)S(1)} %slice_add_fusion.9.kept_ref), channel_id=1, source_target_pairs={{0,4},{1,5},{2,6},{3,7},{4,0},{5,1},{6,2},{7,3},{8,12},{9,13},{10,... | collective-permute-start | bytes 393224 | tf_op jit(solution)/shard_map/ppermute | solution.py:23
  48.2 6.9 %collective-permute-start.17 = (bf16[2,2,16,1024]{3,2,1,0:T(8,128)(2,1)S(1)}, bf16[2,2,16,1024]{3,2,1,0:T(8,128)(2,1)S(1)}, u32[]{:S(2)}, u32[]{:S(2)}) collective-permute-start(bf16[2,2,16,1024]{3,2,1,0:T(8,128)(2,1)S(1)} %slice_add_fusion.7.kept_ref), channel_id=1, source_target_pairs={{0,2},{1,3},{2,0},{3,1},{4,6},{5,7},{6,4},{7,5},{8,10},{9,11},{10,... | collective-permute-start | bytes 393224 | tf_op jit(solution)/shard_map/ppermute | solution.py:23
  49.4 9.9 %collective-permute-start.14 = (bf16[2,2,16,1024]{3,2,1,0:T(8,128)(2,1)S(1)}, bf16[2,2,16,1024]{3,2,1,0:T(8,128)(2,1)S(1)}, u32[]{:S(2)}, u32[]{:S(2)}) collective-permute-start(bf16[2,2,16,1024]{3,2,1,0:T(8,128)(2,1)S(1)} %slice_add_fusion.8.kept_ref), channel_id=1, source_target_pairs={{0,4},{1,5},{2,6},{3,7},{4,0},{5,1},{6,2},{7,3},{8,12},{9,13},{10,... | collective-permute-start | bytes 393224 | tf_op jit(solution)/shard_map/ppermute | solution.py:23
  54.0 7.8 %collective-permute-start.18 = (bf16[2,2,16,1024]{3,2,1,0:T(8,128)(2,1)S(1)}, bf16[2,2,16,1024]{3,2,1,0:T(8,128)(2,1)S(1)}, u32[]{:S(2)}, u32[]{:S(2)}) collective-permute-start(bf16[2,2,16,1024]{3,2,1,0:T(8,128)(2,1)S(1)} %get-tuple-element.74), channel_id=1, source_target_pairs={{0,2},{1,3},{2,0},{3,1},{4,6},{5,7},{6,4},{7,5},{8,10},{9,11},{10,... | collective-permute-start | bytes 393224 | tf_op jit(solution)/shard_map/ppermute | solution.py:23
  55.3 8.8 %collective-permute-start.22 = (bf16[2,2,16,1024]{3,2,1,0:T(8,128)(2,1)S(1)}, bf16[2,2,16,1024]{3,2,1,0:T(8,128)(2,1)S(1)}, u32[]{:S(2)}, u32[]{:S(2)}) collective-permute-start(bf16[2,2,16,1024]{3,2,1,0:T(8,128)(2,1)S(1)} %get-tuple-element.76), channel_id=1, source_target_pairs={{0,4},{1,5},{2,6},{3,7},{4,0},{5,1},{6,2},{7,3},{8,12},{9,13},{10,... | collective-permute-start | bytes 393224 | tf_op jit(solution)/shard_map/ppermute | solution.py:23
  59.4 5.8 %collective-permute-start.20 = (bf16[2,2,16,1024]{3,2,1,0:T(8,128)(2,1)S(1)}, bf16[2,2,16,1024]{3,2,1,0:T(8,128)(2,1)S(1)}, u32[]{:S(2)}, u32[]{:S(2)}) collective-permute-start(bf16[2,2,16,1024]{3,2,1,0:T(8,128)(2,1)S(1)} %get-tuple-element.75), channel_id=1, source_target_pairs={{0,2},{1,3},{2,0},{3,1},{4,6},{5,7},{6,4},{7,5},{8,10},{9,11},{10,... | collective-permute-start | bytes 393224 | tf_op jit(solution)/shard_map/ppermute | solution.py:23
  61.8 8.1 %collective-permute-start.19 = (bf16[2,4,16,1024]{3,2,1,0:T(8,128)(2,1)S(1)}, bf16[2,4,16,1024]{3,2,1,0:T(8,128)(2,1)S(1)}, u32[]{:S(2)}, u32[]{:S(2)}) collective-permute-start(bf16[2,4,16,1024]{3,2,1,0:T(8,128)(2,1)S(1)} %constant_dynamic-update-slice_fusion.2.refs_0_), channel_id=1, source_target_pairs={{0,1},{1,0},{2,3},{3,2},{4,5},{5,4},{6,7},{7,6},{8,9},{9,8},{10,11... | collective-permute-start | bytes 786440 | tf_op jit(solution)/shard_map/ppermute | solution.py:23
  64.1 5.8 %collective-permute-start.23 = (bf16[2,4,16,1024]{3,2,1,0:T(8,128)(2,1)S(1)}, bf16[2,4,16,1024]{3,2,1,0:T(8,128)(2,1)S(1)}, u32[]{:S(2)}, u32[]{:S(2)}) collective-permute-start(bf16[2,4,16,1024]{3,2,1,0:T(8,128)(2,1)S(1)} %constant_dynamic-update-slice_fusion.6.refs_2_), channel_id=1, source_target_pairs={{0,1},{1,0},{2,3},{3,2},{4,5},{5,4},{6,7},{7,6},{8,9},{9,8},{10,11... | collective-permute-start | bytes 786440 | tf_op jit(solution)/shard_map/ppermute | solution.py:23
  65.2 4.6 %collective-permute-start.21 = (bf16[2,4,16,1024]{3,2,1,0:T(8,128)(2,1)S(1)}, bf16[2,4,16,1024]{3,2,1,0:T(8,128)(2,1)S(1)}, u32[]{:S(2)}, u32[]{:S(2)}) collective-permute-start(bf16[2,4,16,1024]{3,2,1,0:T(8,128)(2,1)S(1)} %constant_dynamic-update-slice_fusion.4.refs_1_), channel_id=1, source_target_pairs={{0,1},{1,0},{2,3},{3,2},{4,5},{5,4},{6,7},{7,6},{8,9},{9,8},{10,11... | collective-permute-start | bytes 786440 | tf_op jit(solution)/shard_map/ppermute | solution.py:23
  79.9 6.4 %collective-permute-start.28 = (bf16[4,2,16,512]{3,2,1,0:T(8,128)(2,1)S(1)}, bf16[4,2,16,512]{3,2,1,0:T(8,128)(2,1)S(1)}, u32[]{:S(2)}, u32[]{:S(2)}) collective-permute-start(bf16[4,2,16,512]{3,2,1,0:T(8,128)(2,1)S(1)} %slice.111), channel_id=1, source_target_pairs={{0,2},{1,3},{2,0},{3,1},{4,6},{5,7},{6,4},{7,5},{8,10},{9,11},{10,... | collective-permute-start | bytes 393224 | tf_op jit(solution)/shard_map/ppermute | solution.py:23
  81.5 8.1 %collective-permute-start.25 = (bf16[4,2,16,512]{3,2,1,0:T(8,128)(2,1)S(1)}, bf16[4,2,16,512]{3,2,1,0:T(8,128)(2,1)S(1)}, u32[]{:S(2)}, u32[]{:S(2)}) collective-permute-start(bf16[4,2,16,512]{3,2,1,0:T(8,128)(2,1)S(1)} %slice.105), channel_id=1, source_target_pairs={{0,2},{1,3},{2,0},{3,1},{4,6},{5,7},{6,4},{7,5},{8,10},{9,11},{10,... | collective-permute-start | bytes 393224 | tf_op jit(solution)/shard_map/ppermute | solution.py:23
  86.3 7.0 %collective-permute-start.29 = (bf16[4,1,16,512]{3,2,1,0:T(8,128)(2,1)S(1)}, bf16[4,1,16,512]{3,2,1,0:T(8,128)(2,1)S(1)}, u32[]{:S(2)}, u32[]{:S(2)}) collective-permute-start(bf16[4,1,16,512]{3,2,1,0:T(8,128)(2,1)S(1)} %get-tuple-element.81), channel_id=1, source_target_pairs={{0,4},{1,5},{2,6},{3,7},{4,0},{5,1},{6,2},{7,3},{8,12},{9,13},{10,... | collective-permute-start | bytes 196616 | tf_op jit(solution)/shard_map/ppermute | solution.py:23
  89.7 5.7 %collective-permute-start.26 = (bf16[4,1,16,512]{3,2,1,0:T(8,128)(2,1)S(1)}, bf16[4,1,16,512]{3,2,1,0:T(8,128)(2,1)S(1)}, u32[]{:S(2)}, u32[]{:S(2)}) collective-permute-start(bf16[4,1,16,512]{3,2,1,0:T(8,128)(2,1)S(1)} %get-tuple-element.83), channel_id=1, source_target_pairs={{0,4},{1,5},{2,6},{3,7},{4,0},{5,1},{6,2},{7,3},{8,12},{9,13},{10,... | collective-permute-start | bytes 196616 | tf_op jit(solution)/shard_map/ppermute | solution.py:23
  98.6 4.8 %collective-permute-start.32 = (bf16[16,1024]{1,0:T(8,128)(2,1)S(1)}, bf16[16,1024]{1,0:T(8,128)(2,1)S(1)}, u32[]{:S(2)}, u32[]{:S(2)}) collective-permute-start(bf16[16,1024]{1,0:T(8,128)(2,1)S(1)} %get-tuple-element.80), channel_id=1, source_target_pairs={{0,24},{8,16},{16,8},{24,0},{1,25},{9,17},{17,9},{25,1},{2,26},{10... | collective-permute-start | bytes 98312 | tf_op jit(solution)/shard_map/ppermute | solution.py:23
  (21 other events, 159.7 us)

commit v6 on v5

--- a/solution.py
+++ b/solution.py
@@ -117,7 +117,7 @@
 
 
 def stack_kernel(*refs):
-    for i, ref in enumerate(refs[:-1]):
+    for i, ref in enumerate(refs[-2::-1]):
         refs[-1][i, 0] = ref[...]
 
 
@@ -468,7 +468,7 @@
     rows, width = blocks[0].shape
     for d in range(out_ref.shape[0]):
         total = jnp.zeros((rows, width), jnp.float32)
-        for k, block in enumerate(blocks):
+        for k, block in enumerate(blocks[::-1]):
             chosen = jnp.concatenate([wide(home_ref[d, k], width)] * (rows // 8), 0)
             total = total + jnp.where(chosen > 0.0, block[...].astype(jnp.float32), 0.0)
         out_ref[d] = total.astype(jnp.bfloat16)
@@ -521,7 +521,7 @@
         limit=63,
         flops=WAIT,
     )
-    arrived = [block if k == 0 else swap(block, k, "pair") for k, block in enumerate(arrived)]
+    arrived = [arrived[k] if k == 0 else swap(arrived[k], k, "pair") for k in range(owners)[::-1]][::-1]
     if not direct:
         me = lax.axis_index("pair")
         taken = lax.dynamic_slice_in_dim(route, me, 1, 1)[:, 0] >= 0
@@ -539,9 +539,8 @@
     top = up_bits[0]
     early = join(early, swap(early, top, "tensor"))
     late = kernel_call(
-        stack_kernel, "stack", arrived[direct:], [bf16(slots - direct, 1, doc_rows, width)], flops=WAIT
+        stack_kernel, "stack", arrived[direct:][::-1], [bf16(slots - direct, 1, doc_rows, width)], flops=WAIT
     )[0]
-    late, early = tie(late, early)
     early = gather_blocks(early, up_bits[1:-1])
     first = project("project_early", 1, *spread(early), attn_gain, weights, ())
     late = gather_blocks(join(late, swap(late, top, "tensor")), up_bits[1:-1])
@@ -600,8 +599,8 @@
     if not direct:
         packed = jnp.einsum("sk,srd->krd", table, jnp.stack(blocks), preferred_element_type=jnp.float32)
         blocks = [packed[s].astype(jnp.bfloat16) for s in range(owners)]
-    blocks = [block if k == 0 else swap(block, k, "pair") for k, block in enumerate(blocks)]
-    return kernel_call(home_kernel, "home", (homes, *blocks), [bf16(doc_count, doc_rows, width)])[0]
+    blocks = [blocks[k] if k == 0 else swap(blocks[k], k, "pair") for k in range(owners)[::-1]][::-1]
+    return kernel_call(home_kernel, "home", (homes, *blocks[::-1]), [bf16(doc_count, doc_rows, width)])[0]
 
 
 def solution(mesh):

time: 104 us -> 104 us (level)
  waiting for transfers between devices: 24.5 us -> 22.3 us
  starting transfers between devices: 50.8 us -> 52.2 us
    ppermute x33, waiting for transfers between devices: 24.5 us -> 22.3 us  [swap(): return lax.ppermute(values, axis, [(i, i ^ bit) for i in range(count)])]
    ppermute x33, starting transfers between devices: 50.8 us -> 52.2 us  [swap(): return lax.ppermute(values, axis, [(i, i ^ bit) for i in range(count)])]
  transfers between devices with their start and end apart: 33 -> 33, of which waited for: 17 -> 16; matrix products, arithmetic and copies ran while one was open for 1% -> 1% of each run, Pallas kernels for 10% -> 10%
where the time goes in v6:
time: 104 us; the launch traced here: 103 us
  starting transfers between devices  52.2 us (50%)
  Pallas kernels  27.8 us (27%)
  waiting for transfers between devices  22.3 us (21%)
    ppermute x33, starting transfers between devices, swap(): return lax.ppermute(values, axis, [(i, i ^ bit) for i in range(count)])  52.2 us
    pallas_call x18, Pallas kernels, kernel_call(): pl.pallas_call(kernel, out_shape=out_shape, in_specs=[space(i in smem, i...  27.8 us
    ppermute x33, waiting for transfers between devices, swap(): return lax.ppermute(values, axis, [(i, i ^ bit) for i in range(count)])  22.3 us
  transfers between devices with their start and end apart: 33, of which 16 were waited for; matrix products, arithmetic and copies ran while one was open for 1% of the time, Pallas kernels for 10%

profile of v6, /device:TPU:0, one launch (start us, length us, event | category | flops | bytes accessed | tf_op | source)
XLA Modules:
  0.0 103.3 jit_solution(8371823877103959782)
XLA Ops:
  1.7 4.0 %collective-permute-start = (bf16[16,1024]{1,0:T(8,128)(2,1)}, bf16[16,1024]{1,0:T(8,128)(2,1)S(1)}, u32[]{:S(2)}, u32[]{:S(2)}) collective-permute-start(bf16[16,1024]{1,0:T(8,128)(2,1)} %get-tuple-element.42), channel_id=1, source_target_pairs={{0,24},{8,16},{16,8},{24,0},{1,25},{9,17},{17,9},{25,1},{2,26},{10... | collective-permute-start | bytes 98312 | tf_op jit(solution)/shard_map/ppermute | solution.py:23
  6.3 3.0 %collective-permute-start.5 = (bf16[2,1,16,1024]{3,2,1,0:T(8,128)(2,1)}, bf16[2,1,16,1024]{3,2,1,0:T(8,128)(2,1)S(1)}, u32[]{:S(2)}, u32[]{:S(2)}) collective-permute-start(bf16[2,1,16,1024]{3,2,1,0:T(8,128)(2,1)} %get-tuple-element.45.kept_ref), channel_id=1, source_target_pairs={{0,4},{1,5},{2,6},{3,7},{4,0},{5,1},{6,2},{7,3},{8,12},{9,13},{10,... | collective-permute-start | bytes 196616 | tf_op jit(solution)/shard_map/ppermute | solution.py:23
  10.3 2.7 %collective-permute-start.3 = (bf16[3,1,16,1024]{3,2,1,0:T(8,128)(2,1)S(1)}, bf16[3,1,16,1024]{3,2,1,0:T(8,128)(2,1)S(1)}, u32[]{:S(2)}, u32[]{:S(2)}) collective-permute-start(bf16[3,1,16,1024]{3,2,1,0:T(8,128)(2,1)S(1)} %stack.1.kept_ref), channel_id=1, source_target_pairs={{0,4},{1,5},{2,6},{3,7},{4,0},{5,1},{6,2},{7,3},{8,12},{9,13},{10,... | collective-permute-start | bytes 294920 | tf_op jit(solution)/shard_map/ppermute | solution.py:23
  13.0 2.4 %collective-permute-start.6 = (bf16[2,2,16,1024]{3,2,1,0:T(8,128)(2,1)S(1)}, bf16[2,2,16,1024]{3,2,1,0:T(8,128)(2,1)S(1)}, u32[]{:S(2)}, u32[]{:S(2)}) collective-permute-start(bf16[2,2,16,1024]{3,2,1,0:T(8,128)(2,1)S(1)} %join.3), channel_id=1, source_target_pairs={{0,2},{1,3},{2,0},{3,1},{4,6},{5,7},{6,4},{7,5},{8,10},{9,11},{10,... | collective-permute-start | bytes 393224 | tf_op jit(solution)/shard_map/ppermute | solution.py:23
  16.0 2.1 %collective-permute-start.4 = (bf16[3,2,16,1024]{3,2,1,0:T(8,128)(2,1)S(1)}, bf16[3,2,16,1024]{3,2,1,0:T(8,128)(2,1)S(1)}, u32[]{:S(2)}, u32[]{:S(2)}) collective-permute-start(bf16[3,2,16,1024]{3,2,1,0:T(8,128)(2,1)S(1)} %join.2), channel_id=1, source_target_pairs={{0,2},{1,3},{2,0},{3,1},{4,6},{5,7},{6,4},{7,5},{8,10},{9,11},{10,... | collective-permute-start | bytes 589832 | tf_op jit(solution)/shard_map/ppermute | solution.py:23
  19.3 3.2 %collective-permute-done.4 = bf16[3,2,16,1024]{3,2,1,0:T(8,128)(2,1)S(1)} collective-permute-done((bf16[3,2,16,1024]{3,2,1,0:T(8,128)(2,1)S(1)}, bf16[3,2,16,1024]{3,2,1,0:T(8,128)(2,1)S(1)}, u32[]{:S(2)}, u32[]{:S(2)}) %collective-permute-start.4) | collective-permute-done | bytes 196640 | tf_op jit(solution)/shard_map/ppermute | solution.py:23
  27.6 5.0 %attend.1 = (bf16[2,8,16,1024]{3,2,1,0:T(8,128)(2,1)S(1)}, bf16[512,1024]{1,0:T(8,128)(2,1)S(1)}, bf16[3,2,2,16,1024]{4,3,2,1,0:T(8,128)(2,1)S(1)}, f32[6,4,8,12...) custom-call(s32[4,6]{1,0:T(4,128)S(1)} %copy-done.5, ...), custom_call_target="tpu_custom_call" | custom-call | flops 1744830464 | bytes 2097152 | tf_op jit(solution)/shard_map/attend/pallas_call | solution.py:54
  36.7 3.2 %collective-permute-start.16 = (bf16[2,2,16,1024]{3,2,1,0:T(8,128)(2,1)S(1)}, bf16[2,2,16,1024]{3,2,1,0:T(8,128)(2,1)S(1)}, u32[]{:S(2)}, u32[]{:S(2)}) collective-permute-start(bf16[2,2,16,1024]{3,2,1,0:T(8,128)(2,1)S(1)} %slice.101), channel_id=1, source_target_pairs={{0,4},{1,5},{2,6},{3,7},{4,0},{5,1},{6,2},{7,3},{8,12},{9,13},{10,... | collective-permute-start | bytes 393224 | tf_op jit(solution)/shard_map/ppermute | solution.py:23
  40.9 3.6 %collective-permute-start.11 = (bf16[2,2,16,1024]{3,2,1,0:T(8,128)(2,1)S(1)}, bf16[2,2,16,1024]{3,2,1,0:T(8,128)(2,1)S(1)}, u32[]{:S(2)}, u32[]{:S(2)}) collective-permute-start(bf16[2,2,16,1024]{3,2,1,0:T(8,128)(2,1)S(1)} %slice_add_fusion.9.kept_ref), channel_id=1, source_target_pairs={{0,4},{1,5},{2,6},{3,7},{4,0},{5,1},{6,2},{7,3},{8,12},{9,13},{10,... | collective-permute-start | bytes 393224 | tf_op jit(solution)/shard_map/ppermute | solution.py:23
  44.5 1.9 %collective-permute-done.16 = bf16[2,2,16,1024]{3,2,1,0:T(8,128)(2,1)S(1)} collective-permute-done((bf16[2,2,16,1024]{3,2,1,0:T(8,128)(2,1)S(1)}, bf16[2,2,16,1024]{3,2,1,0:T(8,128)(2,1)S(1)}, u32[]{:S(2)}, u32[]{:S(2)}) %collective-permute-start.16) | collective-permute-done | bytes 131104 | tf_op jit(solution)/shard_map/ppermute | solution.py:23
  47.8 3.9 %collective-permute-start.14 = (bf16[2,2,16,1024]{3,2,1,0:T(8,128)(2,1)S(1)}, bf16[2,2,16,1024]{3,2,1,0:T(8,128)(2,1)S(1)}, u32[]{:S(2)}, u32[]{:S(2)}) collective-permute-start(bf16[2,2,16,1024]{3,2,1,0:T(8,128)(2,1)S(1)} %slice_add_fusion.8.kept_ref), channel_id=1, source_target_pairs={{0,4},{1,5},{2,6},{3,7},{4,0},{5,1},{6,2},{7,3},{8,12},{9,13},{10,... | collective-permute-start | bytes 393224 | tf_op jit(solution)/shard_map/ppermute | solution.py:23
  53.7 3.9 %collective-permute-start.22 = (bf16[2,2,16,1024]{3,2,1,0:T(8,128)(2,1)S(1)}, bf16[2,2,16,1024]{3,2,1,0:T(8,128)(2,1)S(1)}, u32[]{:S(2)}, u32[]{:S(2)}) collective-permute-start(bf16[2,2,16,1024]{3,2,1,0:T(8,128)(2,1)S(1)} %get-tuple-element.72), channel_id=1, source_target_pairs={{0,4},{1,5},{2,6},{3,7},{4,0},{5,1},{6,2},{7,3},{8,12},{9,13},{10,... | collective-permute-start | bytes 393224 | tf_op jit(solution)/shard_map/ppermute | solution.py:23
  59.7 2.8 %collective-permute-done.22 = bf16[2,2,16,1024]{3,2,1,0:T(8,128)(2,1)S(1)} collective-permute-done((bf16[2,2,16,1024]{3,2,1,0:T(8,128)(2,1)S(1)}, bf16[2,2,16,1024]{3,2,1,0:T(8,128)(2,1)S(1)}, u32[]{:S(2)}, u32[]{:S(2)}) %collective-permute-start.22) | collective-permute-done | bytes 131104 | tf_op jit(solution)/shard_map/ppermute | solution.py:23
  63.6 4.5 %expand.2.refs_3_ = bf16[1,4,64,4096]{3,2,1,0:T(8,128)(2,1)S(1)} custom-call(s32[4,6]{1,0:T(4,128)S(1)} %copy-done.5, bf16[1024,4096]{1,0:T(8,128)(2,1)S(1)} %bitcast.5, bf16[2,4,16,1024]{3,2,1,0:T(8,128)(2,1)S(1)} %constant_dynamic-update-slice_fusion.refs_0_, bf16[2,4,16,1024]{3,2,1,0:T(8,128)(2,1)S(1)} %constant_dynamic-update-slice_fusion.2.refs_1_, ...), custom_call_target="tpu_custom_call" | custom-call | flops 3221225472 | bytes 8388608 | tf_op jit(solution)/shard_map/expand/pallas_call | solution.py:54
  68.1 4.5 %expand.3.units_ref = bf16[2,4,64,4096]{3,2,1,0:T(8,128)(2,1)S(1)} custom-call(s32[4,6]{1,0:T(4,128)S(1)} %copy-done.5, bf16[1024,4096]{1,0:T(8,128)(2,1)S(1)} %bitcast.5, bf16[2,4,16,1024]{3,2,1,0:T(8,128)(2,1)S(1)} %collective-permute-done.19.refs_0_, bf16[2,4,16,1024]{3,2,1,0:T(8,128)(2,1)S(1)} %collective-permute-done.21.refs_1_, ...), custom_call_target="tpu_custom_call" | custom-call | flops 3221225472 | bytes 8388608 | tf_op jit(solution)/shard_map/expand/pallas_call | solution.py:54
  72.7 2.3 %shrink.3 = bf16[4,8,16,512]{3,2,1,0:T(8,128)(2,1)S(1)} custom-call(bf16[2,4,64,4096]{3,2,1,0:T(8,128)(2,1)S(1)} %expand.3.units_ref, bf16[4096,1024]{1,0:T(8,128)(2,1)S(1)} %bitcast.3), custom_call_target="tpu_custom_call" | custom-call | flops 2147483648 | bytes 4194304 | tf_op jit(solution)/shard_map/shrink/pallas_call | solution.py:54
  75.6 2.3 %shrink.2 = bf16[4,8,16,512]{3,2,1,0:T(8,128)(2,1)S(1)} custom-call(bf16[2,4,64,4096]{3,2,1,0:T(8,128)(2,1)S(1)} %expand.3.units_ref, bf16[4096,1024]{1,0:T(8,128)(2,1)S(1)} %bitcast.3), custom_call_target="tpu_custom_call" | custom-call | flops 2147483648 | bytes 4194304 | tf_op jit(solution)/shard_map/shrink/pallas_call | solution.py:54
  78.1 1.7 %collective-permute-start.28 = (bf16[4,2,16,512]{3,2,1,0:T(8,128)(2,1)S(1)}, bf16[4,2,16,512]{3,2,1,0:T(8,128)(2,1)S(1)}, u32[]{:S(2)}, u32[]{:S(2)}) collective-permute-start(bf16[4,2,16,512]{3,2,1,0:T(8,128)(2,1)S(1)} %slice.111), channel_id=1, source_target_pairs={{0,2},{1,3},{2,0},{3,1},{4,6},{5,7},{6,4},{7,5},{8,10},{9,11},{10,... | collective-permute-start | bytes 393224 | tf_op jit(solution)/shard_map/ppermute | solution.py:23
  81.2 3.3 %collective-permute-done.28 = bf16[4,2,16,512]{3,2,1,0:T(8,128)(2,1)S(1)} collective-permute-done((bf16[4,2,16,512]{3,2,1,0:T(8,128)(2,1)S(1)}, bf16[4,2,16,512]{3,2,1,0:T(8,128)(2,1)S(1)}, u32[]{:S(2)}, u32[]{:S(2)}) %collective-permute-start.28) | collective-permute-done | bytes 131104 | tf_op jit(solution)/shard_map/ppermute | solution.py:23
  84.5 3.5 %collective-permute-start.29 = (bf16[4,1,16,512]{3,2,1,0:T(8,128)(2,1)S(1)}, bf16[4,1,16,512]{3,2,1,0:T(8,128)(2,1)S(1)}, u32[]{:S(2)}, u32[]{:S(2)}) collective-permute-start(bf16[4,1,16,512]{3,2,1,0:T(8,128)(2,1)S(1)} %get-tuple-element.77), channel_id=1, source_target_pairs={{0,4},{1,5},{2,6},{3,7},{4,0},{5,1},{6,2},{7,3},{8,12},{9,13},{10,... | collective-permute-start | bytes 196616 | tf_op jit(solution)/shard_map/ppermute | solution.py:23
  88.1 2.8 %collective-permute-start.26 = (bf16[4,1,16,512]{3,2,1,0:T(8,128)(2,1)S(1)}, bf16[4,1,16,512]{3,2,1,0:T(8,128)(2,1)S(1)}, u32[]{:S(2)}, u32[]{:S(2)}) collective-permute-start(bf16[4,1,16,512]{3,2,1,0:T(8,128)(2,1)S(1)} %get-tuple-element.79), channel_id=1, source_target_pairs={{0,4},{1,5},{2,6},{3,7},{4,0},{5,1},{6,2},{7,3},{8,12},{9,13},{10,... | collective-permute-start | bytes 196616 | tf_op jit(solution)/shard_map/ppermute | solution.py:23
  91.7 2.1 %collective-permute-done.26.refs_1_ = bf16[4,1,16,512]{3,2,1,0:T(8,128)(2,1)S(1)} collective-permute-done((bf16[4,1,16,512]{3,2,1,0:T(8,128)(2,1)S(1)}, bf16[4,1,16,512]{3,2,1,0:T(8,128)(2,1)S(1)}, u32[]{:S(2)}, u32[]{:S(2)}) %collective-permute-start.26) | collective-permute-done | bytes 65568 | tf_op jit(solution)/shard_map/ppermute | solution.py:23
  93.9 3.7 %collective-permute-start.30 = (bf16[16,1024]{1,0:T(8,128)(2,1)S(1)}, bf16[16,1024]{1,0:T(8,128)(2,1)S(1)}, u32[]{:S(2)}, u32[]{:S(2)}) collective-permute-start(bf16[16,1024]{1,0:T(8,128)(2,1)S(1)} %get-tuple-element.73), channel_id=1, source_target_pairs={{0,24},{8,16},{16,8},{24,0},{1,25},{9,17},{17,9},{25,1},{2,26},{10... | collective-permute-start | bytes 98312 | tf_op jit(solution)/shard_map/ppermute | solution.py:23
  99.5 2.0 %collective-permute-done.31.refs_1_ = bf16[16,1024]{1,0:T(8,128)(2,1)S(1)} collective-permute-done((bf16[16,1024]{1,0:T(8,128)(2,1)S(1)}, bf16[16,1024]{1,0:T(8,128)(2,1)S(1)}, u32[]{:S(2)}, u32[]{:S(2)}) %collective-permute-start.31) | collective-permute-done | bytes 32800 | tf_op jit(solution)/shard_map/ppermute | solution.py:23
  (117 shorter events, 28.3 us)
Async XLA Ops:
  1.7 7.6 %collective-permute-start = (bf16[16,1024]{1,0:T(8,128)(2,1)}, bf16[16,1024]{1,0:T(8,128)(2,1)S(1)}, u32[]{:S(2)}, u32[]{:S(2)}) collective-permute-start(bf16[16,1024]{1,0:T(8,128)(2,1)} %get-tuple-element.42), channel_id=1, source_target_pairs={{0,24},{8,16},{16,8},{24,0},{1,25},{9,17},{17,9},{25,1},{2,26},{10... | collective-permute-start | bytes 98312 | tf_op jit(solution)/shard_map/ppermute | solution.py:23
  5.6 4.1 %collective-permute-start.1 = (bf16[16,1024]{1,0:T(8,128)(2,1)}, bf16[16,1024]{1,0:T(8,128)(2,1)S(1)}, u32[]{:S(2)}, u32[]{:S(2)}) collective-permute-start(bf16[16,1024]{1,0:T(8,128)(2,1)} %get-tuple-element.43), channel_id=1, source_target_pairs={{0,16},{8,24},{16,0},{24,8},{1,17},{9,25},{17,1},{25,9},{2,18},{10... | collective-permute-start | bytes 98312 | tf_op jit(solution)/shard_map/ppermute | solution.py:23
  6.3 6.7 %collective-permute-start.5 = (bf16[2,1,16,1024]{3,2,1,0:T(8,128)(2,1)}, bf16[2,1,16,1024]{3,2,1,0:T(8,128)(2,1)S(1)}, u32[]{:S(2)}, u32[]{:S(2)}) collective-permute-start(bf16[2,1,16,1024]{3,2,1,0:T(8,128)(2,1)} %get-tuple-element.45.kept_ref), channel_id=1, source_target_pairs={{0,4},{1,5},{2,6},{3,7},{4,0},{5,1},{6,2},{7,3},{8,12},{9,13},{10,... | collective-permute-start | bytes 196616 | tf_op jit(solution)/shard_map/ppermute | solution.py:23
  10.3 5.7 %collective-permute-start.3 = (bf16[3,1,16,1024]{3,2,1,0:T(8,128)(2,1)S(1)}, bf16[3,1,16,1024]{3,2,1,0:T(8,128)(2,1)S(1)}, u32[]{:S(2)}, u32[]{:S(2)}) collective-permute-start(bf16[3,1,16,1024]{3,2,1,0:T(8,128)(2,1)S(1)} %stack.1.kept_ref), channel_id=1, source_target_pairs={{0,4},{1,5},{2,6},{3,7},{4,0},{5,1},{6,2},{7,3},{8,12},{9,13},{10,... | collective-permute-start | bytes 294920 | tf_op jit(solution)/shard_map/ppermute | solution.py:23
  13.0 6.2 %collective-permute-start.6 = (bf16[2,2,16,1024]{3,2,1,0:T(8,128)(2,1)S(1)}, bf16[2,2,16,1024]{3,2,1,0:T(8,128)(2,1)S(1)}, u32[]{:S(2)}, u32[]{:S(2)}) collective-permute-start(bf16[2,2,16,1024]{3,2,1,0:T(8,128)(2,1)S(1)} %join.3), channel_id=1, source_target_pairs={{0,2},{1,3},{2,0},{3,1},{4,6},{5,7},{6,4},{7,5},{8,10},{9,11},{10,... | collective-permute-start | bytes 393224 | tf_op jit(solution)/shard_map/ppermute | solution.py:23
  16.0 6.5 %collective-permute-start.4 = (bf16[3,2,16,1024]{3,2,1,0:T(8,128)(2,1)S(1)}, bf16[3,2,16,1024]{3,2,1,0:T(8,128)(2,1)S(1)}, u32[]{:S(2)}, u32[]{:S(2)}) collective-permute-start(bf16[3,2,16,1024]{3,2,1,0:T(8,128)(2,1)S(1)} %join.2), channel_id=1, source_target_pairs={{0,2},{1,3},{2,0},{3,1},{4,6},{5,7},{6,4},{7,5},{8,10},{9,11},{10,... | collective-permute-start | bytes 589832 | tf_op jit(solution)/shard_map/ppermute | solution.py:23
  34.7 5.3 %collective-permute-start.12 = (bf16[2,4,16,1024]{3,2,1,0:T(8,128)(2,1)S(1)}, bf16[2,4,16,1024]{3,2,1,0:T(8,128)(2,1)S(1)}, u32[]{:S(2)}, u32[]{:S(2)}) collective-permute-start(bf16[2,4,16,1024]{3,2,1,0:T(8,128)(2,1)S(1)} %slice.77), channel_id=1, source_target_pairs={{0,1},{1,0},{2,3},{3,2},{4,5},{5,4},{6,7},{7,6},{8,9},{9,8},{10,11... | collective-permute-start | bytes 786440 | tf_op jit(solution)/shard_map/ppermute | solution.py:23
  35.1 5.8 %collective-permute-start.10 = (bf16[2,2,16,1024]{3,2,1,0:T(8,128)(2,1)S(1)}, bf16[2,2,16,1024]{3,2,1,0:T(8,128)(2,1)S(1)}, u32[]{:S(2)}, u32[]{:S(2)}) collective-permute-start(bf16[2,2,16,1024]{3,2,1,0:T(8,128)(2,1)S(1)} %slice.97), channel_id=1, source_target_pairs={{0,2},{1,3},{2,0},{3,1},{4,6},{5,7},{6,4},{7,5},{8,10},{9,11},{10,... | collective-permute-start | bytes 393224 | tf_op jit(solution)/shard_map/ppermute | solution.py:23
  36.7 9.7 %collective-permute-start.16 = (bf16[2,2,16,1024]{3,2,1,0:T(8,128)(2,1)S(1)}, bf16[2,2,16,1024]{3,2,1,0:T(8,128)(2,1)S(1)}, u32[]{:S(2)}, u32[]{:S(2)}) collective-permute-start(bf16[2,2,16,1024]{3,2,1,0:T(8,128)(2,1)S(1)} %slice.101), channel_id=1, source_target_pairs={{0,4},{1,5},{2,6},{3,7},{4,0},{5,1},{6,2},{7,3},{8,12},{9,13},{10,... | collective-permute-start | bytes 393224 | tf_op jit(solution)/shard_map/ppermute | solution.py:23
  40.0 7.7 %collective-permute-start.13 = (bf16[2,2,16,1024]{3,2,1,0:T(8,128)(2,1)S(1)}, bf16[2,2,16,1024]{3,2,1,0:T(8,128)(2,1)S(1)}, u32[]{:S(2)}, u32[]{:S(2)}) collective-permute-start(bf16[2,2,16,1024]{3,2,1,0:T(8,128)(2,1)S(1)} %slice.99), channel_id=1, source_target_pairs={{0,2},{1,3},{2,0},{3,1},{4,6},{5,7},{6,4},{7,5},{8,10},{9,11},{10,... | collective-permute-start | bytes 393224 | tf_op jit(solution)/shard_map/ppermute | solution.py:23
  40.9 11.1 %collective-permute-start.11 = (bf16[2,2,16,1024]{3,2,1,0:T(8,128)(2,1)S(1)}, bf16[2,2,16,1024]{3,2,1,0:T(8,128)(2,1)S(1)}, u32[]{:S(2)}, u32[]{:S(2)}) collective-permute-start(bf16[2,2,16,1024]{3,2,1,0:T(8,128)(2,1)S(1)} %slice_add_fusion.9.kept_ref), channel_id=1, source_target_pairs={{0,4},{1,5},{2,6},{3,7},{4,0},{5,1},{6,2},{7,3},{8,12},{9,13},{10,... | collective-permute-start | bytes 393224 | tf_op jit(solution)/shard_map/ppermute | solution.py:23
  46.5 7.1 %collective-permute-start.17 = (bf16[2,2,16,1024]{3,2,1,0:T(8,128)(2,1)S(1)}, bf16[2,2,16,1024]{3,2,1,0:T(8,128)(2,1)S(1)}, u32[]{:S(2)}, u32[]{:S(2)}) collective-permute-start(bf16[2,2,16,1024]{3,2,1,0:T(8,128)(2,1)S(1)} %slice_add_fusion.7.kept_ref), channel_id=1, source_target_pairs={{0,2},{1,3},{2,0},{3,1},{4,6},{5,7},{6,4},{7,5},{8,10},{9,11},{10,... | collective-permute-start | bytes 393224 | tf_op jit(solution)/shard_map/ppermute | solution.py:23
  47.8 9.9 %collective-permute-start.14 = (bf16[2,2,16,1024]{3,2,1,0:T(8,128)(2,1)S(1)}, bf16[2,2,16,1024]{3,2,1,0:T(8,128)(2,1)S(1)}, u32[]{:S(2)}, u32[]{:S(2)}) collective-permute-start(bf16[2,2,16,1024]{3,2,1,0:T(8,128)(2,1)S(1)} %slice_add_fusion.8.kept_ref), channel_id=1, source_target_pairs={{0,4},{1,5},{2,6},{3,7},{4,0},{5,1},{6,2},{7,3},{8,12},{9,13},{10,... | collective-permute-start | bytes 393224 | tf_op jit(solution)/shard_map/ppermute | solution.py:23
  52.2 7.4 %collective-permute-start.18 = (bf16[2,2,16,1024]{3,2,1,0:T(8,128)(2,1)S(1)}, bf16[2,2,16,1024]{3,2,1,0:T(8,128)(2,1)S(1)}, u32[]{:S(2)}, u32[]{:S(2)}) collective-permute-start(bf16[2,2,16,1024]{3,2,1,0:T(8,128)(2,1)S(1)} %get-tuple-element.70), channel_id=1, source_target_pairs={{0,2},{1,3},{2,0},{3,1},{4,6},{5,7},{6,4},{7,5},{8,10},{9,11},{10,... | collective-permute-start | bytes 393224 | tf_op jit(solution)/shard_map/ppermute | solution.py:23
  53.7 8.8 %collective-permute-start.22 = (bf16[2,2,16,1024]{3,2,1,0:T(8,128)(2,1)S(1)}, bf16[2,2,16,1024]{3,2,1,0:T(8,128)(2,1)S(1)}, u32[]{:S(2)}, u32[]{:S(2)}) collective-permute-start(bf16[2,2,16,1024]{3,2,1,0:T(8,128)(2,1)S(1)} %get-tuple-element.72), channel_id=1, source_target_pairs={{0,4},{1,5},{2,6},{3,7},{4,0},{5,1},{6,2},{7,3},{8,12},{9,13},{10,... | collective-permute-start | bytes 393224 | tf_op jit(solution)/shard_map/ppermute | solution.py:23
  57.8 5.7 %collective-permute-start.20 = (bf16[2,2,16,1024]{3,2,1,0:T(8,128)(2,1)S(1)}, bf16[2,2,16,1024]{3,2,1,0:T(8,128)(2,1)S(1)}, u32[]{:S(2)}, u32[]{:S(2)}) collective-permute-start(bf16[2,2,16,1024]{3,2,1,0:T(8,128)(2,1)S(1)} %get-tuple-element.71), channel_id=1, source_target_pairs={{0,2},{1,3},{2,0},{3,1},{4,6},{5,7},{6,4},{7,5},{8,10},{9,11},{10,... | collective-permute-start | bytes 393224 | tf_op jit(solution)/shard_map/ppermute | solution.py:23
  59.6 8.5 %collective-permute-start.19 = (bf16[2,4,16,1024]{3,2,1,0:T(8,128)(2,1)S(1)}, bf16[2,4,16,1024]{3,2,1,0:T(8,128)(2,1)S(1)}, u32[]{:S(2)}, u32[]{:S(2)}) collective-permute-start(bf16[2,4,16,1024]{3,2,1,0:T(8,128)(2,1)S(1)} %constant_dynamic-update-slice_fusion.refs_0_), channel_id=1, source_target_pairs={{0,1},{1,0},{2,3},{3,2},{4,5},{5,4},{6,7},{7,6},{8,9},{9,8},{10,11... | collective-permute-start | bytes 786440 | tf_op jit(solution)/shard_map/ppermute | solution.py:23
  62.5 5.6 %collective-permute-start.23 = (bf16[2,4,16,1024]{3,2,1,0:T(8,128)(2,1)S(1)}, bf16[2,4,16,1024]{3,2,1,0:T(8,128)(2,1)S(1)}, u32[]{:S(2)}, u32[]{:S(2)}) collective-permute-start(bf16[2,4,16,1024]{3,2,1,0:T(8,128)(2,1)S(1)} %constant_dynamic-update-slice_fusion.4.refs_2_), channel_id=1, source_target_pairs={{0,1},{1,0},{2,3},{3,2},{4,5},{5,4},{6,7},{7,6},{8,9},{9,8},{10,11... | collective-permute-start | bytes 786440 | tf_op jit(solution)/shard_map/ppermute | solution.py:23
  63.5 4.6 %collective-permute-start.21 = (bf16[2,4,16,1024]{3,2,1,0:T(8,128)(2,1)S(1)}, bf16[2,4,16,1024]{3,2,1,0:T(8,128)(2,1)S(1)}, u32[]{:S(2)}, u32[]{:S(2)}) collective-permute-start(bf16[2,4,16,1024]{3,2,1,0:T(8,128)(2,1)S(1)} %constant_dynamic-update-slice_fusion.2.refs_1_), channel_id=1, source_target_pairs={{0,1},{1,0},{2,3},{3,2},{4,5},{5,4},{6,7},{7,6},{8,9},{9,8},{10,11... | collective-permute-start | bytes 786440 | tf_op jit(solution)/shard_map/ppermute | solution.py:23
  78.1 6.4 %collective-permute-start.28 = (bf16[4,2,16,512]{3,2,1,0:T(8,128)(2,1)S(1)}, bf16[4,2,16,512]{3,2,1,0:T(8,128)(2,1)S(1)}, u32[]{:S(2)}, u32[]{:S(2)}) collective-permute-start(bf16[4,2,16,512]{3,2,1,0:T(8,128)(2,1)S(1)} %slice.111), channel_id=1, source_target_pairs={{0,2},{1,3},{2,0},{3,1},{4,6},{5,7},{6,4},{7,5},{8,10},{9,11},{10,... | collective-permute-start | bytes 393224 | tf_op jit(solution)/shard_map/ppermute | solution.py:23
  79.9 8.1 %collective-permute-start.25 = (bf16[4,2,16,512]{3,2,1,0:T(8,128)(2,1)S(1)}, bf16[4,2,16,512]{3,2,1,0:T(8,128)(2,1)S(1)}, u32[]{:S(2)}, u32[]{:S(2)}) collective-permute-start(bf16[4,2,16,512]{3,2,1,0:T(8,128)(2,1)S(1)} %slice.105), channel_id=1, source_target_pairs={{0,2},{1,3},{2,0},{3,1},{4,6},{5,7},{6,4},{7,5},{8,10},{9,11},{10,... | collective-permute-start | bytes 393224 | tf_op jit(solution)/shard_map/ppermute | solution.py:23
  84.5 7.1 %collective-permute-start.29 = (bf16[4,1,16,512]{3,2,1,0:T(8,128)(2,1)S(1)}, bf16[4,1,16,512]{3,2,1,0:T(8,128)(2,1)S(1)}, u32[]{:S(2)}, u32[]{:S(2)}) collective-permute-start(bf16[4,1,16,512]{3,2,1,0:T(8,128)(2,1)S(1)} %get-tuple-element.77), channel_id=1, source_target_pairs={{0,4},{1,5},{2,6},{3,7},{4,0},{5,1},{6,2},{7,3},{8,12},{9,13},{10,... | collective-permute-start | bytes 196616 | tf_op jit(solution)/shard_map/ppermute | solution.py:23
  88.1 5.7 %collective-permute-start.26 = (bf16[4,1,16,512]{3,2,1,0:T(8,128)(2,1)S(1)}, bf16[4,1,16,512]{3,2,1,0:T(8,128)(2,1)S(1)}, u32[]{:S(2)}, u32[]{:S(2)}) collective-permute-start(bf16[4,1,16,512]{3,2,1,0:T(8,128)(2,1)S(1)} %get-tuple-element.79), channel_id=1, source_target_pairs={{0,4},{1,5},{2,6},{3,7},{4,0},{5,1},{6,2},{7,3},{8,12},{9,13},{10,... | collective-permute-start | bytes 196616 | tf_op jit(solution)/shard_map/ppermute | solution.py:23
  93.9 5.6 %collective-permute-start.30 = (bf16[16,1024]{1,0:T(8,128)(2,1)S(1)}, bf16[16,1024]{1,0:T(8,128)(2,1)S(1)}, u32[]{:S(2)}, u32[]{:S(2)}) collective-permute-start(bf16[16,1024]{1,0:T(8,128)(2,1)S(1)} %get-tuple-element.73), channel_id=1, source_target_pairs={{0,24},{8,16},{16,8},{24,0},{1,25},{9,17},{17,9},{25,1},{2,26},{10... | collective-permute-start | bytes 98312 | tf_op jit(solution)/shard_map/ppermute | solution.py:23
  (21 other events, 163.2 us)

commit v7 on v6

--- a/solution.py
+++ b/solution.py
@@ -404,7 +404,7 @@
     units = w_in.shape[1]
     roles = sum(piece.shape[0] for piece in pieces)
     return kernel_call(
-        functools.partial(expand_kernel, swapped, min(512, units)),
+        functools.partial(expand_kernel, swapped, min(1024, units)),
         "expand",
         (meta, w_in, *pieces, *old),
         [bf16(1 + len(old), slots, half * rows, units)],

time: 104 us -> 103 us (level)
  no operation moved by 1% of the time
where the time goes in v7:
time: 103 us
  starting transfers between devices  52.2 us (51%)
  Pallas kernels  27.3 us (27%)
  waiting for transfers between devices  22.2 us (22%)
    ppermute x33, starting transfers between devices, swap(): return lax.ppermute(values, axis, [(i, i ^ bit) for i in range(count)])  52.2 us
    pallas_call x18, Pallas kernels, kernel_call(): pl.pallas_call(kernel, out_shape=out_shape, in_specs=[space(i in smem, i...  27.3 us
    ppermute x33, waiting for transfers between devices, swap(): return lax.ppermute(values, axis, [(i, i ^ bit) for i in range(count)])  22.2 us
  transfers between devices with their start and end apart: 33, of which 16 were waited for; matrix products, arithmetic and copies ran while one was open for 1% of the time, Pallas kernels for 10%

profile of v7, /device:TPU:0, one launch (start us, length us, event | category | flops | bytes accessed | tf_op | source)
XLA Modules:
  0.0 102.9 jit_solution(1133276091924656690)
XLA Ops:
  1.7 4.0 %collective-permute-start = (bf16[16,1024]{1,0:T(8,128)(2,1)}, bf16[16,1024]{1,0:T(8,128)(2,1)S(1)}, u32[]{:S(2)}, u32[]{:S(2)}) collective-permute-start(bf16[16,1024]{1,0:T(8,128)(2,1)} %get-tuple-element.42), channel_id=1, source_target_pairs={{0,24},{8,16},{16,8},{24,0},{1,25},{9,17},{17,9},{25,1},{2,26},{10... | collective-permute-start | bytes 98312 | tf_op jit(solution)/shard_map/ppermute | solution.py:23
  6.3 3.0 %collective-permute-start.5 = (bf16[2,1,16,1024]{3,2,1,0:T(8,128)(2,1)}, bf16[2,1,16,1024]{3,2,1,0:T(8,128)(2,1)S(1)}, u32[]{:S(2)}, u32[]{:S(2)}) collective-permute-start(bf16[2,1,16,1024]{3,2,1,0:T(8,128)(2,1)} %get-tuple-element.45.kept_ref), channel_id=1, source_target_pairs={{0,4},{1,5},{2,6},{3,7},{4,0},{5,1},{6,2},{7,3},{8,12},{9,13},{10,... | collective-permute-start | bytes 196616 | tf_op jit(solution)/shard_map/ppermute | solution.py:23
  10.3 2.7 %collective-permute-start.3 = (bf16[3,1,16,1024]{3,2,1,0:T(8,128)(2,1)S(1)}, bf16[3,1,16,1024]{3,2,1,0:T(8,128)(2,1)S(1)}, u32[]{:S(2)}, u32[]{:S(2)}) collective-permute-start(bf16[3,1,16,1024]{3,2,1,0:T(8,128)(2,1)S(1)} %stack.1.kept_ref), channel_id=1, source_target_pairs={{0,4},{1,5},{2,6},{3,7},{4,0},{5,1},{6,2},{7,3},{8,12},{9,13},{10,... | collective-permute-start | bytes 294920 | tf_op jit(solution)/shard_map/ppermute | solution.py:23
  13.0 2.4 %collective-permute-start.6 = (bf16[2,2,16,1024]{3,2,1,0:T(8,128)(2,1)S(1)}, bf16[2,2,16,1024]{3,2,1,0:T(8,128)(2,1)S(1)}, u32[]{:S(2)}, u32[]{:S(2)}) collective-permute-start(bf16[2,2,16,1024]{3,2,1,0:T(8,128)(2,1)S(1)} %join.3), channel_id=1, source_target_pairs={{0,2},{1,3},{2,0},{3,1},{4,6},{5,7},{6,4},{7,5},{8,10},{9,11},{10,... | collective-permute-start | bytes 393224 | tf_op jit(solution)/shard_map/ppermute | solution.py:23
  16.0 2.1 %collective-permute-start.4 = (bf16[3,2,16,1024]{3,2,1,0:T(8,128)(2,1)S(1)}, bf16[3,2,16,1024]{3,2,1,0:T(8,128)(2,1)S(1)}, u32[]{:S(2)}, u32[]{:S(2)}) collective-permute-start(bf16[3,2,16,1024]{3,2,1,0:T(8,128)(2,1)S(1)} %join.2), channel_id=1, source_target_pairs={{0,2},{1,3},{2,0},{3,1},{4,6},{5,7},{6,4},{7,5},{8,10},{9,11},{10,... | collective-permute-start | bytes 589832 | tf_op jit(solution)/shard_map/ppermute | solution.py:23
  19.3 3.2 %collective-permute-done.4 = bf16[3,2,16,1024]{3,2,1,0:T(8,128)(2,1)S(1)} collective-permute-done((bf16[3,2,16,1024]{3,2,1,0:T(8,128)(2,1)S(1)}, bf16[3,2,16,1024]{3,2,1,0:T(8,128)(2,1)S(1)}, u32[]{:S(2)}, u32[]{:S(2)}) %collective-permute-start.4) | collective-permute-done | bytes 196640 | tf_op jit(solution)/shard_map/ppermute | solution.py:23
  27.6 5.0 %attend.1 = (bf16[2,8,16,1024]{3,2,1,0:T(8,128)(2,1)S(1)}, bf16[512,1024]{1,0:T(8,128)(2,1)S(1)}, bf16[3,2,2,16,1024]{4,3,2,1,0:T(8,128)(2,1)S(1)}, f32[6,4,8,12...) custom-call(s32[4,6]{1,0:T(4,128)S(1)} %copy-done.5, ...), custom_call_target="tpu_custom_call" | custom-call | flops 1744830464 | bytes 2097152 | tf_op jit(solution)/shard_map/attend/pallas_call | solution.py:54
  36.7 3.2 %collective-permute-start.16 = (bf16[2,2,16,1024]{3,2,1,0:T(8,128)(2,1)S(1)}, bf16[2,2,16,1024]{3,2,1,0:T(8,128)(2,1)S(1)}, u32[]{:S(2)}, u32[]{:S(2)}) collective-permute-start(bf16[2,2,16,1024]{3,2,1,0:T(8,128)(2,1)S(1)} %slice.101), channel_id=1, source_target_pairs={{0,4},{1,5},{2,6},{3,7},{4,0},{5,1},{6,2},{7,3},{8,12},{9,13},{10,... | collective-permute-start | bytes 393224 | tf_op jit(solution)/shard_map/ppermute | solution.py:23
  40.9 3.6 %collective-permute-start.11 = (bf16[2,2,16,1024]{3,2,1,0:T(8,128)(2,1)S(1)}, bf16[2,2,16,1024]{3,2,1,0:T(8,128)(2,1)S(1)}, u32[]{:S(2)}, u32[]{:S(2)}) collective-permute-start(bf16[2,2,16,1024]{3,2,1,0:T(8,128)(2,1)S(1)} %slice_add_fusion.9.kept_ref), channel_id=1, source_target_pairs={{0,4},{1,5},{2,6},{3,7},{4,0},{5,1},{6,2},{7,3},{8,12},{9,13},{10,... | collective-permute-start | bytes 393224 | tf_op jit(solution)/shard_map/ppermute | solution.py:23
  44.5 1.9 %collective-permute-done.16 = bf16[2,2,16,1024]{3,2,1,0:T(8,128)(2,1)S(1)} collective-permute-done((bf16[2,2,16,1024]{3,2,1,0:T(8,128)(2,1)S(1)}, bf16[2,2,16,1024]{3,2,1,0:T(8,128)(2,1)S(1)}, u32[]{:S(2)}, u32[]{:S(2)}) %collective-permute-start.16) | collective-permute-done | bytes 131104 | tf_op jit(solution)/shard_map/ppermute | solution.py:23
  47.8 3.9 %collective-permute-start.14 = (bf16[2,2,16,1024]{3,2,1,0:T(8,128)(2,1)S(1)}, bf16[2,2,16,1024]{3,2,1,0:T(8,128)(2,1)S(1)}, u32[]{:S(2)}, u32[]{:S(2)}) collective-permute-start(bf16[2,2,16,1024]{3,2,1,0:T(8,128)(2,1)S(1)} %slice_add_fusion.8.kept_ref), channel_id=1, source_target_pairs={{0,4},{1,5},{2,6},{3,7},{4,0},{5,1},{6,2},{7,3},{8,12},{9,13},{10,... | collective-permute-start | bytes 393224 | tf_op jit(solution)/shard_map/ppermute | solution.py:23
  53.7 3.9 %collective-permute-start.22 = (bf16[2,2,16,1024]{3,2,1,0:T(8,128)(2,1)S(1)}, bf16[2,2,16,1024]{3,2,1,0:T(8,128)(2,1)S(1)}, u32[]{:S(2)}, u32[]{:S(2)}) collective-permute-start(bf16[2,2,16,1024]{3,2,1,0:T(8,128)(2,1)S(1)} %get-tuple-element.72), channel_id=1, source_target_pairs={{0,4},{1,5},{2,6},{3,7},{4,0},{5,1},{6,2},{7,3},{8,12},{9,13},{10,... | collective-permute-start | bytes 393224 | tf_op jit(solution)/shard_map/ppermute | solution.py:23
  59.7 2.8 %collective-permute-done.22 = bf16[2,2,16,1024]{3,2,1,0:T(8,128)(2,1)S(1)} collective-permute-done((bf16[2,2,16,1024]{3,2,1,0:T(8,128)(2,1)S(1)}, bf16[2,2,16,1024]{3,2,1,0:T(8,128)(2,1)S(1)}, u32[]{:S(2)}, u32[]{:S(2)}) %collective-permute-start.22) | collective-permute-done | bytes 131104 | tf_op jit(solution)/shard_map/ppermute | solution.py:23
  63.6 4.3 %expand.2.refs_3_ = bf16[1,4,64,4096]{3,2,1,0:T(8,128)(2,1)S(1)} custom-call(s32[4,6]{1,0:T(4,128)S(1)} %copy-done.5, bf16[1024,4096]{1,0:T(8,128)(2,1)S(1)} %bitcast.5, bf16[2,4,16,1024]{3,2,1,0:T(8,128)(2,1)S(1)} %constant_dynamic-update-slice_fusion.refs_0_, bf16[2,4,16,1024]{3,2,1,0:T(8,128)(2,1)S(1)} %constant_dynamic-update-slice_fusion.2.refs_1_, ...), custom_call_target="tpu_custom_call" | custom-call | flops 3221225472 | bytes 8388608 | tf_op jit(solution)/shard_map/expand/pallas_call | solution.py:54
  68.0 4.3 %expand.3.units_ref = bf16[2,4,64,4096]{3,2,1,0:T(8,128)(2,1)S(1)} custom-call(s32[4,6]{1,0:T(4,128)S(1)} %copy-done.5, bf16[1024,4096]{1,0:T(8,128)(2,1)S(1)} %bitcast.5, bf16[2,4,16,1024]{3,2,1,0:T(8,128)(2,1)S(1)} %collective-permute-done.19.refs_0_, bf16[2,4,16,1024]{3,2,1,0:T(8,128)(2,1)S(1)} %collective-permute-done.21.refs_1_, ...), custom_call_target="tpu_custom_call" | custom-call | flops 3221225472 | bytes 8388608 | tf_op jit(solution)/shard_map/expand/pallas_call | solution.py:54
  72.3 2.3 %shrink.3 = bf16[4,8,16,512]{3,2,1,0:T(8,128)(2,1)S(1)} custom-call(bf16[2,4,64,4096]{3,2,1,0:T(8,128)(2,1)S(1)} %expand.3.units_ref, bf16[4096,1024]{1,0:T(8,128)(2,1)S(1)} %bitcast.3), custom_call_target="tpu_custom_call" | custom-call | flops 2147483648 | bytes 4194304 | tf_op jit(solution)/shard_map/shrink/pallas_call | solution.py:54
  75.2 2.3 %shrink.2 = bf16[4,8,16,512]{3,2,1,0:T(8,128)(2,1)S(1)} custom-call(bf16[2,4,64,4096]{3,2,1,0:T(8,128)(2,1)S(1)} %expand.3.units_ref, bf16[4096,1024]{1,0:T(8,128)(2,1)S(1)} %bitcast.3), custom_call_target="tpu_custom_call" | custom-call | flops 2147483648 | bytes 4194304 | tf_op jit(solution)/shard_map/shrink/pallas_call | solution.py:54
  77.7 1.7 %collective-permute-start.28 = (bf16[4,2,16,512]{3,2,1,0:T(8,128)(2,1)S(1)}, bf16[4,2,16,512]{3,2,1,0:T(8,128)(2,1)S(1)}, u32[]{:S(2)}, u32[]{:S(2)}) collective-permute-start(bf16[4,2,16,512]{3,2,1,0:T(8,128)(2,1)S(1)} %slice.111), channel_id=1, source_target_pairs={{0,2},{1,3},{2,0},{3,1},{4,6},{5,7},{6,4},{7,5},{8,10},{9,11},{10,... | collective-permute-start | bytes 393224 | tf_op jit(solution)/shard_map/ppermute | solution.py:23
  80.8 3.3 %collective-permute-done.28 = bf16[4,2,16,512]{3,2,1,0:T(8,128)(2,1)S(1)} collective-permute-done((bf16[4,2,16,512]{3,2,1,0:T(8,128)(2,1)S(1)}, bf16[4,2,16,512]{3,2,1,0:T(8,128)(2,1)S(1)}, u32[]{:S(2)}, u32[]{:S(2)}) %collective-permute-start.28) | collective-permute-done | bytes 131104 | tf_op jit(solution)/shard_map/ppermute | solution.py:23
  84.1 3.5 %collective-permute-start.29 = (bf16[4,1,16,512]{3,2,1,0:T(8,128)(2,1)S(1)}, bf16[4,1,16,512]{3,2,1,0:T(8,128)(2,1)S(1)}, u32[]{:S(2)}, u32[]{:S(2)}) collective-permute-start(bf16[4,1,16,512]{3,2,1,0:T(8,128)(2,1)S(1)} %get-tuple-element.77), channel_id=1, source_target_pairs={{0,4},{1,5},{2,6},{3,7},{4,0},{5,1},{6,2},{7,3},{8,12},{9,13},{10,... | collective-permute-start | bytes 196616 | tf_op jit(solution)/shard_map/ppermute | solution.py:23
  87.6 2.8 %collective-permute-start.26 = (bf16[4,1,16,512]{3,2,1,0:T(8,128)(2,1)S(1)}, bf16[4,1,16,512]{3,2,1,0:T(8,128)(2,1)S(1)}, u32[]{:S(2)}, u32[]{:S(2)}) collective-permute-start(bf16[4,1,16,512]{3,2,1,0:T(8,128)(2,1)S(1)} %get-tuple-element.79), channel_id=1, source_target_pairs={{0,4},{1,5},{2,6},{3,7},{4,0},{5,1},{6,2},{7,3},{8,12},{9,13},{10,... | collective-permute-start | bytes 196616 | tf_op jit(solution)/shard_map/ppermute | solution.py:23
  91.2 2.1 %collective-permute-done.26.refs_1_ = bf16[4,1,16,512]{3,2,1,0:T(8,128)(2,1)S(1)} collective-permute-done((bf16[4,1,16,512]{3,2,1,0:T(8,128)(2,1)S(1)}, bf16[4,1,16,512]{3,2,1,0:T(8,128)(2,1)S(1)}, u32[]{:S(2)}, u32[]{:S(2)}) %collective-permute-start.26) | collective-permute-done | bytes 65568 | tf_op jit(solution)/shard_map/ppermute | solution.py:23
  93.5 3.7 %collective-permute-start.30 = (bf16[16,1024]{1,0:T(8,128)(2,1)S(1)}, bf16[16,1024]{1,0:T(8,128)(2,1)S(1)}, u32[]{:S(2)}, u32[]{:S(2)}) collective-permute-start(bf16[16,1024]{1,0:T(8,128)(2,1)S(1)} %get-tuple-element.73), channel_id=1, source_target_pairs={{0,24},{8,16},{16,8},{24,0},{1,25},{9,17},{17,9},{25,1},{2,26},{10... | collective-permute-start | bytes 98312 | tf_op jit(solution)/shard_map/ppermute | solution.py:23
  99.1 2.0 %collective-permute-done.31.refs_1_ = bf16[16,1024]{1,0:T(8,128)(2,1)S(1)} collective-permute-done((bf16[16,1024]{1,0:T(8,128)(2,1)S(1)}, bf16[16,1024]{1,0:T(8,128)(2,1)S(1)}, u32[]{:S(2)}, u32[]{:S(2)}) %collective-permute-start.31) | collective-permute-done | bytes 32800 | tf_op jit(solution)/shard_map/ppermute | solution.py:23
  (117 shorter events, 28.3 us)
Async XLA Ops:
  1.7 7.6 %collective-permute-start = (bf16[16,1024]{1,0:T(8,128)(2,1)}, bf16[16,1024]{1,0:T(8,128)(2,1)S(1)}, u32[]{:S(2)}, u32[]{:S(2)}) collective-permute-start(bf16[16,1024]{1,0:T(8,128)(2,1)} %get-tuple-element.42), channel_id=1, source_target_pairs={{0,24},{8,16},{16,8},{24,0},{1,25},{9,17},{17,9},{25,1},{2,26},{10... | collective-permute-start | bytes 98312 | tf_op jit(solution)/shard_map/ppermute | solution.py:23
  5.6 4.1 %collective-permute-start.1 = (bf16[16,1024]{1,0:T(8,128)(2,1)}, bf16[16,1024]{1,0:T(8,128)(2,1)S(1)}, u32[]{:S(2)}, u32[]{:S(2)}) collective-permute-start(bf16[16,1024]{1,0:T(8,128)(2,1)} %get-tuple-element.43), channel_id=1, source_target_pairs={{0,16},{8,24},{16,0},{24,8},{1,17},{9,25},{17,1},{25,9},{2,18},{10... | collective-permute-start | bytes 98312 | tf_op jit(solution)/shard_map/ppermute | solution.py:23
  6.3 6.7 %collective-permute-start.5 = (bf16[2,1,16,1024]{3,2,1,0:T(8,128)(2,1)}, bf16[2,1,16,1024]{3,2,1,0:T(8,128)(2,1)S(1)}, u32[]{:S(2)}, u32[]{:S(2)}) collective-permute-start(bf16[2,1,16,1024]{3,2,1,0:T(8,128)(2,1)} %get-tuple-element.45.kept_ref), channel_id=1, source_target_pairs={{0,4},{1,5},{2,6},{3,7},{4,0},{5,1},{6,2},{7,3},{8,12},{9,13},{10,... | collective-permute-start | bytes 196616 | tf_op jit(solution)/shard_map/ppermute | solution.py:23
  10.3 5.7 %collective-permute-start.3 = (bf16[3,1,16,1024]{3,2,1,0:T(8,128)(2,1)S(1)}, bf16[3,1,16,1024]{3,2,1,0:T(8,128)(2,1)S(1)}, u32[]{:S(2)}, u32[]{:S(2)}) collective-permute-start(bf16[3,1,16,1024]{3,2,1,0:T(8,128)(2,1)S(1)} %stack.1.kept_ref), channel_id=1, source_target_pairs={{0,4},{1,5},{2,6},{3,7},{4,0},{5,1},{6,2},{7,3},{8,12},{9,13},{10,... | collective-permute-start | bytes 294920 | tf_op jit(solution)/shard_map/ppermute | solution.py:23
  13.0 6.2 %collective-permute-start.6 = (bf16[2,2,16,1024]{3,2,1,0:T(8,128)(2,1)S(1)}, bf16[2,2,16,1024]{3,2,1,0:T(8,128)(2,1)S(1)}, u32[]{:S(2)}, u32[]{:S(2)}) collective-permute-start(bf16[2,2,16,1024]{3,2,1,0:T(8,128)(2,1)S(1)} %join.3), channel_id=1, source_target_pairs={{0,2},{1,3},{2,0},{3,1},{4,6},{5,7},{6,4},{7,5},{8,10},{9,11},{10,... | collective-permute-start | bytes 393224 | tf_op jit(solution)/shard_map/ppermute | solution.py:23
  16.0 6.5 %collective-permute-start.4 = (bf16[3,2,16,1024]{3,2,1,0:T(8,128)(2,1)S(1)}, bf16[3,2,16,1024]{3,2,1,0:T(8,128)(2,1)S(1)}, u32[]{:S(2)}, u32[]{:S(2)}) collective-permute-start(bf16[3,2,16,1024]{3,2,1,0:T(8,128)(2,1)S(1)} %join.2), channel_id=1, source_target_pairs={{0,2},{1,3},{2,0},{3,1},{4,6},{5,7},{6,4},{7,5},{8,10},{9,11},{10,... | collective-permute-start | bytes 589832 | tf_op jit(solution)/shard_map/ppermute | solution.py:23
  34.7 5.3 %collective-permute-start.12 = (bf16[2,4,16,1024]{3,2,1,0:T(8,128)(2,1)S(1)}, bf16[2,4,16,1024]{3,2,1,0:T(8,128)(2,1)S(1)}, u32[]{:S(2)}, u32[]{:S(2)}) collective-permute-start(bf16[2,4,16,1024]{3,2,1,0:T(8,128)(2,1)S(1)} %slice.77), channel_id=1, source_target_pairs={{0,1},{1,0},{2,3},{3,2},{4,5},{5,4},{6,7},{7,6},{8,9},{9,8},{10,11... | collective-permute-start | bytes 786440 | tf_op jit(solution)/shard_map/ppermute | solution.py:23
  35.1 5.8 %collective-permute-start.10 = (bf16[2,2,16,1024]{3,2,1,0:T(8,128)(2,1)S(1)}, bf16[2,2,16,1024]{3,2,1,0:T(8,128)(2,1)S(1)}, u32[]{:S(2)}, u32[]{:S(2)}) collective-permute-start(bf16[2,2,16,1024]{3,2,1,0:T(8,128)(2,1)S(1)} %slice.97), channel_id=1, source_target_pairs={{0,2},{1,3},{2,0},{3,1},{4,6},{5,7},{6,4},{7,5},{8,10},{9,11},{10,... | collective-permute-start | bytes 393224 | tf_op jit(solution)/shard_map/ppermute | solution.py:23
  36.7 9.7 %collective-permute-start.16 = (bf16[2,2,16,1024]{3,2,1,0:T(8,128)(2,1)S(1)}, bf16[2,2,16,1024]{3,2,1,0:T(8,128)(2,1)S(1)}, u32[]{:S(2)}, u32[]{:S(2)}) collective-permute-start(bf16[2,2,16,1024]{3,2,1,0:T(8,128)(2,1)S(1)} %slice.101), channel_id=1, source_target_pairs={{0,4},{1,5},{2,6},{3,7},{4,0},{5,1},{6,2},{7,3},{8,12},{9,13},{10,... | collective-permute-start | bytes 393224 | tf_op jit(solution)/shard_map/ppermute | solution.py:23
  40.0 7.7 %collective-permute-start.13 = (bf16[2,2,16,1024]{3,2,1,0:T(8,128)(2,1)S(1)}, bf16[2,2,16,1024]{3,2,1,0:T(8,128)(2,1)S(1)}, u32[]{:S(2)}, u32[]{:S(2)}) collective-permute-start(bf16[2,2,16,1024]{3,2,1,0:T(8,128)(2,1)S(1)} %slice.99), channel_id=1, source_target_pairs={{0,2},{1,3},{2,0},{3,1},{4,6},{5,7},{6,4},{7,5},{8,10},{9,11},{10,... | collective-permute-start | bytes 393224 | tf_op jit(solution)/shard_map/ppermute | solution.py:23
  40.9 11.1 %collective-permute-start.11 = (bf16[2,2,16,1024]{3,2,1,0:T(8,128)(2,1)S(1)}, bf16[2,2,16,1024]{3,2,1,0:T(8,128)(2,1)S(1)}, u32[]{:S(2)}, u32[]{:S(2)}) collective-permute-start(bf16[2,2,16,1024]{3,2,1,0:T(8,128)(2,1)S(1)} %slice_add_fusion.9.kept_ref), channel_id=1, source_target_pairs={{0,4},{1,5},{2,6},{3,7},{4,0},{5,1},{6,2},{7,3},{8,12},{9,13},{10,... | collective-permute-start | bytes 393224 | tf_op jit(solution)/shard_map/ppermute | solution.py:23
  46.5 7.1 %collective-permute-start.17 = (bf16[2,2,16,1024]{3,2,1,0:T(8,128)(2,1)S(1)}, bf16[2,2,16,1024]{3,2,1,0:T(8,128)(2,1)S(1)}, u32[]{:S(2)}, u32[]{:S(2)}) collective-permute-start(bf16[2,2,16,1024]{3,2,1,0:T(8,128)(2,1)S(1)} %slice_add_fusion.7.kept_ref), channel_id=1, source_target_pairs={{0,2},{1,3},{2,0},{3,1},{4,6},{5,7},{6,4},{7,5},{8,10},{9,11},{10,... | collective-permute-start | bytes 393224 | tf_op jit(solution)/shard_map/ppermute | solution.py:23
  47.8 9.9 %collective-permute-start.14 = (bf16[2,2,16,1024]{3,2,1,0:T(8,128)(2,1)S(1)}, bf16[2,2,16,1024]{3,2,1,0:T(8,128)(2,1)S(1)}, u32[]{:S(2)}, u32[]{:S(2)}) collective-permute-start(bf16[2,2,16,1024]{3,2,1,0:T(8,128)(2,1)S(1)} %slice_add_fusion.8.kept_ref), channel_id=1, source_target_pairs={{0,4},{1,5},{2,6},{3,7},{4,0},{5,1},{6,2},{7,3},{8,12},{9,13},{10,... | collective-permute-start | bytes 393224 | tf_op jit(solution)/shard_map/ppermute | solution.py:23
  52.2 7.4 %collective-permute-start.18 = (bf16[2,2,16,1024]{3,2,1,0:T(8,128)(2,1)S(1)}, bf16[2,2,16,1024]{3,2,1,0:T(8,128)(2,1)S(1)}, u32[]{:S(2)}, u32[]{:S(2)}) collective-permute-start(bf16[2,2,16,1024]{3,2,1,0:T(8,128)(2,1)S(1)} %get-tuple-element.70), channel_id=1, source_target_pairs={{0,2},{1,3},{2,0},{3,1},{4,6},{5,7},{6,4},{7,5},{8,10},{9,11},{10,... | collective-permute-start | bytes 393224 | tf_op jit(solution)/shard_map/ppermute | solution.py:23
  53.7 8.8 %collective-permute-start.22 = (bf16[2,2,16,1024]{3,2,1,0:T(8,128)(2,1)S(1)}, bf16[2,2,16,1024]{3,2,1,0:T(8,128)(2,1)S(1)}, u32[]{:S(2)}, u32[]{:S(2)}) collective-permute-start(bf16[2,2,16,1024]{3,2,1,0:T(8,128)(2,1)S(1)} %get-tuple-element.72), channel_id=1, source_target_pairs={{0,4},{1,5},{2,6},{3,7},{4,0},{5,1},{6,2},{7,3},{8,12},{9,13},{10,... | collective-permute-start | bytes 393224 | tf_op jit(solution)/shard_map/ppermute | solution.py:23
  57.8 5.7 %collective-permute-start.20 = (bf16[2,2,16,1024]{3,2,1,0:T(8,128)(2,1)S(1)}, bf16[2,2,16,1024]{3,2,1,0:T(8,128)(2,1)S(1)}, u32[]{:S(2)}, u32[]{:S(2)}) collective-permute-start(bf16[2,2,16,1024]{3,2,1,0:T(8,128)(2,1)S(1)} %get-tuple-element.71), channel_id=1, source_target_pairs={{0,2},{1,3},{2,0},{3,1},{4,6},{5,7},{6,4},{7,5},{8,10},{9,11},{10,... | collective-permute-start | bytes 393224 | tf_op jit(solution)/shard_map/ppermute | solution.py:23
  59.6 8.4 %collective-permute-start.19 = (bf16[2,4,16,1024]{3,2,1,0:T(8,128)(2,1)S(1)}, bf16[2,4,16,1024]{3,2,1,0:T(8,128)(2,1)S(1)}, u32[]{:S(2)}, u32[]{:S(2)}) collective-permute-start(bf16[2,4,16,1024]{3,2,1,0:T(8,128)(2,1)S(1)} %constant_dynamic-update-slice_fusion.refs_0_), channel_id=1, source_target_pairs={{0,1},{1,0},{2,3},{3,2},{4,5},{5,4},{6,7},{7,6},{8,9},{9,8},{10,11... | collective-permute-start | bytes 786440 | tf_op jit(solution)/shard_map/ppermute | solution.py:23
  62.5 5.5 %collective-permute-start.23 = (bf16[2,4,16,1024]{3,2,1,0:T(8,128)(2,1)S(1)}, bf16[2,4,16,1024]{3,2,1,0:T(8,128)(2,1)S(1)}, u32[]{:S(2)}, u32[]{:S(2)}) collective-permute-start(bf16[2,4,16,1024]{3,2,1,0:T(8,128)(2,1)S(1)} %constant_dynamic-update-slice_fusion.4.refs_2_), channel_id=1, source_target_pairs={{0,1},{1,0},{2,3},{3,2},{4,5},{5,4},{6,7},{7,6},{8,9},{9,8},{10,11... | collective-permute-start | bytes 786440 | tf_op jit(solution)/shard_map/ppermute | solution.py:23
  63.5 4.5 %collective-permute-start.21 = (bf16[2,4,16,1024]{3,2,1,0:T(8,128)(2,1)S(1)}, bf16[2,4,16,1024]{3,2,1,0:T(8,128)(2,1)S(1)}, u32[]{:S(2)}, u32[]{:S(2)}) collective-permute-start(bf16[2,4,16,1024]{3,2,1,0:T(8,128)(2,1)S(1)} %constant_dynamic-update-slice_fusion.2.refs_1_), channel_id=1, source_target_pairs={{0,1},{1,0},{2,3},{3,2},{4,5},{5,4},{6,7},{7,6},{8,9},{9,8},{10,11... | collective-permute-start | bytes 786440 | tf_op jit(solution)/shard_map/ppermute | solution.py:23
  77.7 6.4 %collective-permute-start.28 = (bf16[4,2,16,512]{3,2,1,0:T(8,128)(2,1)S(1)}, bf16[4,2,16,512]{3,2,1,0:T(8,128)(2,1)S(1)}, u32[]{:S(2)}, u32[]{:S(2)}) collective-permute-start(bf16[4,2,16,512]{3,2,1,0:T(8,128)(2,1)S(1)} %slice.111), channel_id=1, source_target_pairs={{0,2},{1,3},{2,0},{3,1},{4,6},{5,7},{6,4},{7,5},{8,10},{9,11},{10,... | collective-permute-start | bytes 393224 | tf_op jit(solution)/shard_map/ppermute | solution.py:23
  79.5 8.1 %collective-permute-start.25 = (bf16[4,2,16,512]{3,2,1,0:T(8,128)(2,1)S(1)}, bf16[4,2,16,512]{3,2,1,0:T(8,128)(2,1)S(1)}, u32[]{:S(2)}, u32[]{:S(2)}) collective-permute-start(bf16[4,2,16,512]{3,2,1,0:T(8,128)(2,1)S(1)} %slice.105), channel_id=1, source_target_pairs={{0,2},{1,3},{2,0},{3,1},{4,6},{5,7},{6,4},{7,5},{8,10},{9,11},{10,... | collective-permute-start | bytes 393224 | tf_op jit(solution)/shard_map/ppermute | solution.py:23
  84.1 7.1 %collective-permute-start.29 = (bf16[4,1,16,512]{3,2,1,0:T(8,128)(2,1)S(1)}, bf16[4,1,16,512]{3,2,1,0:T(8,128)(2,1)S(1)}, u32[]{:S(2)}, u32[]{:S(2)}) collective-permute-start(bf16[4,1,16,512]{3,2,1,0:T(8,128)(2,1)S(1)} %get-tuple-element.77), channel_id=1, source_target_pairs={{0,4},{1,5},{2,6},{3,7},{4,0},{5,1},{6,2},{7,3},{8,12},{9,13},{10,... | collective-permute-start | bytes 196616 | tf_op jit(solution)/shard_map/ppermute | solution.py:23
  87.6 5.7 %collective-permute-start.26 = (bf16[4,1,16,512]{3,2,1,0:T(8,128)(2,1)S(1)}, bf16[4,1,16,512]{3,2,1,0:T(8,128)(2,1)S(1)}, u32[]{:S(2)}, u32[]{:S(2)}) collective-permute-start(bf16[4,1,16,512]{3,2,1,0:T(8,128)(2,1)S(1)} %get-tuple-element.79), channel_id=1, source_target_pairs={{0,4},{1,5},{2,6},{3,7},{4,0},{5,1},{6,2},{7,3},{8,12},{9,13},{10,... | collective-permute-start | bytes 196616 | tf_op jit(solution)/shard_map/ppermute | solution.py:23
  93.5 5.6 %collective-permute-start.30 = (bf16[16,1024]{1,0:T(8,128)(2,1)S(1)}, bf16[16,1024]{1,0:T(8,128)(2,1)S(1)}, u32[]{:S(2)}, u32[]{:S(2)}) collective-permute-start(bf16[16,1024]{1,0:T(8,128)(2,1)S(1)} %get-tuple-element.73), channel_id=1, source_target_pairs={{0,24},{8,16},{16,8},{24,0},{1,25},{9,17},{17,9},{25,1},{2,26},{10... | collective-permute-start | bytes 98312 | tf_op jit(solution)/shard_map/ppermute | solution.py:23
  (21 other events, 162.5 us)
